TPU v7x, 128 devices: a whole 4x4x4 slice. The times are simulated.
128 devices in a mesh: band: 16 (over y, x_lo, core), cross: 8 (over z, x_hi).
Axes of the slice: x: 4 (x_hi: 2, x_lo: 2; x = x_hi * 2 + x_lo), y: 4, z: 4, core: 2. Of those that a mesh axis runs over, the one named last changes fastest.
Arguments:
- rasters: int32 [4, 512, 8192], P(None, 'cross', 'band'), may hold values 0 or 1
- aerial: float32 [512, 8192], P('cross', 'band'), may hold values from -6 to 6
- w_in: float32 [32, 4], replicated, may hold values from -3 to 3
- aerial_gain: float32 [32], replicated, may hold values from -4 to 4
- b_in: float32 [32], replicated, may hold values from -2 to 2
- w_conv1: bfloat16 [32, 288], replicated, may hold values from -0.375 to 0.375
- b_conv1: float32 [32], replicated, may hold values from -2 to 2
- w_proj: bfloat16 [128, 32], replicated, may hold values from -1 to 1
- b_proj: float32 [128], replicated, may hold values from -2 to 2
- w_ctx: bfloat16 [128, 1920], replicated, may hold values from -0.25 to 0.25
- w_up: bfloat16 [32, 128], replicated, may hold values from -0.5 to 0.5
- b_up: float32 [32], replicated, may hold values from -2 to 2
- w_head: bfloat16 [2, 800], replicated, may hold values from -0.21875 to 0.21875
- b_head: float32 [2], replicated, may hold values from -3 to 3
Outputs:
- logits: float32 [2, 512, 8192], P(None, 'cross', 'band')
All inputs are finite; a program needn't handle non-finite values. No bound on the sum of `rasters` on one device may be relied on, other than what follows from the above.
Results may differ from a plain program's by a relative error of at most 0.015.
Values may be sent and summed in bfloat16 or wider, within the bound.
No kernel may reach another device: no remote copies, remote signals or barrier semaphores. Data moves between devices by JAX's collectives and lax.ppermute only.
A program may use at most 192 MiB of HBM per device.

v0:
```python
import jax
import jax.numpy as jnp
from jax import lax
from jax.sharding import PartitionSpec as P


def padded_2(block, sides, width):
    for axis, dim in sides:
        count = lax.axis_size(axis)
        forward = [(i, i + 1) for i in range(count - 1)]
        backward = [(target, source) for source, target in forward]
        low = lax.ppermute(
            lax.slice_in_dim(block, block.shape[dim] - width, None, axis=dim), axis, forward
        )
        high = lax.ppermute(lax.slice_in_dim(block, 0, width, axis=dim), axis, backward)
        block = jnp.concatenate([low, block, high], axis=dim)
    return block


def passed_along(block, axis, distance):
    devices = range(lax.axis_size(axis))
    route = [(i - distance, i) for i in devices if i - distance in devices]
    return lax.ppermute(block, axis, route)


def stem_layer(rasters, aerial, w_in, aerial_gain, b_in):
    layer_count, row_count, col_count = rasters.shape
    flat_rasters = rasters.reshape(layer_count, row_count * col_count).astype(jnp.float32)
    combined = jnp.dot(w_in, flat_rasters, precision=lax.Precision.HIGHEST)
    combined = (
        combined.reshape(-1, row_count, col_count)
        + aerial_gain[:, None, None] * aerial[None]
        + b_in[:, None, None]
    )
    return jax.nn.relu(combined).astype(jnp.bfloat16)


def conv_rows(padded, weights, taps, row_count, col_count):
    channels = padded.shape[0]
    stacked = jnp.concatenate(
        [padded[:, :, offset : offset + col_count] for offset in range(taps)], axis=0
    )
    summed = jnp.zeros((weights.shape[0], row_count * col_count), jnp.float32)
    for row_off in range(taps):
        window = stacked[:, row_off : row_off + row_count, :].reshape(
            taps * channels, row_count * col_count
        )
        part_w = weights[:, row_off * taps * channels : (row_off + 1) * taps * channels]
        summed = summed + jnp.dot(part_w, window, preferred_element_type=jnp.float32)
    return summed.reshape(-1, row_count, col_count)


def pool_map(features):
    channels, row_count, col_count = features.shape
    blocks = features.reshape(channels, row_count // 4, 4, col_count // 4, 4).astype(jnp.float32)
    return jnp.mean(blocks, axis=(2, 4)).astype(jnp.bfloat16)


def body(
    rasters,
    aerial,
    w_in,
    aerial_gain,
    b_in,
    w_conv1,
    b_conv1,
    w_proj,
    b_proj,
    w_ctx,
    w_up,
    b_up,
    w_head,
    b_head,
):
    row_count, col_count = aerial.shape
    stem_out = stem_layer(rasters, aerial, w_in, aerial_gain, b_in)
    channels = stem_out.shape[0]
    stem_pad = padded_2(stem_out, (("band", 2), ("cross", 1)), 1)
    features = jax.nn.relu(
        conv_rows(stem_pad, w_conv1, 3, row_count, col_count) + b_conv1[:, None, None]
    ).astype(jnp.bfloat16)
    pooled = pool_map(features)
    pool_rows = pooled.shape[1]
    pool_cols = pooled.shape[2]
    pool_size = pool_rows * pool_cols
    wide_count = w_proj.shape[0]
    flat_pooled = pooled.reshape(channels, pool_size)
    own_map = jnp.dot(w_proj, flat_pooled, preferred_element_type=jnp.float32)
    own_map = jax.nn.relu(own_map + b_proj[:, None]).astype(jnp.bfloat16)
    band_list = []
    for col_off in (-2, -1, 0, 1, 2):
        if col_off == 0:
            band_list.append(own_map)
        else:
            band_list.append(passed_along(own_map, "band", -col_off))
    band_stack = jnp.stack(band_list)
    cross_list = []
    for row_off in (-1, 0, 1):
        if row_off == 0:
            cross_list.append(band_stack)
        else:
            cross_list.append(passed_along(band_stack, "cross", -row_off))
    near_maps = jnp.stack(cross_list).reshape(15 * wide_count, pool_size)
    context = jnp.dot(w_ctx, near_maps, preferred_element_type=jnp.float32) + own_map.astype(
        jnp.float32
    )
    mixed_map = jax.nn.relu(context).astype(jnp.bfloat16)
    lifted = jnp.dot(w_up, mixed_map, preferred_element_type=jnp.float32).reshape(
        channels, pool_rows, 1, pool_cols, 1
    )
    lifted = jnp.broadcast_to(lifted, (channels, pool_rows, 4, pool_cols, 4)).reshape(
        channels, row_count, col_count
    )
    decoded = jax.nn.relu(features.astype(jnp.float32) + lifted + b_up[:, None, None]).astype(
        jnp.bfloat16
    )
    classes = w_head.shape[0]
    per_tap = jnp.transpose(w_head.reshape(classes, 25, channels), (1, 0, 2)).reshape(
        25 * classes, channels
    )
    spread = jnp.dot(
        per_tap,
        decoded.reshape(channels, row_count * col_count),
        preferred_element_type=jnp.float32,
    )
    spread = spread.reshape(25, classes, row_count, col_count)
    extended = jnp.zeros((classes, row_count + 4, col_count + 4), jnp.float32)
    for tap_index in range(25):
        row_off = tap_index // 5
        col_off = tap_index % 5
        extended = extended.at[:, row_off : row_off + row_count, col_off : col_off + col_count].add(
            spread[tap_index]
        )
    for strip_first, shift_by, target_first in ((col_count + 2, 1, 2), (0, -1, col_count)):
        margin_strip = extended[:, :, strip_first : strip_first + 2]
        arrived = passed_along(margin_strip, "band", shift_by)
        extended = extended.at[:, :, target_first : target_first + 2].add(arrived)
    banded = extended[:, :, 2 : col_count + 2]
    for strip_first, shift_by, target_first in ((row_count + 2, 1, 2), (0, -1, row_count)):
        margin_strip = banded[:, strip_first : strip_first + 2, :]
        arrived = passed_along(margin_strip, "cross", shift_by)
        banded = banded.at[:, target_first : target_first + 2, :].add(arrived)
    logits = banded[:, 2 : row_count + 2, :] + b_head[:, None, None]
    return logits


def solution(mesh):
    placed = (
        P(None, "cross", "band"),
        P("cross", "band"),
        P(),
        P(),
        P(),
        P(),
        P(),
        P(),
        P(),
        P(),
        P(),
        P(),
        P(),
        P(),
    )
    return jax.shard_map(
        body, mesh=mesh, in_specs=placed, out_specs=P(None, "cross", "band"), check_vma=False
    )
```

profile of v0, /device:TPU:40, one launch (start us, length us, event | category | flops | bytes accessed | tf_op | source)
XLA Modules:
  0.0 406.3 jit_solution(15498621572235428076)
XLA Ops:
  1.1 5.2 %maximum_convert_fusion.3 = bf16[32,64,512]{2,0,1:T(8,128)(2,1)S(1)} fusion(f32[32]{0:T(128)} %param.76, f32[64,512]{1,0:T(8,128)} %param.73, f32[32]{0:T(128)} %param.75, f32[32,4]{0,1:T(4,128)} %param.74, f32[1,4,64,512]{3,2,1,0:T(8,128)S(1)} %convert_bitcast_fusion), kind=kOutput, calls=%fused_computation.13 | convolution fusion | flops 55574528 | bytes 2753280 | tf_op jit(solution)/shard_map/dot_general | solution.py:29
  8.5 4.5 %collective-permute-start.1 = (bf16[32,64,1]{2,0,1:T(8,128)(2,1)S(1)}, bf16[32,64,1]{2,0,1:T(8,128)(2,1)S(1)}, u32[]{:S(2)}, u32[]{:S(2)}) collective-permute-start(bf16[32,64,1]{2,0,1:T(8,128)(2,1)S(1)} %get-tuple-element.390), channel_id=1, source_target_pairs={{8,0},{16,8},{24,16},{32,24},{40,32},{48,40},{56,48},{64,56},{72,6... | collective-permute-start | bytes 12296 | tf_op jit(solution)/shard_map/ppermute | solution.py:15
  13.1 7.8 %collective-permute-done = bf16[32,64,1]{2,0,1:T(8,128)(2,1)S(1)} collective-permute-done((bf16[32,64,1]{2,0,1:T(8,128)(2,1)S(1)}, bf16[32,64,1]{2,0,1:T(8,128)(2,1)S(1)}, u32[]{:S(2)}, u32[]{:S(2)}) %collective-permute-start) | collective-permute-done | bytes 4128 | tf_op jit(solution)/shard_map/ppermute | solution.py:12
  21.8 4.6 %collective-permute-start.2 = (bf16[32,1,514]{2,0,1:T(8,128)(2,1)S(1)}, bf16[32,1,514]{2,0,1:T(8,128)(2,1)S(1)}, u32[]{:S(2)}, u32[]{:S(2)}) collective-permute-start(bf16[32,1,514]{2,0,1:T(8,128)(2,1)S(1)} %get-tuple-element.384), channel_id=1, source_target_pairs={{0,1},{1,2},{2,3},{3,4},{4,5},{5,6},{6,7},{8,9},{9,10},{10,11},{11... | collective-permute-start | bytes 98696 | tf_op jit(solution)/shard_map/ppermute | solution.py:12
  26.5 3.8 collective-permute-start.3
  30.3 3.6 collective-permute-done.3
  38.3 4.8 %slice_bitcast_fusion = (bf16[64,12,8,512]{3,2,1,0:T(8,128)(2,1)S(1)}, bf16[64,12,8,512]{3,2,1,0:T(8,128)(2,1)}, bf16[64,12,8,512]{3,2,1,0:T(8,128)(2,1)S(1)}) fusion(bf16[96,66,512]{2,0,1:T(8,128)(2,1)S(1)} %pad_maximum_fusion.1), kind=kLoop, calls=%fused_computation.6 | loop fusion | bytes 37748736
  43.7 3.4 copy.44
  47.2 3.3 copy.45
  54.3 3.0 fusion
  57.3 10.4 %copy.33 = f32[32,32768]{0,1:T(8,128)} copy(f32[32,32768]{1,0:T(8,128)} %fusion) | data formatting | bytes 8388608 | tf_op jit(solution)/shard_map/add | solution.py:49
  67.7 11.8 %copy.34 = f32[32,16,4,128,4]{3,1,4,2,0:T(8,128)} copy(f32[32,16,4,128,4]{0,4,3,2,1:T(4,128)} %bitcast.155) | data formatting | bytes 8388608 | tf_op jit(solution)/shard_map/reshape | solution.py:50
  79.4 2.9 convert_reduce_fusion
  83.2 3.4 collective-permute-start.4
  88.5 4.5 %collective-permute-start.6 = (bf16[128,2048]{1,0:T(8,128)(2,1)S(1)}, bf16[128,2048]{1,0:T(8,128)(2,1)S(1)}, u32[]{:S(2)}, u32[]{:S(2)}) collective-permute-start(bf16[128,2048]{1,0:T(8,128)(2,1)S(1)} %bitcast.165), channel_id=1, source_target_pairs={{8,0},{16,8},{24,16},{32,24},{40,32},{48,40},{56,48},{64,56},{72,6... | collective-permute-start | bytes 1572872 | tf_op jit(solution)/shard_map/ppermute | solution.py:23
  95.5 5.3 %collective-permute-done.4 = bf16[128,2048]{1,0:T(8,128)(2,1)S(1)} collective-permute-done((bf16[128,2048]{1,0:T(8,128)(2,1)S(1)}, bf16[128,2048]{1,0:T(8,128)(2,1)S(1)}, u32[]{:S(2)}, u32[]{:S(2)}) %collective-permute-start.4) | collective-permute-done | bytes 524320 | tf_op jit(solution)/shard_map/ppermute | solution.py:23
  101.6 9.8 %collective-permute-done.5 = bf16[128,2048]{1,0:T(8,128)(2,1)S(1)} collective-permute-done((bf16[128,2048]{1,0:T(8,128)(2,1)S(1)}, bf16[128,2048]{1,0:T(8,128)(2,1)S(1)}, u32[]{:S(2)}, u32[]{:S(2)}) %collective-permute-start.5) | collective-permute-done | bytes 524320 | tf_op jit(solution)/shard_map/ppermute | solution.py:23
  114.0 8.8 %collective-permute-done.7 = bf16[128,2048]{1,0:T(8,128)(2,1)S(1)} collective-permute-done((bf16[128,2048]{1,0:T(8,128)(2,1)S(1)}, bf16[128,2048]{1,0:T(8,128)(2,1)S(1)}, u32[]{:S(2)}, u32[]{:S(2)}) %collective-permute-start.7) | collective-permute-done | bytes 524320 | tf_op jit(solution)/shard_map/ppermute | solution.py:23
  123.6 4.8 %collective-permute-start.8 = (bf16[5,128,2048]{2,1,0:T(8,128)(2,1)}, bf16[5,128,2048]{2,1,0:T(8,128)(2,1)}, u32[]{:S(2)}, u32[]{:S(2)}) collective-permute-start(bf16[5,128,2048]{2,1,0:T(8,128)(2,1)} %bitcast_dynamic-update-slice_fusion.1), channel_id=1, source_target_pairs={{0,1},{1,2},{2,3},{3,4},{4,5},{5,6},{6,7},{8,9},{9,10},{10,11},{11... | collective-permute-start | bytes 7864328 | tf_op jit(solution)/shard_map/ppermute | solution.py:23
  128.4 3.6 collective-permute-start.9
  135.4 52.6 %collective-permute-done.8 = bf16[5,128,2048]{2,1,0:T(8,128)(2,1)} collective-permute-done((bf16[5,128,2048]{2,1,0:T(8,128)(2,1)}, bf16[5,128,2048]{2,1,0:T(8,128)(2,1)}, u32[]{:S(2)}, u32[]{:S(2)}) %collective-permute-start.8) | collective-permute-done | bytes 2621472 | tf_op jit(solution)/shard_map/ppermute | solution.py:23
  188.0 55.2 %collective-permute-done.9 = bf16[5,128,2048]{2,1,0:T(8,128)(2,1)} collective-permute-done((bf16[5,128,2048]{2,1,0:T(8,128)(2,1)}, bf16[5,128,2048]{2,1,0:T(8,128)(2,1)}, u32[]{:S(2)}, u32[]{:S(2)}) %collective-permute-start.9) | collective-permute-done | bytes 2621472 | tf_op jit(solution)/shard_map/ppermute | solution.py:23
  243.2 6.8 %pad_maximum_fusion = bf16[3,5,128,2048]{3,2,1,0:T(8,128)(2,1)} fusion(bf16[1,5,128,2048]{3,2,1,0:T(8,128)(2,1)} %bitcast.14, bf16[1,5,128,2048]{3,2,1,0:T(8,128)(2,1)} %bitcast.13, bf16[1,5,128,2048]{3,2,1,0:T(8,128)(2,1)} %bitcast.12), kind=kLoop, calls=%fused_computation.4 | loop fusion | flops 7864320 | bytes 15728640 | tf_op jit(solution)/shard_map/stack | solution.py:103
  250.0 4.6 %convolution_bitcast_fusion.2 = f32[32,2048]{1,0:T(8,128)S(1)} fusion(bf16[32,128]{1,0:T(8,128)(2,1)S(1)} %copy-done.3, bf16[128,1920]{1,0:T(8,128)(2,1)S(1)} %copy-done, bf16[1920,2048]{1,0:T(8,128)(2,1)} %bitcast.157, bf16[2048,128]{0,1:T(8,128)(2,1)S(1)} %fusion.5), kind=kOutput, calls=%fused_computation.22 | convolution fusion | flops 1024458752 | bytes 9150464 | tf_op jit(solution)/shard_map/dot_general | solution.py:108
  255.0 6.0 %broadcast_in_dim.5 = f32[32,16,4,128,4]{0,4,3,2,1:T(4,128)} broadcast(f32[32,16,128]{0,2,1:T(8,128)S(1)} %bitcast.167), dimensions={0,1,3} | broadcast | bytes 4456448 | tf_op jit(solution)/shard_map/broadcast_in_dim | solution.py:111
  261.1 11.7 %copy.38 = f32[32,32768]{1,0:T(8,128)} copy(f32[32,32768]{0,1:T(8,128)} %bitcast.156) | data formatting | bytes 8388608 | tf_op jit(solution)/shard_map/reshape | solution.py:111
  272.7 4.6 %convolution_bitcast_fusion = f32[50,32768]{1,0:T(8,128)S(1)} fusion(bf16[50,32]{1,0:T(8,128)(2,1)S(1)} %reshape.1145, f32[32,32768]{1,0:T(8,128)} %copy.38, f32[32,32768]{1,0:T(8,128)} %fusion, f32[32]{0:T(128)S(1)} %copy-done.6, f32[32]{0:T(128)S(1)} %copy-done.4), kind=kOutput, calls=%fused_computation | convolution fusion | flops 113246208 | bytes 14945664 | tf_op jit(solution)/shard_map/dot_general | solution.py:121
  278.8 2.6 fusion.21
  283.6 4.2 %scatter-add.99 = f32[2,68,516]{2,1,0:T(8,128)S(1)} dynamic-update-slice(f32[2,68,516]{2,1,0:T(8,128)S(1)} %scatter-add.96, f32[2,64,512]{2,1,0:T(8,128)} %bitcast_add_fusion.20, s32[]{:T(128)} %constant.856.clone.1, s32[]{:T(128)} %bitcast.22, s32[]{:T(128)} %bitcast.23) | dynamic-update-slice | bytes 524292 | tf_op jit(solution)/shard_map/scatter-add | solution.py:131
  287.8 3.5 add_select_fusion.2
  291.3 4.1 scatter-add.100
  295.4 3.7 add_select_fusion.1
  299.0 4.3 %scatter-add.101 = f32[2,68,516]{2,1,0:T(8,128)S(1)} dynamic-update-slice(f32[2,68,516]{2,1,0:T(8,128)S(1)} %scatter-add.100, f32[2,64,512]{2,1,0:T(8,128)} %add_select_fusion.1, s32[]{:T(128)} %constant.856.clone.1, s32[]{:T(128)} %bitcast.26, s32[]{:T(128)} %bitcast.27) | dynamic-update-slice | bytes 524292 | tf_op jit(solution)/shard_map/scatter-add | solution.py:131
  303.3 3.6 add_select_fusion
  306.9 4.1 %scatter-add.104 = f32[2,68,516]{2,1,0:T(8,128)S(1)} dynamic-update-slice(f32[2,68,516]{2,1,0:T(8,128)S(1)} %scatter-add.101, f32[2,64,512]{2,1,0:T(8,128)} %add_select_fusion, s32[]{:T(128)} %constant.856.clone.1, s32[]{:T(128)} %bitcast.28, s32[]{:T(128)} %bitcast.29) | dynamic-update-slice | bytes 524292 | tf_op jit(solution)/shard_map/scatter-add | solution.py:131
  316.8 2.9 scatter-add.106
  321.5 2.9 scatter-add.109
  326.2 2.9 scatter-add.110
  331.0 2.9 scatter-add.111
  339.6 3.2 scatter-add.115
  344.6 2.9 scatter-add.116
  349.3 2.9 scatter-add.119
  354.1 2.9 scatter-add.120
  380.0 4.6 %collective-permute-done.10 = f32[2,68,2]{2,1,0:T(8,128)S(1)} collective-permute-done((f32[2,68,2]{2,1,0:T(8,128)S(1)}, f32[2,68,2]{2,1,0:T(8,128)S(1)}, u32[]{:S(2)}, u32[]{:S(2)}) %collective-permute-start.10) | collective-permute-done | bytes 1120 | tf_op jit(solution)/shard_map/ppermute | solution.py:23
  389.9 4.3 %collective-permute-start.12 = (f32[2,2,512]{2,1,0:T(2,128)S(1)}, f32[2,2,512]{2,1,0:T(2,128)S(1)}, u32[]{:S(2)}, u32[]{:S(2)}) collective-permute-start(f32[2,2,512]{2,1,0:T(2,128)S(1)} %slice.1132), channel_id=1, source_target_pairs={{0,1},{1,2},{2,3},{3,4},{4,5},{5,6},{6,7},{8,9},{9,10},{10,11},{11... | collective-permute-start | bytes 24584 | tf_op jit(solution)/shard_map/ppermute | solution.py:23
  394.4 3.5 collective-permute-done.12
  398.0 3.2 collective-permute-start.13
  401.2 3.8 collective-permute-done.13
  (111 shorter events, 81.2 us)
Async XLA Ops:
  0.0 250.0 %copy-start = (bf16[128,1920]{1,0:T(8,128)(2,1)S(1)}, bf16[128,1920]{1,0:T(8,128)(2,1)}, u32[]{:S(2)}) copy-start(bf16[128,1920]{1,0:T(8,128)(2,1)} %param.81) | copy-start | bytes 1474564
  6.6 14.3 %collective-permute-start = (bf16[32,64,1]{2,0,1:T(8,128)(2,1)S(1)}, bf16[32,64,1]{2,0,1:T(8,128)(2,1)S(1)}, u32[]{:S(2)}, u32[]{:S(2)}) collective-permute-start(bf16[32,64,1]{2,0,1:T(8,128)(2,1)S(1)} %get-tuple-element.389), channel_id=1, source_target_pairs={{0,8},{8,16},{16,24},{24,32},{32,40},{40,48},{48,56},{56,64},{64,7... | collective-permute-start | bytes 12296 | tf_op jit(solution)/shard_map/ppermute | solution.py:12
  8.5 13.2 %collective-permute-start.1 = (bf16[32,64,1]{2,0,1:T(8,128)(2,1)S(1)}, bf16[32,64,1]{2,0,1:T(8,128)(2,1)S(1)}, u32[]{:S(2)}, u32[]{:S(2)}) collective-permute-start(bf16[32,64,1]{2,0,1:T(8,128)(2,1)S(1)} %get-tuple-element.390), channel_id=1, source_target_pairs={{8,0},{16,8},{24,16},{32,24},{40,32},{48,40},{56,48},{64,56},{72,6... | collective-permute-start | bytes 12296 | tf_op jit(solution)/shard_map/ppermute | solution.py:15
  21.8 8.4 %collective-permute-start.2 = (bf16[32,1,514]{2,0,1:T(8,128)(2,1)S(1)}, bf16[32,1,514]{2,0,1:T(8,128)(2,1)S(1)}, u32[]{:S(2)}, u32[]{:S(2)}) collective-permute-start(bf16[32,1,514]{2,0,1:T(8,128)(2,1)S(1)} %get-tuple-element.384), channel_id=1, source_target_pairs={{0,1},{1,2},{2,3},{3,4},{4,5},{5,6},{6,7},{8,9},{9,10},{10,11},{11... | collective-permute-start | bytes 98696 | tf_op jit(solution)/shard_map/ppermute | solution.py:12
  26.5 7.4 %collective-permute-start.3 = (bf16[32,1,514]{2,0,1:T(8,128)(2,1)S(1)}, bf16[32,1,514]{2,0,1:T(8,128)(2,1)S(1)}, u32[]{:S(2)}, u32[]{:S(2)}) collective-permute-start(bf16[32,1,514]{2,0,1:T(8,128)(2,1)S(1)} %get-tuple-element.385), channel_id=1, source_target_pairs={{1,0},{2,1},{3,2},{4,3},{5,4},{6,5},{7,6},{9,8},{10,9},{11,10},{12... | collective-permute-start | bytes 98696 | tf_op jit(solution)/shard_map/ppermute | solution.py:15
  47.2 3.3 copy-start.1
  51.4 2.2 slice-start
  51.4 2.9 slice-start.1
  67.7 11.8 %copy-start.4 = (f32[32]{0:T(128)S(1)}, f32[32]{0:T(128)}, u32[]{:S(2)}) copy-start(f32[32]{0:T(128)} %param.78) | copy-start | bytes 388
  79.4 3.4 copy-start.2
  79.4 3.4 copy-start.7
  82.7 49.4 %copy-start.5 = (bf16[2,800]{1,0:T(2,128)(2,1)S(1)}, bf16[2,800]{1,0:T(2,128)(2,1)}, u32[]{:S(2)}) copy-start(bf16[2,800]{1,0:T(2,128)(2,1)} %param.84) | copy-start | bytes 9604
  82.7 52.0 %copy-start.9 = (s32[3]{0:T(128)S(1)}, s32[3]{0:T(128)}, u32[]{:S(2)}) copy-start(s32[3]{0:T(128)} %constant.859.clone.1) | copy-start | bytes 40
  83.2 17.6 %collective-permute-start.4 = (bf16[128,2048]{1,0:T(8,128)(2,1)S(1)}, bf16[128,2048]{1,0:T(8,128)(2,1)S(1)}, u32[]{:S(2)}, u32[]{:S(2)}) collective-permute-start(bf16[128,2048]{1,0:T(8,128)(2,1)S(1)} %bitcast.163), channel_id=1, source_target_pairs={{0,16},{8,24},{16,32},{24,40},{32,48},{40,56},{48,64},{56,72},{64,... | collective-permute-start | bytes 1572872 | tf_op jit(solution)/shard_map/ppermute | solution.py:23
  86.5 24.9 %collective-permute-start.5 = (bf16[128,2048]{1,0:T(8,128)(2,1)S(1)}, bf16[128,2048]{1,0:T(8,128)(2,1)S(1)}, u32[]{:S(2)}, u32[]{:S(2)}) collective-permute-start(bf16[128,2048]{1,0:T(8,128)(2,1)S(1)} %bitcast.164), channel_id=1, source_target_pairs={{0,8},{8,16},{16,24},{24,32},{32,40},{40,48},{48,56},{56,64},{64,7... | collective-permute-start | bytes 1572872 | tf_op jit(solution)/shard_map/ppermute | solution.py:23
  88.5 24.7 %collective-permute-start.6 = (bf16[128,2048]{1,0:T(8,128)(2,1)S(1)}, bf16[128,2048]{1,0:T(8,128)(2,1)S(1)}, u32[]{:S(2)}, u32[]{:S(2)}) collective-permute-start(bf16[128,2048]{1,0:T(8,128)(2,1)S(1)} %bitcast.165), channel_id=1, source_target_pairs={{8,0},{16,8},{24,16},{32,24},{40,32},{48,40},{56,48},{64,56},{72,6... | collective-permute-start | bytes 1572872 | tf_op jit(solution)/shard_map/ppermute | solution.py:23
  93.0 29.8 %collective-permute-start.7 = (bf16[128,2048]{1,0:T(8,128)(2,1)S(1)}, bf16[128,2048]{1,0:T(8,128)(2,1)S(1)}, u32[]{:S(2)}, u32[]{:S(2)}) collective-permute-start(bf16[128,2048]{1,0:T(8,128)(2,1)S(1)} %bitcast.166), channel_id=1, source_target_pairs={{16,0},{24,8},{32,16},{40,24},{48,32},{56,40},{64,48},{72,56},{80,... | collective-permute-start | bytes 1572872 | tf_op jit(solution)/shard_map/ppermute | solution.py:23
  123.6 64.4 %collective-permute-start.8 = (bf16[5,128,2048]{2,1,0:T(8,128)(2,1)}, bf16[5,128,2048]{2,1,0:T(8,128)(2,1)}, u32[]{:S(2)}, u32[]{:S(2)}) collective-permute-start(bf16[5,128,2048]{2,1,0:T(8,128)(2,1)} %bitcast_dynamic-update-slice_fusion.1), channel_id=1, source_target_pairs={{0,1},{1,2},{2,3},{3,4},{4,5},{5,6},{6,7},{8,9},{9,10},{10,11},{11... | collective-permute-start | bytes 7864328 | tf_op jit(solution)/shard_map/ppermute | solution.py:23
  128.4 114.7 %collective-permute-start.9 = (bf16[5,128,2048]{2,1,0:T(8,128)(2,1)}, bf16[5,128,2048]{2,1,0:T(8,128)(2,1)}, u32[]{:S(2)}, u32[]{:S(2)}) collective-permute-start(bf16[5,128,2048]{2,1,0:T(8,128)(2,1)} %bitcast_dynamic-update-slice_fusion.1), channel_id=1, source_target_pairs={{1,0},{2,1},{3,2},{4,3},{5,4},{6,5},{7,6},{9,8},{10,9},{11,10},{12... | collective-permute-start | bytes 7864328 | tf_op jit(solution)/shard_map/ppermute | solution.py:23
  243.2 6.9 %copy-start.3 = (bf16[32,128]{1,0:T(8,128)(2,1)S(1)}, bf16[32,128]{1,0:T(8,128)(2,1)}, u32[]{:S(2)}) copy-start(bf16[32,128]{1,0:T(8,128)(2,1)} %param.82) | copy-start | bytes 24580
  261.1 11.7 %copy-start.6 = (f32[32]{0:T(128)S(1)}, f32[32]{0:T(128)}, u32[]{:S(2)}) copy-start(f32[32]{0:T(128)} %param.83) | copy-start | bytes 388
  368.4 36.6 %copy-start.8 = (f32[2]{0:T(128)S(1)}, f32[2]{0:T(128)}, u32[]{:S(2)}) copy-start(f32[2]{0:T(128)} %param.85) | copy-start | bytes 28
  378.1 6.6 %collective-permute-start.10 = (f32[2,68,2]{2,1,0:T(8,128)S(1)}, f32[2,68,2]{2,1,0:T(8,128)S(1)}, u32[]{:S(2)}, u32[]{:S(2)}) collective-permute-start(f32[2,68,2]{2,1,0:T(8,128)S(1)} %slice.1127), channel_id=1, source_target_pairs={{0,8},{8,16},{16,24},{24,32},{32,40},{40,48},{48,56},{56,64},{64,7... | collective-permute-start | bytes 3272 | tf_op jit(solution)/shard_map/ppermute | solution.py:23
  385.6 3.9 collective-permute-start.11
  389.9 7.9 %collective-permute-start.12 = (f32[2,2,512]{2,1,0:T(2,128)S(1)}, f32[2,2,512]{2,1,0:T(2,128)S(1)}, u32[]{:S(2)}, u32[]{:S(2)}) collective-permute-start(f32[2,2,512]{2,1,0:T(2,128)S(1)} %slice.1132), channel_id=1, source_target_pairs={{0,1},{1,2},{2,3},{3,4},{4,5},{5,6},{6,7},{8,9},{9,10},{10,11},{11... | collective-permute-start | bytes 24584 | tf_op jit(solution)/shard_map/ppermute | solution.py:23
  398.0 7.0 %collective-permute-start.13 = (f32[2,2,512]{2,1,0:T(2,128)S(1)}, f32[2,2,512]{2,1,0:T(2,128)S(1)}, u32[]{:S(2)}, u32[]{:S(2)}) collective-permute-start(f32[2,2,512]{2,1,0:T(2,128)S(1)} %slice.1134), channel_id=1, source_target_pairs={{1,0},{2,1},{3,2},{4,3},{5,4},{6,5},{7,6},{9,8},{10,9},{11,10},{12... | collective-permute-start | bytes 24584 | tf_op jit(solution)/shard_map/ppermute | solution.py:23
where the time goes:
time: 412 us; the launch traced here: 406 us
  waiting for transfers between devices  158 us (38%)
  local copies, waits for them, and re-layouts  132 us (32%)
  other arithmetic  48 us (12%)
  starting transfers between devices  46.9 us (11%)
  matrix products  20 us (5%)
    ppermute x10, waiting for transfers between devices, passed_along(): return lax.ppermute(block, axis, route)  146 us
    scatter-add x25, local copies, waits for them, and re-layouts, body(): extended.at[:, row_off:row_off + row_count, col_off:col_off + col_count]  63.8 us
    ppermute x10, starting transfers between devices, passed_along(): return lax.ppermute(block, axis, route)  32.1 us
    add x21, other arithmetic, body(): extended.at[:, row_off:row_off + row_count, col_off:col_off + col_count]  21.8 us
    reshape x1, local copies, waits for them, and re-layouts, conv_rows(): return summed.reshape(-1, row_count, col_count)  11.8 us
    reshape x1, local copies, waits for them, and re-layouts, body(): jnp.broadcast_to(lifted, (channels, pool_rows, 4, pool_cols, 4))  11.7 us
    another operation x6, other arithmetic  11.5 us
    add x1, local copies, waits for them, and re-layouts, conv_rows(): summed + jnp.dot(part_w, window, preferred_element_type=jnp.float32)  10.4 us
  transfers between devices with their start and end apart: 14, of which 12 were waited for; matrix products, arithmetic and copies ran while one was open for 2% of the time, Pallas kernels for 0%

commit v1 on v0

v1 whole, which is shorter than its diff:
```python
import functools

import jax
import jax.numpy as jnp
from jax import lax
from jax.experimental import pallas as pl
from jax.experimental.pallas import tpu as pltpu
from jax.sharding import PartitionSpec as P

ROWS, COLS = 64, 512
CH, WIDE, KINDS = 32, 128, 8
POOL_ROWS, POOL_COLS = 16, 128
SPOTS = POOL_ROWS * POOL_COLS
VMEM = pl.BlockSpec(memory_space=pltpu.VMEM)
SMEM = pl.BlockSpec(memory_space=pltpu.SMEM)
F32, BF16 = jnp.float32, jnp.bfloat16


def iota(shape, dim):
    return lax.broadcasted_iota(jnp.int32, shape, dim)


def shape_of(*dims, dtype=F32):
    return jax.ShapeDtypeStruct(dims, dtype)


def params():
    return pltpu.CompilerParams(vmem_limit_bytes=56 * 1024 * 1024)


def mm(a, b):
    return jnp.dot(a, b, preferred_element_type=F32)


def column(row):
    count = row.shape[1]
    eye = iota((count, count), 0) == iota((count, count), 1)
    return jnp.sum(jnp.where(eye, row, 0.0), axis=1, keepdims=True)


def halo_kernel(rasters, aerial, col_low, col_high, row_low, row_high, corners):
    lane = iota((ROWS, 128), 1)
    for out, x, at in ((col_low, 0, 0), (col_high, COLS - 128, 127)):
        packed = jnp.zeros((ROWS, 128), F32)
        for kind in range(5):
            if kind < 4:
                slab = rasters[kind, :, x : x + 128].astype(F32)
            else:
                slab = aerial[:, x : x + 128]
            packed = jnp.where(lane == kind, slab[:, at : at + 1], packed)
        out[...] = packed
    rows = []
    for out, y in ((row_low, 0), (row_high, ROWS - 1)):
        parts = [rasters[kind, y : y + 1, :].astype(F32) for kind in range(4)]
        parts += [aerial[y : y + 1, :], jnp.zeros((3, COLS), F32)]
        rows.append(jnp.concatenate(parts, axis=0))
        out[...] = rows[-1]
    lane = iota((KINDS, 128), 1)
    packed = jnp.zeros((KINDS, 128), F32)
    spots = [(0, 0), (0, COLS - 1), (1, 0), (1, COLS - 1)]
    for spot, (which, x) in enumerate(spots):
        packed = jnp.where(lane == spot, rows[which][:, x : x + 1], packed)
    corners[...] = packed


def features_kernel(
    cells, place, rasters, aerial, left, right, above, below, c_tl, c_tr, c_bl, c_br,
    kinds_w, conv_w, conv_b, features, pooled, stem_w, wide_w, pool_w, stem3,
):
    last_cross, last_band = cells
    has_above = (place[0] > 0).astype(F32)
    has_below = (place[0] < last_cross).astype(F32)
    has_left = (place[1] > 0).astype(F32)
    has_right = (place[1] < last_band).astype(F32)

    kinds = kinds_w[...]
    spread = jnp.where(iota((KINDS, 64), 1) // 8 == iota((KINDS, 64), 0), 1.0, 0.0).astype(BF16)
    same = iota((256, 64), 0) // CH == iota((256, 64), 1) % 8
    high = kinds.astype(BF16)
    low = (kinds - high.astype(F32)).astype(BF16)
    halves = []
    for part in (high, low):
        rows = mm(jnp.concatenate([part] * 8, axis=0), spread)
        halves.append(jnp.where(same, rows, 0.0))
    stem_w[...] = jnp.concatenate(halves, axis=1).astype(BF16)

    pool_w[...] = jnp.where(
        iota((COLS, POOL_COLS), 0) // 4 == iota((COLS, POOL_COLS), 1), 1.0 / 16, 0.0
    ).astype(BF16)

    wide_w[...] = jnp.zeros(wide_w.shape, BF16)
    taps = conv_w[...]
    for y in range(8):
        wide_w[y * CH : (y + 1) * CH, y * 96 : y * 96 + 288] = taps

    def stem(values, aerial_part, ones):
        top = aerial_part.astype(BF16)
        rest = (aerial_part - top.astype(F32)).astype(BF16)
        x = jnp.concatenate(
            [values.astype(BF16), jnp.concatenate([top, rest], axis=0),
             jnp.concatenate([ones, jnp.zeros_like(ones)], axis=0).astype(BF16)], axis=0
        )
        out = mm(stem_w[...], jnp.concatenate([x, x], axis=0))
        return jnp.maximum(out, 0.0)

    def put(first, s):
        shifted_up = pltpu.roll(s, 1, 1)[:, :COLS].astype(BF16)
        shifted_down = pltpu.roll(s, COLS + 127, 1)[:, :COLS].astype(BF16)
        middle = s[:, :COLS].astype(BF16)
        stem3[pl.ds(first, 96), :] = jnp.concatenate([shifted_up, middle, shifted_down], axis=0)

    lane8 = iota((8, 128), 1)

    def stem_rows(block, carry):
        y = pl.multiple_of(block * 8, 8)
        low_cols = left[pl.ds(y, 8), :] * has_left
        high_cols = right[pl.ds(y, 8), :] * has_right

        def edge(kind):
            return jnp.where(
                lane8 == 127, low_cols[:, kind : kind + 1],
                jnp.where(lane8 == 0, high_cols[:, kind : kind + 1], 0.0),
            )

        values = [
            jnp.concatenate([rasters[k, pl.ds(y, 8), :].astype(F32), edge(k)], axis=1)
            for k in range(4)
        ]
        aerial_part = jnp.concatenate([aerial[pl.ds(y, 8), :], edge(4)], axis=1)
        edge_ones = jnp.where(lane8 == 127, has_left, jnp.where(lane8 == 0, has_right, 0.0))
        ones = jnp.concatenate([jnp.ones((8, COLS), F32), edge_ones], axis=1)
        out = stem(jnp.concatenate(values, axis=0), aerial_part, ones)
        for r in range(8):
            first = pl.multiple_of((block * 8 + r + 1) * 96, 96)
            put(first, out[r * CH : (r + 1) * CH, :])
        return carry

    lax.fori_loop(0, ROWS // 8, stem_rows, 0)

    row8 = iota((8, 640), 0)
    upper, lower = above[...] * has_above, below[...] * has_below
    tl = c_tl[...] * (has_above * has_left)
    tr = c_tr[...] * (has_above * has_right)
    bl = c_bl[...] * (has_below * has_left)
    br = c_br[...] * (has_below * has_right)

    def rim(kind):
        up = jnp.where(
            lane8 == 127, tl[kind : kind + 1, 3:4],
            jnp.where(lane8 == 0, tr[kind : kind + 1, 2:3], 0.0),
        )
        down = jnp.where(
            lane8 == 127, bl[kind : kind + 1, 1:2],
            jnp.where(lane8 == 0, br[kind : kind + 1, 0:1], 0.0),
        )
        up = jnp.concatenate([jnp.broadcast_to(upper[kind : kind + 1, :], (8, COLS)), up], axis=1)
        down = jnp.concatenate([jnp.broadcast_to(lower[kind : kind + 1, :], (8, COLS)), down], axis=1)
        return jnp.where(row8 == 0, up, jnp.where(row8 == 1, down, 0.0))

    up = jnp.where(lane8 == 127, has_left, jnp.where(lane8 == 0, has_right, 0.0))
    side = jnp.concatenate([jnp.ones((8, COLS), F32), up], axis=1)
    ones = jnp.where(row8 == 0, side * has_above, jnp.where(row8 == 1, side * has_below, 0.0))
    out = stem(jnp.concatenate([rim(k) for k in range(4)], axis=0), rim(4), ones)
    put(0, out[:CH, :])
    put((ROWS + 1) * 96, out[CH : 2 * CH, :])

    bias = jnp.concatenate([jnp.broadcast_to(column(conv_b[...]), (CH, COLS))] * 8, axis=0)

    def conv_rows(block, carry):
        first = pl.multiple_of(block * 8 * 96, 96)
        out = mm(wide_w[...], stem3[pl.ds(first, 960), :])
        value = jnp.maximum(out + bias, 0.0).astype(BF16)
        features[pl.ds(pl.multiple_of(block * 256, 256), 256), :] = value
        means = mm(value, pool_w[...])
        for half in range(2):
            part = means[half * 128 : (half + 1) * 128, :]
            total = (part[:32] + part[32:64]) + (part[64:96] + part[96:])
            at = pl.multiple_of((block * 2 + half) * POOL_COLS, POOL_COLS)
            pooled[:, pl.ds(at, POOL_COLS)] = total.astype(BF16)
        return carry

    lax.fori_loop(0, ROWS // 8, conv_rows, 0)


def logits_kernel(
    cells, place, features, *rest,
):
    (maps, (proj_w, proj_b, ctx_w, up_w, up_b, head_w, rim_w, head_b),
     (logits, col_out, row_out, corner_out),
     (weights, proj, low_up, lifted, decoded)) = (rest[:15], rest[15:23], rest[23:27], rest[27:])
    last_cross, last_band = cells
    cross, band = place[0], place[1]
    core = band % 2
    sign = 1 - 2 * core

    for at in range(15):
        u, v = at // 5 - 1, at % 5 - 2
        row, col = cross + u, band + v * sign
        inside = (row >= 0) & (row <= last_cross) & (col >= 0) & (col <= last_band)
        mirrored = (at // 5) * 5 + (4 - at % 5)
        one = ctx_w[:, at * WIDE : (at + 1) * WIDE]
        two = ctx_w[:, mirrored * WIDE : (mirrored + 1) * WIDE]
        chosen = jnp.where(core == 0, one, two)
        weights[:, at * WIDE : (at + 1) * WIDE] = jnp.where(inside, chosen, jnp.zeros_like(chosen))

    p_bias = jnp.broadcast_to(column(proj_b[...]), (WIDE, 256))
    u_bias = jnp.broadcast_to(column(up_b[...]), (CH, 256))

    def context_part(part, carry):
        at = pl.multiple_of(part * 256, 256)
        for k in range(15):
            out = mm(proj_w[...], maps[k][:, pl.ds(at, 256)])
            proj[k * WIDE : (k + 1) * WIDE, :] = jnp.maximum(out + p_bias, 0.0).astype(BF16)
        context = mm(weights[...], proj[...]) + proj[7 * WIDE : 8 * WIDE, :].astype(F32)
        mixed = jnp.maximum(context, 0.0).astype(BF16)
        up = mm(up_w[...], mixed) + u_bias
        high = up.astype(BF16)
        low = (up - high.astype(F32)).astype(BF16)
        both = [
            jnp.concatenate([high[:, h * 128 : (h + 1) * 128], low[:, h * 128 : (h + 1) * 128]], axis=1)
            for h in range(2)
        ]
        low_up[pl.ds(pl.multiple_of(part * 64, 64), 64), :] = jnp.concatenate(both, axis=0)
        return carry

    lax.fori_loop(0, SPOTS // 256, context_part, 0)

    widen = jnp.where(
        iota((256, COLS), 0) % 128 == iota((256, COLS), 1) // 4, 1.0, 0.0
    ).astype(BF16)
    lifted[...] = mm(low_up[...], widen)

    decoded[0:64, :] = jnp.zeros((64, COLS), BF16)
    decoded[66 * CH :, :] = jnp.zeros((64, COLS), BF16)

    def decode(p, carry):
        up = lifted[pl.ds(pl.multiple_of(p * CH, CH), CH), :]
        for r in range(4):
            at = pl.multiple_of((4 * p + r) * CH, CH)
            value = jnp.maximum(features[pl.ds(at, CH), :].astype(F32) + up, 0.0).astype(BF16)
            decoded[pl.ds(pl.multiple_of(at + 64, CH), CH), :] = value
        return carry

    lax.fori_loop(0, POOL_ROWS, decode, 0)

    def gather_taps(z, count):
        total = None
        for dx in range(5):
            part = z[dx * count : (dx + 1) * count, :]
            part = jnp.concatenate([part, jnp.zeros((count, 128), F32)], axis=1)
            if dx != 2:
                part = pltpu.roll(part, (dx - 2) % 640, 1)
            total = part if total is None else total + part
        return total

    lane16 = iota((16, 128), 1)
    first_lanes = (lane16 < 2) | (lane16 >= 126)

    def head(block, carry):
        first = pl.multiple_of(block * 16 * CH, 16 * CH)
        total = gather_taps(mm(head_w[...], decoded[pl.ds(first, 20 * CH), :]), 32)
        y = pl.multiple_of(block * 16, 16)
        for k in range(2):
            logits[k, pl.ds(y, 16), :] = total[k * 16 : (k + 1) * 16, :COLS] + head_b[k]
        rim = total[:, COLS:]
        col_out[pl.ds(y, 16), :] = jnp.where(first_lanes, rim[:16], pltpu.roll(rim[16:], 4, 1))
        return carry

    lax.fori_loop(0, ROWS // 16, head, 0)

    ends = jnp.concatenate([decoded[64:128, :], decoded[64 * CH : 66 * CH, :]], axis=0)
    total = gather_taps(mm(rim_w[...], ends), 8)
    row_out[...] = total[:, :COLS]
    corner_out[...] = total[:, COLS:]


def sum_kernel(cells, place, inner, left, right, above, below, c_tl, c_tr, c_bl, c_br, out):
    last_cross, last_band = cells
    has_above = (place[0] > 0).astype(F32)
    has_below = (place[0] < last_cross).astype(F32)
    has_left = (place[1] > 0).astype(F32)
    has_right = (place[1] < last_band).astype(F32)
    out[...] = inner[...]
    lane = iota((ROWS, 128), 1)
    low, high = left[...] * has_left, right[...] * has_right
    for k in range(2):
        part = low if k == 0 else pltpu.roll(low, 124, 1)
        out[k, :, 0:128] += jnp.where(lane < 2, part, 0.0)
        part = high if k == 0 else pltpu.roll(high, 124, 1)
        out[k, :, COLS - 128 : COLS] += jnp.where(lane >= 126, part, 0.0)
    lane2 = iota((2, 128), 1)
    upper, lower = above[...] * has_above, below[...] * has_below
    tl = c_tl[...] * (has_above * has_left)
    tr = c_tr[...] * (has_above * has_right)
    bl = c_bl[...] * (has_below * has_left)
    br = c_br[...] * (has_below * has_right)
    none = jnp.zeros((2, COLS - 256), F32)
    for k in range(2):
        arrived = slice(4 * k + 2, 4 * k + 4)
        sides = [jnp.where(lane2 < 2, tl[arrived], 0.0), none, jnp.where(lane2 >= 126, tr[arrived], 0.0)]
        out[k, 0:2, :] += upper[arrived] + jnp.concatenate(sides, axis=1)
        arrived = slice(4 * k, 4 * k + 2)
        sides = [jnp.where(lane2 < 2, bl[arrived], 0.0), none, jnp.where(lane2 >= 126, br[arrived], 0.0)]
        out[k, ROWS - 2 : ROWS, :] += lower[arrived] + jnp.concatenate(sides, axis=1)


def call(kernel, outs, args, spaces=None, scratch=()):
    return pl.pallas_call(
        kernel,
        out_shape=outs,
        in_specs=spaces or [VMEM] * len(args),
        out_specs=jax.tree.map(lambda _: VMEM, outs),
        scratch_shapes=list(scratch),
        compiler_params=params(),
    )(*args)


def body(
    n_cross, n_band, rasters, aerial, w_in, aerial_gain, b_in, w_conv1, b_conv1, w_proj, b_proj,
    w_ctx, w_up, b_up, w_head, b_head,
):
    cells = (n_cross - 1, n_band - 1)
    place = jnp.stack([lax.axis_index("cross"), lax.axis_index("band")]).astype(jnp.int32)

    def moved(x, source):
        route = []
        for cross in range(n_cross):
            for band in range(n_band):
                c, b = source(cross, band)
                route.append(((b % n_band) * n_cross + c % n_cross, band * n_cross + cross))
        return lax.ppermute(x, ("band", "cross"), route)

    def fetched(x, u, v):
        return moved(x, lambda c, b: (c + u, b + v))

    def around(cols, rows, corners):
        return [
            fetched(cols[0], 0, -1), fetched(cols[1], 0, 1),
            fetched(rows[0], -1, 0), fetched(rows[1], 1, 0),
            fetched(corners, -1, -1), fetched(corners, -1, 1),
            fetched(corners, 1, -1), fetched(corners, 1, 1),
        ]

    col_low, col_high, row_low, row_high, corners = call(
        halo_kernel,
        [shape_of(ROWS, 128)] * 2 + [shape_of(KINDS, COLS)] * 2 + [shape_of(KINDS, 128)],
        [rasters, aerial],
    )
    rims = around((col_high, col_low), (row_high, row_low), corners)

    gain = aerial_gain[:, None]
    kinds_w = jnp.concatenate([w_in, gain, gain, b_in[:, None], jnp.zeros_like(gain)], axis=1)
    features, pooled = call(
        functools.partial(features_kernel, cells),
        [shape_of(ROWS * CH, COLS, dtype=BF16), shape_of(CH, SPOTS, dtype=BF16)],
        [place, rasters, aerial, *rims, kinds_w, w_conv1, b_conv1[None, :]],
        [SMEM] + [VMEM] * 13,
        [
            pltpu.VMEM((256, 128), BF16),
            pltpu.VMEM((256, 960), BF16),
            pltpu.VMEM((COLS, POOL_COLS), BF16),
            pltpu.VMEM(((ROWS + 2) * 96, COLS), BF16),
        ],
    )

    def far(x, u):
        return moved(x, lambda c, b: (c + u, b + 2 - 4 * (b % 2)))

    def other(x, u):
        return moved(x, lambda c, b: (c + u, b - 2 + 4 * (b % 2)))

    def partner(x):
        return moved(x, lambda c, b: (c, b ^ 1))

    maps = []
    for u in (-1, 0, 1):
        own = pooled if u == 0 else fetched(pooled, u, 0)
        away = far(pooled, u)
        maps.append([other(pooled, u), partner(away), own, partner(own), away])
    maps = sum(maps, [])

    taps = w_head.reshape(2, 5, 5, CH)[:, ::-1].transpose(2, 0, 1, 3).reshape(10, 5 * CH)
    skewed = jnp.broadcast_to(jnp.pad(taps, ((0, 0), (0, 16 * CH)))[:, None, :], (10, 16, 21 * CH))
    head_w = skewed.reshape(10, 16 * 21 * CH)[:, : 16 * 20 * CH].reshape(160, 20 * CH)
    gap = jnp.zeros((10, CH), BF16)
    at = [taps[:, (4 - d) * CH : (5 - d) * CH] for d in range(5)]
    rim_rows = [[at[0], gap, gap, gap], [at[1], at[0], gap, gap], [gap, gap, at[4], at[3]], [gap, gap, gap, at[4]]]
    rim_w = jnp.stack([jnp.concatenate(r, axis=1) for r in rim_rows], axis=1).reshape(40, 4 * CH)

    inner, col_out, row_out, corner_out = call(
        functools.partial(logits_kernel, cells),
        [shape_of(2, ROWS, COLS), shape_of(ROWS, 128), shape_of(8, COLS), shape_of(8, 128)],
        [place, features, *maps, w_proj, b_proj[None, :], w_ctx, w_up, b_up[None, :], head_w, rim_w, b_head],
        [SMEM] + [VMEM] * 23 + [SMEM],
        [
            pltpu.VMEM((WIDE, 15 * WIDE), BF16),
            pltpu.VMEM((15 * WIDE, 256), BF16),
            pltpu.VMEM((POOL_ROWS * CH, 256), BF16),
            pltpu.VMEM((POOL_ROWS * CH, COLS), F32),
            pltpu.VMEM(((ROWS + 4) * CH, COLS), BF16),
        ],
    )
    rims = around((col_out, col_out), (row_out, row_out), corner_out)
    return call(
        functools.partial(sum_kernel, cells),
        shape_of(2, ROWS, COLS),
        [place, inner, *rims],
        [SMEM] + [VMEM] * 9,
    )


def solution(mesh):
    sizes = dict(mesh.shape)
    return jax.shard_map(
        functools.partial(body, sizes["cross"], sizes["band"]),
        mesh=mesh,
        in_specs=(P(None, "cross", "band"), P("cross", "band")) + (P(),) * 12,
        out_specs=P(None, "cross", "band"),
        check_vma=False,
    )
```

time: 412 us -> 117 us (0.28)
  the two profiles are of different devices: /device:TPU:40 before, /device:TPU:0 now
where the time goes in v1:
time: 117 us
  starting transfers between devices  45.7 us (39%)
  waiting for transfers between devices  34.7 us (30%)
  Pallas kernels  27.6 us (24%)
  local copies, waits for them, and re-layouts  7.76 us (7%)
    ppermute x30, starting transfers between devices, moved(): return lax.ppermute(x, ('band', 'cross'), route)  45.7 us
    ppermute x30, waiting for transfers between devices, moved(): return lax.ppermute(x, ('band', 'cross'), route)  34.7 us
    pallas_call x4, Pallas kernels, call(): pl.pallas_call(kernel, out_shape=outs, in_specs=spaces or [VMEM] * len(ar...  27.6 us
    unnamed x61, local copies, waits for them, and re-layouts  3.33 us
  transfers between devices with their start and end apart: 30, of which 9 were waited for; matrix products, arithmetic and copies ran while one was open for 6% of the time, Pallas kernels for 0%

profile of v1, /device:TPU:0, one launch (start us, length us, event | category | flops | bytes accessed | tf_op | source)
XLA Modules:
  0.0 116.8 jit_solution(10703894093587276095)
XLA Ops:
  0.0 1.8 %shard_map.136 = (f32[64,128]{1,0:T(8,128)}, f32[64,128]{1,0:T(8,128)}, f32[8,512]{1,0:T(8,128)}, f32[8,512]{1,0:T(8,128)}, f32[8,128]{1,0:T(8,128)}) custom-call(s32[4,64,512]{2,1,0:T(8,128)} %rasters.3, f32[64,512]{1,0:T(8,128)} %aerial.3), custom_call_target="tpu_custom_call" | custom-call | tf_op jit(solution)/shard_map/pallas_call | solution.py:308
  1.8 8.2 %collective-permute-start.7 = (f32[8,128]{1,0:T(8,128)}, f32[8,128]{1,0:T(8,128)S(1)}, u32[]{:S(2)}, u32[]{:S(2)}) collective-permute-start(f32[8,128]{1,0:T(8,128)} %get-tuple-element.20), channel_id=1, source_target_pairs={{9,0},{17,8},{25,16},{33,24},{41,32},{49,40},{57,48},{65,56},{73,6... | collective-permute-start | bytes 12296 | tf_op jit(solution)/shard_map/ppermute | solution.py:331
  10.1 5.1 %collective-permute-start.5 = (f32[8,128]{1,0:T(8,128)}, f32[8,128]{1,0:T(8,128)S(1)}, u32[]{:S(2)}, u32[]{:S(2)}) collective-permute-start(f32[8,128]{1,0:T(8,128)} %get-tuple-element.20), channel_id=1, source_target_pairs={{15,0},{23,8},{31,16},{39,24},{47,32},{55,40},{63,48},{71,56},{79,... | collective-permute-start | bytes 12296 | tf_op jit(solution)/shard_map/ppermute | solution.py:331
  15.1 0.8 reshape.16
  15.9 5.7 %collective-permute-start.3 = (f32[8,512]{1,0:T(8,128)}, f32[8,512]{1,0:T(8,128)S(1)}, u32[]{:S(2)}, u32[]{:S(2)}) collective-permute-start(f32[8,512]{1,0:T(8,128)} %get-tuple-element.19), channel_id=1, source_target_pairs={{1,0},{9,8},{17,16},{25,24},{33,32},{41,40},{49,48},{57,56},{65,64... | collective-permute-start | bytes 49160 | tf_op jit(solution)/shard_map/ppermute | solution.py:331
  21.7 3.8 %collective-permute-start.1 = (f32[64,128]{1,0:T(8,128)}, f32[64,128]{1,0:T(8,128)S(1)}, u32[]{:S(2)}, u32[]{:S(2)}) collective-permute-start(f32[64,128]{1,0:T(8,128)} %get-tuple-element.17), channel_id=1, source_target_pairs={{8,0},{16,8},{24,16},{32,24},{40,32},{48,40},{56,48},{64,56},{72,6... | collective-permute-start | bytes 98312 | tf_op jit(solution)/shard_map/ppermute | solution.py:331
  25.5 0.6 pad_add_fusion.place
  26.1 0.8 concatenate.17
  26.9 0.7 copy.31.kinds_w
  27.5 0.1 reshape.17
  27.7 0.5 copy-done.25
  28.3 11.2 %shard_map.137 = (bf16[2048,512]{1,0:T(8,128)(2,1)}, bf16[32,2048]{1,0:T(8,128)(2,1)}) custom-call(s32[2]{0:T(128)} %pad_add_fusion.place, s32[4,64,512]{2,1,0:T(8,128)} %rasters.3, f32[64,512]{1,0:T(8,128)} %aerial.3, f32[64,128]{1,0:T(8,128)} %copy-done.16, f32[64,128]{1,0:T(8,128)} %copy-done.17, f32[8,512]{1,0:T(8,128)} %copy-done.18, ...), custom_call_target="tpu_custom_call" | custom-call | tf_op jit(solution)/shard_map/pallas_call | solution.py:308
  39.5 2.2 %collective-permute-start.20 = (bf16[32,2048]{1,0:T(8,128)(2,1)}, bf16[32,2048]{1,0:T(8,128)(2,1)S(1)}, u32[]{:S(2)}, u32[]{:S(2)}) collective-permute-start(bf16[32,2048]{1,0:T(8,128)(2,1)} %get-tuple-element.22.rest_7_), channel_id=1, source_target_pairs={{1,0},{9,8},{17,16},{25,24},{33,32},{41,40},{49,48},{57,56},{65,64... | collective-permute-start | bytes 393224 | tf_op jit(solution)/shard_map/ppermute | solution.py:331
  41.7 1.9 %collective-permute-start.17 = (bf16[32,2048]{1,0:T(8,128)(2,1)}, bf16[32,2048]{1,0:T(8,128)(2,1)S(1)}, u32[]{:S(2)}, u32[]{:S(2)}) collective-permute-start(bf16[32,2048]{1,0:T(8,128)(2,1)} %get-tuple-element.22.rest_7_), channel_id=1, source_target_pairs={{113,0},{25,8},{1,16},{41,24},{17,32},{57,40},{33,48},{73,56},{49,... | collective-permute-start | bytes 393224 | tf_op jit(solution)/shard_map/ppermute | solution.py:331
  43.6 1.0 collective-permute-start.16
  44.6 0.1 fusion.1
  44.6 1.0 collective-permute-start.14
  45.7 0.6 collective-permute-done.20.rest_12_
  46.3 0.4 collective-permute-start.13
  46.7 2.3 %collective-permute-done.18.rest_14_ = bf16[32,2048]{1,0:T(8,128)(2,1)S(1)} collective-permute-done((bf16[32,2048]{1,0:T(8,128)(2,1)}, bf16[32,2048]{1,0:T(8,128)(2,1)S(1)}, u32[]{:S(2)}, u32[]{:S(2)}) %collective-permute-start.18) | collective-permute-done | bytes 131104 | tf_op jit(solution)/shard_map/ppermute | solution.py:331
  49.0 0.5 collective-permute-start.11
  49.5 2.5 %collective-permute-done.17.rest_10_ = bf16[32,2048]{1,0:T(8,128)(2,1)S(1)} collective-permute-done((bf16[32,2048]{1,0:T(8,128)(2,1)}, bf16[32,2048]{1,0:T(8,128)(2,1)S(1)}, u32[]{:S(2)}, u32[]{:S(2)}) %collective-permute-start.17) | collective-permute-done | bytes 131104 | tf_op jit(solution)/shard_map/ppermute | solution.py:331
  52.0 1.9 %collective-permute-start.9 = (bf16[32,2048]{1,0:T(8,128)(2,1)}, bf16[32,2048]{1,0:T(8,128)(2,1)S(1)}, u32[]{:S(2)}, u32[]{:S(2)}) collective-permute-start(bf16[32,2048]{1,0:T(8,128)(2,1)} %get-tuple-element.22.rest_7_), channel_id=1, source_target_pairs={{23,0},{127,8},{39,16},{15,24},{55,32},{31,40},{71,48},{47,56},{87... | collective-permute-start | bytes 393224 | tf_op jit(solution)/shard_map/ppermute | solution.py:331
  54.0 0.3 collective-permute-start.8
  54.2 0.1 pad_bitcast_fusion.1
  54.3 1.4 %collective-permute-start.21 = (bf16[32,2048]{1,0:T(8,128)(2,1)S(1)}, bf16[32,2048]{1,0:T(8,128)(2,1)S(1)}, u32[]{:S(2)}, u32[]{:S(2)}) collective-permute-start(bf16[32,2048]{1,0:T(8,128)(2,1)S(1)} %collective-permute-done.20.rest_12_), channel_id=1, source_target_pairs={{8,0},{0,8},{24,16},{16,24},{40,32},{32,40},{56,48},{48,56},{72,64... | collective-permute-start | bytes 393224 | tf_op jit(solution)/shard_map/ppermute | solution.py:331
  55.7 0.1 collective-permute-start.19
  55.8 4.2 %collective-permute-done.11.rest_2_ = bf16[32,2048]{1,0:T(8,128)(2,1)S(1)} collective-permute-done((bf16[32,2048]{1,0:T(8,128)(2,1)}, bf16[32,2048]{1,0:T(8,128)(2,1)S(1)}, u32[]{:S(2)}, u32[]{:S(2)}) %collective-permute-start.11) | collective-permute-done | bytes 131104 | tf_op jit(solution)/shard_map/ppermute | solution.py:331
  60.0 2.5 %collective-permute-done.9.rest_4_ = bf16[32,2048]{1,0:T(8,128)(2,1)S(1)} collective-permute-done((bf16[32,2048]{1,0:T(8,128)(2,1)}, bf16[32,2048]{1,0:T(8,128)(2,1)S(1)}, u32[]{:S(2)}, u32[]{:S(2)}) %collective-permute-start.9) | collective-permute-done | bytes 131104 | tf_op jit(solution)/shard_map/ppermute | solution.py:331
  62.5 2.4 %collective-permute-done.8.rest_0_ = bf16[32,2048]{1,0:T(8,128)(2,1)S(1)} collective-permute-done((bf16[32,2048]{1,0:T(8,128)(2,1)}, bf16[32,2048]{1,0:T(8,128)(2,1)S(1)}, u32[]{:S(2)}, u32[]{:S(2)}) %collective-permute-start.8) | collective-permute-done | bytes 131104 | tf_op jit(solution)/shard_map/ppermute | solution.py:331
  64.9 0.1 pad_bitcast_fusion
  65.0 0.6 copy.33
  65.6 1.4 %copy.34.rest_15_ = bf16[128,32]{1,0:T(8,128)(2,1)} copy(bf16[128,32]{0,1:T(8,128)(2,1)} %param.21) | data formatting | bytes 16384 | tf_op args[7]
  67.0 0.4 reshape.18
  67.5 0.8 reshape.19.rest_20_
  68.5 0.5 copy-done.9
  69.2 12.8 %shard_map.138 = (f32[2,64,512]{2,1,0:T(8,128)}, f32[64,128]{1,0:T(8,128)}, f32[8,512]{1,0:T(8,128)}, f32[8,128]{1,0:T(8,128)}) custom-call(s32[2]{0:T(128)} %pad_add_fusion.place, bf16[2048,512]{1,0:T(8,128)(2,1)} %get-tuple-element.21.features, bf16[32,2048]{1,0:T(8,128)(2,1)} %copy-done.8, bf16[32,2048]{1,0:T(8,128)(2,1)} %copy-done.13, ...), custom_call_target="tpu_custom_call" | custom-call | tf_op jit(solution)/shard_map/pallas_call | solution.py:308
  81.9 1.6 %collective-permute-start.23 = (f32[64,128]{1,0:T(8,128)}, f32[64,128]{1,0:T(8,128)S(1)}, u32[]{:S(2)}, u32[]{:S(2)}) collective-permute-start(f32[64,128]{1,0:T(8,128)} %get-tuple-element.24), channel_id=1, source_target_pairs={{8,0},{16,8},{24,16},{32,24},{40,32},{48,40},{56,48},{64,56},{72,6... | collective-permute-start | bytes 98312 | tf_op jit(solution)/shard_map/ppermute | solution.py:331
  83.6 5.1 %collective-permute-start.29 = (f32[8,128]{1,0:T(8,128)}, f32[8,128]{1,0:T(8,128)S(1)}, u32[]{:S(2)}, u32[]{:S(2)}) collective-permute-start(f32[8,128]{1,0:T(8,128)} %get-tuple-element.26), channel_id=1, source_target_pairs={{9,0},{17,8},{25,16},{33,24},{41,32},{49,40},{57,48},{65,56},{73,6... | collective-permute-start | bytes 12296 | tf_op jit(solution)/shard_map/ppermute | solution.py:331
  88.7 1.6 %collective-permute-start.25 = (f32[8,512]{1,0:T(8,128)}, f32[8,512]{1,0:T(8,128)S(1)}, u32[]{:S(2)}, u32[]{:S(2)}) collective-permute-start(f32[8,512]{1,0:T(8,128)} %get-tuple-element.25), channel_id=1, source_target_pairs={{1,0},{9,8},{17,16},{25,24},{33,32},{41,40},{49,48},{57,56},{65,64... | collective-permute-start | bytes 49160 | tf_op jit(solution)/shard_map/ppermute | solution.py:331
  90.3 1.9 %collective-permute-start.24 = (f32[8,512]{1,0:T(8,128)}, f32[8,512]{1,0:T(8,128)S(1)}, u32[]{:S(2)}, u32[]{:S(2)}) collective-permute-start(f32[8,512]{1,0:T(8,128)} %get-tuple-element.25), channel_id=1, source_target_pairs={{7,0},{15,8},{23,16},{31,24},{39,32},{47,40},{55,48},{63,56},{71,6... | collective-permute-start | bytes 49160 | tf_op jit(solution)/shard_map/ppermute | solution.py:331
  92.2 1.0 collective-permute-start.28
  93.2 5.6 %collective-permute-done.28.c_bl = f32[8,128]{1,0:T(8,128)S(1)} collective-permute-done((f32[8,128]{1,0:T(8,128)}, f32[8,128]{1,0:T(8,128)S(1)}, u32[]{:S(2)}, u32[]{:S(2)}) %collective-permute-start.28) | collective-permute-done | bytes 4128 | tf_op jit(solution)/shard_map/ppermute | solution.py:331
  98.8 1.0 collective-permute-start.27
  99.7 5.9 %collective-permute-done.27.c_tr = f32[8,128]{1,0:T(8,128)S(1)} collective-permute-done((f32[8,128]{1,0:T(8,128)}, f32[8,128]{1,0:T(8,128)S(1)}, u32[]{:S(2)}, u32[]{:S(2)}) %collective-permute-start.27) | collective-permute-done | bytes 4128 | tf_op jit(solution)/shard_map/ppermute | solution.py:331
  105.6 8.7 %collective-permute-done.26.c_tl = f32[8,128]{1,0:T(8,128)S(1)} collective-permute-done((f32[8,128]{1,0:T(8,128)}, f32[8,128]{1,0:T(8,128)S(1)}, u32[]{:S(2)}, u32[]{:S(2)}) %collective-permute-start.26) | collective-permute-done | bytes 4128 | tf_op jit(solution)/shard_map/ppermute | solution.py:331
  114.4 0.5 copy-done.29
  115.0 1.8 %shard_map.139 = f32[2,64,512]{2,1,0:T(8,128)} custom-call(s32[2]{0:T(128)} %pad_add_fusion.place, f32[2,64,512]{2,1,0:T(8,128)} %get-tuple-element.23.inner, f32[64,128]{1,0:T(8,128)} %copy-done.15, f32[64,128]{1,0:T(8,128)} %copy-done.14, f32[8,512]{1,0:T(8,128)} %copy-done.21, f32[8,512]{1,0:T(8,128)} %copy-done.20, f32[8,128]{1,0:T(8,128)} %copy-done.29, ...), custom_call_target="tpu_custom_call" | custom-call | tf_op jit(solution)/shard_map/pallas_call | solution.py:308
  (96 shorter events, 0.6 us)
Async XLA Ops:
  1.8 14.1 %collective-permute-start.7 = (f32[8,128]{1,0:T(8,128)}, f32[8,128]{1,0:T(8,128)S(1)}, u32[]{:S(2)}, u32[]{:S(2)}) collective-permute-start(f32[8,128]{1,0:T(8,128)} %get-tuple-element.20), channel_id=1, source_target_pairs={{9,0},{17,8},{25,16},{33,24},{41,32},{49,40},{57,48},{65,56},{73,6... | collective-permute-start | bytes 12296 | tf_op jit(solution)/shard_map/ppermute | solution.py:331
  10.0 11.6 %collective-permute-start.6 = (f32[8,128]{1,0:T(8,128)}, f32[8,128]{1,0:T(8,128)S(1)}, u32[]{:S(2)}, u32[]{:S(2)}) collective-permute-start(f32[8,128]{1,0:T(8,128)} %get-tuple-element.20), channel_id=1, source_target_pairs={{121,0},{1,8},{9,16},{17,24},{25,32},{33,40},{41,48},{49,56},{57,6... | collective-permute-start | bytes 12296 | tf_op jit(solution)/shard_map/ppermute | solution.py:331
  10.1 11.6 %collective-permute-start.5 = (f32[8,128]{1,0:T(8,128)}, f32[8,128]{1,0:T(8,128)S(1)}, u32[]{:S(2)}, u32[]{:S(2)}) collective-permute-start(f32[8,128]{1,0:T(8,128)} %get-tuple-element.20), channel_id=1, source_target_pairs={{15,0},{23,8},{31,16},{39,24},{47,32},{55,40},{63,48},{71,56},{79,... | collective-permute-start | bytes 12296 | tf_op jit(solution)/shard_map/ppermute | solution.py:331
  15.1 12.5 %collective-permute-start.4 = (f32[8,128]{1,0:T(8,128)}, f32[8,128]{1,0:T(8,128)S(1)}, u32[]{:S(2)}, u32[]{:S(2)}) collective-permute-start(f32[8,128]{1,0:T(8,128)} %get-tuple-element.20), channel_id=1, source_target_pairs={{127,0},{7,8},{15,16},{23,24},{31,32},{39,40},{47,48},{55,56},{63,... | collective-permute-start | bytes 12296 | tf_op jit(solution)/shard_map/ppermute | solution.py:331
  15.1 12.5 %collective-permute-start.2 = (f32[8,512]{1,0:T(8,128)}, f32[8,512]{1,0:T(8,128)S(1)}, u32[]{:S(2)}, u32[]{:S(2)}) collective-permute-start(f32[8,512]{1,0:T(8,128)} %get-tuple-element.18), channel_id=1, source_target_pairs={{7,0},{15,8},{23,16},{31,24},{39,32},{47,40},{55,48},{63,56},{71,6... | collective-permute-start | bytes 49160 | tf_op jit(solution)/shard_map/ppermute | solution.py:331
  15.9 11.8 %copy-start.22 = (f32[8,128]{1,0:T(8,128)}, f32[8,128]{1,0:T(8,128)S(1)}, u32[]{:S(2)}) copy-start(f32[8,128]{1,0:T(8,128)S(1)} %collective-permute-done.7.c_br) | copy-start | bytes 12292
  15.9 11.7 %collective-permute-start.3 = (f32[8,512]{1,0:T(8,128)}, f32[8,512]{1,0:T(8,128)S(1)}, u32[]{:S(2)}, u32[]{:S(2)}) collective-permute-start(f32[8,512]{1,0:T(8,128)} %get-tuple-element.19), channel_id=1, source_target_pairs={{1,0},{9,8},{17,16},{25,24},{33,32},{41,40},{49,48},{57,56},{65,64... | collective-permute-start | bytes 49160 | tf_op jit(solution)/shard_map/ppermute | solution.py:331
  21.6 6.1 %copy-start.23 = (f32[8,128]{1,0:T(8,128)}, f32[8,128]{1,0:T(8,128)S(1)}, u32[]{:S(2)}) copy-start(f32[8,128]{1,0:T(8,128)S(1)} %collective-permute-done.6.c_bl) | copy-start | bytes 12292
  21.6 6.0 %collective-permute-start = (f32[64,128]{1,0:T(8,128)}, f32[64,128]{1,0:T(8,128)S(1)}, u32[]{:S(2)}, u32[]{:S(2)}) collective-permute-start(f32[64,128]{1,0:T(8,128)} %get-tuple-element.16), channel_id=1, source_target_pairs={{120,0},{0,8},{8,16},{16,24},{24,32},{32,40},{40,48},{48,56},{56,6... | collective-permute-start | bytes 98312 | tf_op jit(solution)/shard_map/ppermute | solution.py:331
  21.7 6.1 %copy-start.24 = (f32[8,128]{1,0:T(8,128)}, f32[8,128]{1,0:T(8,128)S(1)}, u32[]{:S(2)}) copy-start(f32[8,128]{1,0:T(8,128)S(1)} %collective-permute-done.5.c_tr) | copy-start | bytes 12292
  21.7 6.0 %collective-permute-start.1 = (f32[64,128]{1,0:T(8,128)}, f32[64,128]{1,0:T(8,128)S(1)}, u32[]{:S(2)}, u32[]{:S(2)}) collective-permute-start(f32[64,128]{1,0:T(8,128)} %get-tuple-element.17), channel_id=1, source_target_pairs={{8,0},{16,8},{24,16},{32,24},{40,32},{48,40},{56,48},{64,56},{72,6... | collective-permute-start | bytes 98312 | tf_op jit(solution)/shard_map/ppermute | solution.py:331
  39.5 6.8 %collective-permute-start.20 = (bf16[32,2048]{1,0:T(8,128)(2,1)}, bf16[32,2048]{1,0:T(8,128)(2,1)S(1)}, u32[]{:S(2)}, u32[]{:S(2)}) collective-permute-start(bf16[32,2048]{1,0:T(8,128)(2,1)} %get-tuple-element.22.rest_7_), channel_id=1, source_target_pairs={{1,0},{9,8},{17,16},{25,24},{33,32},{41,40},{49,48},{57,56},{65,64... | collective-permute-start | bytes 393224 | tf_op jit(solution)/shard_map/ppermute | solution.py:331
  41.7 7.3 %collective-permute-start.18 = (bf16[32,2048]{1,0:T(8,128)(2,1)}, bf16[32,2048]{1,0:T(8,128)(2,1)S(1)}, u32[]{:S(2)}, u32[]{:S(2)}) collective-permute-start(bf16[32,2048]{1,0:T(8,128)(2,1)} %get-tuple-element.22.rest_7_), channel_id=1, source_target_pairs={{17,0},{121,8},{33,16},{9,24},{49,32},{25,40},{65,48},{41,56},{81,... | collective-permute-start | bytes 393224 | tf_op jit(solution)/shard_map/ppermute | solution.py:331
  41.7 10.3 %collective-permute-start.17 = (bf16[32,2048]{1,0:T(8,128)(2,1)}, bf16[32,2048]{1,0:T(8,128)(2,1)S(1)}, u32[]{:S(2)}, u32[]{:S(2)}) collective-permute-start(bf16[32,2048]{1,0:T(8,128)(2,1)} %get-tuple-element.22.rest_7_), channel_id=1, source_target_pairs={{113,0},{25,8},{1,16},{41,24},{17,32},{57,40},{33,48},{73,56},{49,... | collective-permute-start | bytes 393224 | tf_op jit(solution)/shard_map/ppermute | solution.py:331
  43.6 10.4 %collective-permute-start.16 = (bf16[32,2048]{1,0:T(8,128)(2,1)}, bf16[32,2048]{1,0:T(8,128)(2,1)S(1)}, u32[]{:S(2)}, u32[]{:S(2)}) collective-permute-start(bf16[32,2048]{1,0:T(8,128)(2,1)} %get-tuple-element.22.rest_7_), channel_id=1, source_target_pairs={{8,0},{0,8},{24,16},{16,24},{40,32},{32,40},{56,48},{48,56},{72,64... | collective-permute-start | bytes 393224 | tf_op jit(solution)/shard_map/ppermute | solution.py:331
  44.6 9.7 %collective-permute-start.14 = (bf16[32,2048]{1,0:T(8,128)(2,1)}, bf16[32,2048]{1,0:T(8,128)(2,1)S(1)}, u32[]{:S(2)}, u32[]{:S(2)}) collective-permute-start(bf16[32,2048]{1,0:T(8,128)(2,1)} %get-tuple-element.22.rest_7_), channel_id=1, source_target_pairs={{16,0},{120,8},{32,16},{8,24},{48,32},{24,40},{64,48},{40,56},{80,... | collective-permute-start | bytes 393224 | tf_op jit(solution)/shard_map/ppermute | solution.py:331
  46.3 22.1 %copy-start = (bf16[32,2048]{1,0:T(8,128)(2,1)}, bf16[32,2048]{1,0:T(8,128)(2,1)S(1)}, u32[]{:S(2)}) copy-start(bf16[32,2048]{1,0:T(8,128)(2,1)S(1)} %collective-permute-done.20.rest_12_) | copy-start | bytes 393220
  46.3 9.4 %collective-permute-start.13 = (bf16[32,2048]{1,0:T(8,128)(2,1)}, bf16[32,2048]{1,0:T(8,128)(2,1)S(1)}, u32[]{:S(2)}, u32[]{:S(2)}) collective-permute-start(bf16[32,2048]{1,0:T(8,128)(2,1)} %get-tuple-element.22.rest_7_), channel_id=1, source_target_pairs={{112,0},{24,8},{0,16},{40,24},{16,32},{56,40},{32,48},{72,56},{48,... | collective-permute-start | bytes 393224 | tf_op jit(solution)/shard_map/ppermute | solution.py:331
  49.0 19.4 %copy-start.1 = (bf16[32,2048]{1,0:T(8,128)(2,1)}, bf16[32,2048]{1,0:T(8,128)(2,1)S(1)}, u32[]{:S(2)}) copy-start(bf16[32,2048]{1,0:T(8,128)(2,1)S(1)} %collective-permute-done.18.rest_14_) | copy-start | bytes 393220
  49.0 11.0 %collective-permute-start.11 = (bf16[32,2048]{1,0:T(8,128)(2,1)}, bf16[32,2048]{1,0:T(8,128)(2,1)S(1)}, u32[]{:S(2)}, u32[]{:S(2)}) collective-permute-start(bf16[32,2048]{1,0:T(8,128)(2,1)} %get-tuple-element.22.rest_7_), channel_id=1, source_target_pairs={{7,0},{15,8},{23,16},{31,24},{39,32},{47,40},{55,48},{63,56},{71,6... | collective-permute-start | bytes 393224 | tf_op jit(solution)/shard_map/ppermute | solution.py:331
  52.0 16.4 %copy-start.2 = (bf16[32,2048]{1,0:T(8,128)(2,1)}, bf16[32,2048]{1,0:T(8,128)(2,1)S(1)}, u32[]{:S(2)}) copy-start(bf16[32,2048]{1,0:T(8,128)(2,1)S(1)} %collective-permute-done.17.rest_10_) | copy-start | bytes 393220
  52.0 10.5 %collective-permute-start.9 = (bf16[32,2048]{1,0:T(8,128)(2,1)}, bf16[32,2048]{1,0:T(8,128)(2,1)S(1)}, u32[]{:S(2)}, u32[]{:S(2)}) collective-permute-start(bf16[32,2048]{1,0:T(8,128)(2,1)} %get-tuple-element.22.rest_7_), channel_id=1, source_target_pairs={{23,0},{127,8},{39,16},{15,24},{55,32},{31,40},{71,48},{47,56},{87... | collective-permute-start | bytes 393224 | tf_op jit(solution)/shard_map/ppermute | solution.py:331
  54.0 14.5 %copy-start.3 = (bf16[32,2048]{1,0:T(8,128)(2,1)}, bf16[32,2048]{1,0:T(8,128)(2,1)S(1)}, u32[]{:S(2)}) copy-start(bf16[32,2048]{1,0:T(8,128)(2,1)S(1)} %collective-permute-done.16.rest_8_) | copy-start | bytes 393220
  54.0 10.9 %collective-permute-start.8 = (bf16[32,2048]{1,0:T(8,128)(2,1)}, bf16[32,2048]{1,0:T(8,128)(2,1)S(1)}, u32[]{:S(2)}, u32[]{:S(2)}) collective-permute-start(bf16[32,2048]{1,0:T(8,128)(2,1)} %get-tuple-element.22.rest_7_), channel_id=1, source_target_pairs={{119,0},{31,8},{7,16},{47,24},{23,32},{63,40},{39,48},{79,56},{55,... | collective-permute-start | bytes 393224 | tf_op jit(solution)/shard_map/ppermute | solution.py:331
  54.3 14.1 %copy-start.4 = (bf16[32,2048]{1,0:T(8,128)(2,1)}, bf16[32,2048]{1,0:T(8,128)(2,1)S(1)}, u32[]{:S(2)}) copy-start(bf16[32,2048]{1,0:T(8,128)(2,1)S(1)} %collective-permute-done.14.rest_9_) | copy-start | bytes 393220
  54.3 14.0 %collective-permute-start.21 = (bf16[32,2048]{1,0:T(8,128)(2,1)S(1)}, bf16[32,2048]{1,0:T(8,128)(2,1)S(1)}, u32[]{:S(2)}, u32[]{:S(2)}) collective-permute-start(bf16[32,2048]{1,0:T(8,128)(2,1)S(1)} %collective-permute-done.20.rest_12_), channel_id=1, source_target_pairs={{8,0},{0,8},{24,16},{16,24},{40,32},{32,40},{56,48},{48,56},{72,64... | collective-permute-start | bytes 393224 | tf_op jit(solution)/shard_map/ppermute | solution.py:331
  55.7 12.8 %copy-start.5 = (bf16[32,2048]{1,0:T(8,128)(2,1)}, bf16[32,2048]{1,0:T(8,128)(2,1)S(1)}, u32[]{:S(2)}) copy-start(bf16[32,2048]{1,0:T(8,128)(2,1)S(1)} %collective-permute-done.13.rest_5_) | copy-start | bytes 393220
  55.7 12.6 %collective-permute-start.19 = (bf16[32,2048]{1,0:T(8,128)(2,1)S(1)}, bf16[32,2048]{1,0:T(8,128)(2,1)S(1)}, u32[]{:S(2)}, u32[]{:S(2)}) collective-permute-start(bf16[32,2048]{1,0:T(8,128)(2,1)S(1)} %collective-permute-done.18.rest_14_), channel_id=1, source_target_pairs={{8,0},{0,8},{24,16},{16,24},{40,32},{32,40},{56,48},{48,56},{72,64... | collective-permute-start | bytes 393224 | tf_op jit(solution)/shard_map/ppermute | solution.py:331
  60.0 8.5 %copy-start.6 = (bf16[32,2048]{1,0:T(8,128)(2,1)}, bf16[32,2048]{1,0:T(8,128)(2,1)S(1)}, u32[]{:S(2)}) copy-start(bf16[32,2048]{1,0:T(8,128)(2,1)S(1)} %collective-permute-done.11.rest_2_) | copy-start | bytes 393220
  60.0 8.4 %collective-permute-start.15 = (bf16[32,2048]{1,0:T(8,128)(2,1)S(1)}, bf16[32,2048]{1,0:T(8,128)(2,1)S(1)}, u32[]{:S(2)}, u32[]{:S(2)}) collective-permute-start(bf16[32,2048]{1,0:T(8,128)(2,1)S(1)} %collective-permute-done.14.rest_9_), channel_id=1, source_target_pairs={{8,0},{0,8},{24,16},{16,24},{40,32},{32,40},{56,48},{48,56},{72,64... | collective-permute-start | bytes 393224 | tf_op jit(solution)/shard_map/ppermute | solution.py:331
  62.5 6.0 %copy-start.7 = (bf16[32,2048]{1,0:T(8,128)(2,1)}, bf16[32,2048]{1,0:T(8,128)(2,1)S(1)}, u32[]{:S(2)}) copy-start(bf16[32,2048]{1,0:T(8,128)(2,1)S(1)} %collective-permute-done.9.rest_4_) | copy-start | bytes 393220
  62.5 5.9 %collective-permute-start.12 = (bf16[32,2048]{1,0:T(8,128)(2,1)S(1)}, bf16[32,2048]{1,0:T(8,128)(2,1)S(1)}, u32[]{:S(2)}, u32[]{:S(2)}) collective-permute-start(bf16[32,2048]{1,0:T(8,128)(2,1)S(1)} %collective-permute-done.11.rest_2_), channel_id=1, source_target_pairs={{8,0},{0,8},{24,16},{16,24},{40,32},{32,40},{56,48},{48,56},{72,64... | collective-permute-start | bytes 393224 | tf_op jit(solution)/shard_map/ppermute | solution.py:331
  64.9 3.6 %copy-start.8 = (bf16[32,2048]{1,0:T(8,128)(2,1)}, bf16[32,2048]{1,0:T(8,128)(2,1)S(1)}, u32[]{:S(2)}) copy-start(bf16[32,2048]{1,0:T(8,128)(2,1)S(1)} %collective-permute-done.8.rest_0_) | copy-start | bytes 393220
  64.9 3.5 %collective-permute-start.10 = (bf16[32,2048]{1,0:T(8,128)(2,1)S(1)}, bf16[32,2048]{1,0:T(8,128)(2,1)S(1)}, u32[]{:S(2)}, u32[]{:S(2)}) collective-permute-start(bf16[32,2048]{1,0:T(8,128)(2,1)S(1)} %collective-permute-done.9.rest_4_), channel_id=1, source_target_pairs={{8,0},{0,8},{24,16},{16,24},{40,32},{32,40},{56,48},{48,56},{72,64... | collective-permute-start | bytes 393224 | tf_op jit(solution)/shard_map/ppermute | solution.py:331
  68.3 0.7 copy-start.11
  68.4 0.7 copy-start.12
  68.4 0.8 copy-start.13
  81.9 32.4 %collective-permute-start.23 = (f32[64,128]{1,0:T(8,128)}, f32[64,128]{1,0:T(8,128)S(1)}, u32[]{:S(2)}, u32[]{:S(2)}) collective-permute-start(f32[64,128]{1,0:T(8,128)} %get-tuple-element.24), channel_id=1, source_target_pairs={{8,0},{16,8},{24,16},{32,24},{40,32},{48,40},{56,48},{64,56},{72,6... | collective-permute-start | bytes 98312 | tf_op jit(solution)/shard_map/ppermute | solution.py:331
  83.6 30.8 %collective-permute-start.22 = (f32[64,128]{1,0:T(8,128)}, f32[64,128]{1,0:T(8,128)S(1)}, u32[]{:S(2)}, u32[]{:S(2)}) collective-permute-start(f32[64,128]{1,0:T(8,128)} %get-tuple-element.24), channel_id=1, source_target_pairs={{120,0},{0,8},{8,16},{16,24},{24,32},{32,40},{40,48},{48,56},{56,6... | collective-permute-start | bytes 98312 | tf_op jit(solution)/shard_map/ppermute | solution.py:331
  83.6 8.6 %collective-permute-start.29 = (f32[8,128]{1,0:T(8,128)}, f32[8,128]{1,0:T(8,128)S(1)}, u32[]{:S(2)}, u32[]{:S(2)}) collective-permute-start(f32[8,128]{1,0:T(8,128)} %get-tuple-element.26), channel_id=1, source_target_pairs={{9,0},{17,8},{25,16},{33,24},{41,32},{49,40},{57,48},{65,56},{73,6... | collective-permute-start | bytes 12296 | tf_op jit(solution)/shard_map/ppermute | solution.py:331
  88.7 25.6 %collective-permute-start.25 = (f32[8,512]{1,0:T(8,128)}, f32[8,512]{1,0:T(8,128)S(1)}, u32[]{:S(2)}, u32[]{:S(2)}) collective-permute-start(f32[8,512]{1,0:T(8,128)} %get-tuple-element.25), channel_id=1, source_target_pairs={{1,0},{9,8},{17,16},{25,24},{33,32},{41,40},{49,48},{57,56},{65,64... | collective-permute-start | bytes 49160 | tf_op jit(solution)/shard_map/ppermute | solution.py:331
  90.3 24.1 %collective-permute-start.24 = (f32[8,512]{1,0:T(8,128)}, f32[8,512]{1,0:T(8,128)S(1)}, u32[]{:S(2)}, u32[]{:S(2)}) collective-permute-start(f32[8,512]{1,0:T(8,128)} %get-tuple-element.25), channel_id=1, source_target_pairs={{7,0},{15,8},{23,16},{31,24},{39,32},{47,40},{55,48},{63,56},{71,6... | collective-permute-start | bytes 49160 | tf_op jit(solution)/shard_map/ppermute | solution.py:331
  92.2 22.2 %copy-start.26 = (f32[8,128]{1,0:T(8,128)}, f32[8,128]{1,0:T(8,128)S(1)}, u32[]{:S(2)}) copy-start(f32[8,128]{1,0:T(8,128)S(1)} %collective-permute-done.29.c_br) | copy-start | bytes 12292
  92.2 6.6 %collective-permute-start.28 = (f32[8,128]{1,0:T(8,128)}, f32[8,128]{1,0:T(8,128)S(1)}, u32[]{:S(2)}, u32[]{:S(2)}) collective-permute-start(f32[8,128]{1,0:T(8,128)} %get-tuple-element.26), channel_id=1, source_target_pairs={{121,0},{1,8},{9,16},{17,24},{25,32},{33,40},{41,48},{49,56},{57,6... | collective-permute-start | bytes 12296 | tf_op jit(solution)/shard_map/ppermute | solution.py:331
  98.8 15.6 %copy-start.27 = (f32[8,128]{1,0:T(8,128)}, f32[8,128]{1,0:T(8,128)S(1)}, u32[]{:S(2)}) copy-start(f32[8,128]{1,0:T(8,128)S(1)} %collective-permute-done.28.c_bl) | copy-start | bytes 12292
  98.8 6.9 %collective-permute-start.27 = (f32[8,128]{1,0:T(8,128)}, f32[8,128]{1,0:T(8,128)S(1)}, u32[]{:S(2)}, u32[]{:S(2)}) collective-permute-start(f32[8,128]{1,0:T(8,128)} %get-tuple-element.26), channel_id=1, source_target_pairs={{15,0},{23,8},{31,16},{39,24},{47,32},{55,40},{63,48},{71,56},{79,... | collective-permute-start | bytes 12296 | tf_op jit(solution)/shard_map/ppermute | solution.py:331
  105.6 8.8 %copy-start.28 = (f32[8,128]{1,0:T(8,128)}, f32[8,128]{1,0:T(8,128)S(1)}, u32[]{:S(2)}) copy-start(f32[8,128]{1,0:T(8,128)S(1)} %collective-permute-done.27.c_tr) | copy-start | bytes 12292
  105.6 8.7 %collective-permute-start.26 = (f32[8,128]{1,0:T(8,128)}, f32[8,128]{1,0:T(8,128)S(1)}, u32[]{:S(2)}, u32[]{:S(2)}) collective-permute-start(f32[8,128]{1,0:T(8,128)} %get-tuple-element.26), channel_id=1, source_target_pairs={{127,0},{7,8},{15,16},{23,24},{31,32},{39,40},{47,48},{55,56},{63,... | collective-permute-start | bytes 12296 | tf_op jit(solution)/shard_map/ppermute | solution.py:331
  (12 other events, 7.4 us)

commit v2 on v1

v2 whole, which is shorter than its diff:
```python
import functools

import jax
import jax.numpy as jnp
from jax import lax
from jax.experimental import pallas as pl
from jax.experimental.pallas import tpu as pltpu
from jax.sharding import PartitionSpec as P

ROWS, COLS = 64, 512
CH, WIDE, KINDS = 32, 128, 8
POOL_ROWS, POOL_COLS = 16, 128
SPOTS = POOL_ROWS * POOL_COLS
HALF = ROWS // 2
VMEM = pl.BlockSpec(memory_space=pltpu.VMEM)
SMEM = pl.BlockSpec(memory_space=pltpu.SMEM)
F32, BF16 = jnp.float32, jnp.bfloat16


def iota(shape, dim):
    return lax.broadcasted_iota(jnp.int32, shape, dim)


def shape_of(*dims, dtype=F32):
    return jax.ShapeDtypeStruct(dims, dtype)


def mm(a, b):
    return jnp.dot(a, b, preferred_element_type=F32)


def split(x):
    high = x.astype(BF16)
    return high, (x - high.astype(F32)).astype(BF16)


def column(row):
    count = row.shape[1]
    eye = iota((count, count), 0) == iota((count, count), 1)
    return jnp.sum(jnp.where(eye, row, 0.0), axis=1, keepdims=True)


def flags(place, last_cross, last_band):
    one = lambda truth: truth.astype(F32)
    return (
        one(place[0] > 0), one(place[0] < last_cross), one(place[1] > 0), one(place[1] < last_band)
    )


def pool_weights():
    x, q = iota((COLS, POOL_COLS), 0), iota((COLS, POOL_COLS), 1)
    inner = (x // 4 == q) & (x > 0) & (x < COLS - 1)
    return jnp.where(inner, 1.0 / 16, 0.0).astype(BF16)


def halo_kernel(rasters, aerial, rows, cols, message):
    ones, none = jnp.ones((1, COLS), F32), jnp.zeros((2, COLS), F32)
    for at, y in enumerate((0, 1, ROWS - 2, ROWS - 1)):
        parts = [rasters[kind, y : y + 1, :].astype(F32) for kind in range(4)]
        rows[at * 8 : (at + 1) * 8, :] = jnp.concatenate(parts + [aerial[y : y + 1, :], ones, none], axis=0)
    lane = iota((ROWS, 128), 1)
    packed = jnp.where((lane < 32) & (lane % 8 == 5), 1.0, 0.0)
    for at, x in enumerate((0, 1, COLS - 2, COLS - 1)):
        first = x // 128 * 128
        for kind in range(5):
            if kind < 4:
                slab = rasters[kind, :, first : first + 128].astype(F32)
            else:
                slab = aerial[:, first : first + 128]
            packed = jnp.where(lane == at * 8 + kind, slab[:, x - first : x - first + 1], packed)
    turned = jnp.transpose(jnp.concatenate([packed, jnp.zeros((128 - ROWS, 128), F32)], axis=0))
    cols[...] = turned[:32]
    message[...] = jnp.concatenate([turned[:8], turned[24:32]], axis=0)


def sides(place, partner, outer, low, high):
    even = place[1] % 2 == 0
    left = jnp.where(even, outer[high], partner[high])
    right = jnp.where(even, partner[low], outer[low])
    return left, right


def row_message_kernel(cells, place, rows, partner, outer, even_message, odd_message):
    _, _, has_left, has_right = flags(place, *cells)
    left, right = sides(place, partner, outer, slice(0, 8), slice(8, 16))
    left, right = left * has_left, right * has_right
    lane = iota((8, 128), 1)

    def row(at, y):
        side = jnp.where(lane == 0, right[:, y : y + 1], jnp.where(lane == 1, left[:, y : y + 1], 0.0))
        return jnp.concatenate([rows[at * 8 : (at + 1) * 8, :], side], axis=1)

    low, high = row(0, 0), row(3, ROWS - 1)
    even = place[0] % 2 == 0
    even_message[...] = jnp.where(even, high, low)
    odd_message[...] = jnp.where(even, low, high)


def inner_kernel(half, rasters, aerial, kinds_w, conv_w, conv_b, features, sums, stem_w, wide_w, stem3):
    spread = jnp.where(iota((KINDS, 64), 1) // 8 == iota((KINDS, 64), 0), 1.0, 0.0).astype(BF16)
    same = iota((256, 64), 0) // CH == iota((256, 64), 1) % 8
    halves = []
    for part in split(kinds_w[...]):
        rows = mm(jnp.concatenate([part] * 8, axis=0), spread)
        halves.append(jnp.where(same, rows, 0.0))
    stem_w[...] = jnp.concatenate(halves, axis=1).astype(BF16)
    wide_w[...] = jnp.zeros(wide_w.shape, BF16)
    taps = conv_w[...]
    for y in range(8):
        wide_w[y * CH : (y + 1) * CH, y * 96 : y * 96 + 288] = taps
    pool_w = pool_weights()
    bias = jnp.broadcast_to(column(conv_b[...]), (CH, COLS))
    bias = jnp.concatenate([bias] * 8, axis=0)

    blocks = range(5) if half == 0 else range(3, 8)
    base = half * HALF - 1
    edge = 0 if half == 0 else HALF + 1
    stem3[edge * 96 : (edge + 1) * 96, :] = jnp.zeros((96, COLS), BF16)
    for block in blocks:
        y = block * 8
        values = jnp.concatenate([rasters[k, y : y + 8, :] for k in range(4)], axis=0).astype(F32)
        high, low = split(aerial[y : y + 8, :])
        tail = jnp.concatenate([jnp.ones((8, COLS), BF16), jnp.zeros((8, COLS), BF16)], axis=0)
        x = jnp.concatenate([values.astype(BF16), high, low, tail], axis=0)
        out = jnp.maximum(mm(stem_w[...], jnp.concatenate([x, x], axis=0)), 0.0)
        for r in range(8):
            at = y + r - base
            if at < 0 or at > HALF + 1:
                continue
            s = out[r * CH : (r + 1) * CH, :]
            parts = [pltpu.roll(s, 1, 1), s, pltpu.roll(s, COLS - 1, 1)]
            stem3[at * 96 : (at + 1) * 96, :] = jnp.concatenate(parts, axis=0).astype(BF16)

    for block in range(HALF // 8):
        out = mm(wide_w[...], stem3[block * 768 : block * 768 + 960, :])
        value = jnp.maximum(out + bias, 0.0).astype(BF16)
        features[block * 256 : (block + 1) * 256, :] = value
        means = mm(value, pool_w)
        for p in range(2):
            rows = [means[p * 128 + r * 32 : p * 128 + (r + 1) * 32, :] for r in range(4)]
            if half == 0 and block == 0 and p == 0:
                rows = rows[1:]
            if half == 1 and block == HALF // 8 - 1 and p == 1:
                rows = rows[:3]
            at = (block * 2 + p) * POOL_COLS
            sums[:, at : at + POOL_COLS] = sum(rows[1:], rows[0])


def rim_kernel(
    cells, place, rows, cols, partner, outer, even_message, odd_message, sums_low, sums_high,
    kinds_w, conv_w, conv_b, rim_rows, rim_cols, pooled,
):
    has_above, has_below, has_left, has_right = flags(place, *cells)
    left, right = sides(place, partner, outer, slice(0, 8), slice(8, 16))
    left, right = left * has_left, right * has_right
    even = place[0] % 2 == 0
    above = jnp.where(even, odd_message[...], even_message[...]) * has_above
    below = jnp.where(even, even_message[...], odd_message[...]) * has_below
    kind_high, kind_low = split(kinds_w[...])
    stem_w = jnp.concatenate([kind_high, kind_high, kind_low], axis=1)
    bias = column(conv_b[...])

    def stem(x):
        high, low = split(x)
        high = high.astype(F32)
        stacked = jnp.concatenate([high, low.astype(F32), high], axis=0).astype(BF16)
        return jnp.maximum(mm(stem_w, stacked), 0.0)

    def conv(stacked):
        return jnp.maximum(mm(conv_w[...], stacked) + bias, 0.0).astype(BF16)

    def row(at):
        return rows[at * 8 : (at + 1) * 8, :]

    pool_w = pool_weights()
    row_sums = []
    trios = [(above[:, :COLS], row(0), row(1)), (row(2), row(3), below[:, :COLS])]
    for at, trio in enumerate(trios):
        stacked = []
        for x in trio:
            s = stem(x)
            stacked += [pltpu.roll(s, 1, 1), s, pltpu.roll(s, COLS - 1, 1)]
        value = conv(jnp.concatenate(stacked, axis=0).astype(BF16))
        rim_rows[at * CH : (at + 1) * CH, :] = value
        row_sums.append(mm(value, pool_w))

    lane = iota((8, 128), 1)

    def line(inside, top, bottom, x):
        top, bottom = top[:, x : x + 1], bottom[:, x : x + 1]
        return jnp.where(lane < ROWS, inside, jnp.where(lane == ROWS, bottom, 0.0)), top

    x_of = {-1: COLS + 1, COLS: COLS}
    lines = {-1: left, COLS: right}
    for at, x in enumerate((0, 1, COLS - 2, COLS - 1)):
        lines[x] = cols[at * 8 : (at + 1) * 8, :]
    columns = []
    for dx in (-1, 0, 1):
        low, low_top = line(lines[dx], above, below, x_of.get(dx, dx))
        x = COLS - 1 + dx
        high, high_top = line(lines[x], above, below, x_of.get(x, x))
        low = jnp.where(lane == 127, high_top, low)
        high = jnp.where(lane == 127, low_top, high)
        columns.append(stem(jnp.concatenate([low, high], axis=1)))
    s = jnp.concatenate(columns, axis=0)
    stacked = [pltpu.roll(s, 1, 1), s, pltpu.roll(s, 255, 1)]
    value = conv(jnp.concatenate(stacked, axis=0).astype(BF16))
    rim_cols[...] = value
    y, at = iota((256, SPOTS), 0), iota((256, SPOTS), 1)
    p, q = at // POOL_COLS, at % POOL_COLS
    picked = ((y // 4 == p) & (q == 0)) | (((y - 128) // 4 == p) & (y >= 128) & (q == POOL_COLS - 1))
    col_sums = mm(value, jnp.where(picked, 1.0 / 16, 0.0).astype(BF16))
    for p in range(POOL_ROWS):
        at = p * POOL_COLS
        near = sums_low if p < POOL_ROWS // 2 else sums_high
        first = at % (SPOTS // 2)
        total = near[:, first : first + POOL_COLS] + col_sums[:, at : at + POOL_COLS]
        if p == 0:
            total += row_sums[0]
        if p == POOL_ROWS - 1:
            total += row_sums[1]
        pooled[:, at : at + POOL_COLS] = total.astype(BF16)


def merge_kernel(low, high, rim_rows, rim_cols, features):
    lane = iota((CH, 128), 1)
    columns = rim_cols[...].astype(F32)
    for y in range(ROWS):
        if y == 0:
            f = rim_rows[0:CH, :]
        elif y == ROWS - 1:
            f = rim_rows[CH : 2 * CH, :]
        else:
            source = low if y < HALF else high
            at = y % HALF * CH
            f = source[at : at + CH, :]
        f = f.astype(F32)
        first = jnp.where(lane == 0, columns[:, y : y + 1], f[:, :128])
        last = jnp.where(lane == 127, columns[:, 128 + y : 129 + y], f[:, COLS - 128 :])
        f = jnp.concatenate([first, f[:, 128 : COLS - 128], last], axis=1)
        features[y * CH : (y + 1) * CH, :] = f.astype(BF16)


MAPS = {
    (0, -2): ("band", 0), (0, -1): ("band", 1), (0, 0): ("own", 0), (0, 1): ("own", 1), (0, 2): ("band_p", 1),
    (-1, -2): ("one", 0), (-1, -1): ("one", 1), (-1, 0): ("relay_p", 0), (-1, 1): ("relay_p", 1), (-1, 2): ("two_p", 1),
    (1, -2): ("two", 0), (1, -1): ("two", 1), (1, 0): ("relay", 1), (1, 1): ("relay", 0), (1, 2): ("one_p", 1),
}
NAMES = ("own", "band", "band_p", "one", "one_p", "two", "two_p", "relay", "relay_p")


def logits_kernel(
    cells, place, features, own, band_m, band_p, one_m, one_p, two_m, two_p, relay, relay_p,
    proj_w, proj_b, ctx_w, up_w, up_b, head_w, rim_w, head_b,
    logits, col_out, row_out, weights, proj, low_up, lifted, decoded,
):
    arrays = dict(zip(NAMES, (own, band_m, band_p, one_m, one_p, two_m, two_p, relay, relay_p)))
    last_cross, last_band = cells
    cross, band = place[0], place[1]
    core = band % 2
    sign = 1 - 2 * core
    maps = []

    for at in range(15):
        u, v = at // 5 - 1, at % 5 - 2
        maps.append(MAPS[(u, v)])
        row, col = cross + u * sign, band + v * sign
        inside = (row >= 0) & (row <= last_cross) & (col >= 0) & (col <= last_band)
        one = ctx_w[:, at * WIDE : (at + 1) * WIDE]
        two = ctx_w[:, (14 - at) * WIDE : (15 - at) * WIDE]
        chosen = jnp.where(core == 0, one, two)
        weights[:, at * WIDE : (at + 1) * WIDE] = jnp.where(inside, chosen, jnp.zeros_like(chosen))

    p_bias = jnp.broadcast_to(column(proj_b[...]), (WIDE, 256))
    u_bias = jnp.broadcast_to(column(up_b[...]), (CH, 256))

    def context_part(part, carry):
        at = pl.multiple_of(part * 256, 256)
        for k in range(15):
            name, half = maps[k]
            out = mm(proj_w[...], arrays[name][half, :, pl.ds(at, 256)])
            proj[k * WIDE : (k + 1) * WIDE, :] = jnp.maximum(out + p_bias, 0.0).astype(BF16)
        context = mm(weights[...], proj[...]) + proj[7 * WIDE : 8 * WIDE, :].astype(F32)
        mixed = jnp.maximum(context, 0.0).astype(BF16)
        up = mm(up_w[...], mixed) + u_bias
        high = up.astype(BF16)
        low = (up - high.astype(F32)).astype(BF16)
        both = [
            jnp.concatenate([high[:, h * 128 : (h + 1) * 128], low[:, h * 128 : (h + 1) * 128]], axis=1)
            for h in range(2)
        ]
        low_up[pl.ds(pl.multiple_of(part * 64, 64), 64), :] = jnp.concatenate(both, axis=0)
        return carry

    lax.fori_loop(0, SPOTS // 256, context_part, 0)

    widen = jnp.where(
        iota((256, COLS), 0) % 128 == iota((256, COLS), 1) // 4, 1.0, 0.0
    ).astype(BF16)
    lifted[...] = mm(low_up[...], widen)

    decoded[0:64, :] = jnp.zeros((64, COLS), BF16)
    decoded[66 * CH :, :] = jnp.zeros((64, COLS), BF16)

    def decode(p, carry):
        up = lifted[pl.ds(pl.multiple_of(p * CH, CH), CH), :]
        for r in range(4):
            at = pl.multiple_of((4 * p + r) * CH, CH)
            value = jnp.maximum(features[pl.ds(at, CH), :].astype(F32) + up, 0.0).astype(BF16)
            decoded[pl.ds(pl.multiple_of(at + 64, CH), CH), :] = value
        return carry

    lax.fori_loop(0, POOL_ROWS, decode, 0)

    def gather_taps(z, count):
        total = None
        for dx in range(5):
            part = z[dx * count : (dx + 1) * count, :]
            part = jnp.concatenate([part, jnp.zeros((count, 128), F32)], axis=1)
            if dx != 2:
                part = pltpu.roll(part, (dx - 2) % 640, 1)
            total = part if total is None else total + part
        return total

    lane16 = iota((16, 128), 1)
    first_lanes = (lane16 < 2) | (lane16 >= 126)

    def head(block, carry):
        first = pl.multiple_of(block * 16 * CH, 16 * CH)
        total = gather_taps(mm(head_w[...], decoded[pl.ds(first, 20 * CH), :]), 32)
        y = pl.multiple_of(block * 16, 16)
        for k in range(2):
            logits[k, pl.ds(y, 16), :] = total[k * 16 : (k + 1) * 16, :COLS] + head_b[k]
        rim = total[:, COLS:]
        col_out[pl.ds(y, 16), :] = jnp.where(first_lanes, rim[:16], pltpu.roll(rim[16:], 4, 1))
        return carry

    lax.fori_loop(0, ROWS // 16, head, 0)

    ends = jnp.concatenate([decoded[64:128, :], decoded[64 * CH : 66 * CH, :]], axis=0)
    total = gather_taps(mm(rim_w[...], ends), 8)
    row_out[...] = total[:, :COLS]
    col_out[ROWS : ROWS + 8, :] = total[:, COLS:]


def row_sum_kernel(cells, place, row_out, partner, outer, out):
    _, _, has_left, has_right = flags(place, *cells)
    corners = slice(ROWS, ROWS + 8)
    left, right = sides(place, partner, outer, corners, corners)
    lane = iota((8, 128), 1)
    out[...] = row_out[...] + jnp.concatenate(
        [
            jnp.where(lane < 2, left * has_left, 0.0),
            jnp.zeros((8, COLS - 256), F32),
            jnp.where(lane >= 126, right * has_right, 0.0),
        ],
        axis=1,
    )


def sum_kernel(cells, place, inner, partner, outer, even_message, odd_message, out):
    has_above, has_below, has_left, has_right = flags(place, *cells)
    even = place[0] % 2 == 0
    above = jnp.where(even, odd_message[...], even_message[...]) * has_above
    below = jnp.where(even, even_message[...], odd_message[...]) * has_below
    left, right = sides(place, partner, outer, slice(0, ROWS), slice(0, ROWS))
    left, right = left * has_left, right * has_right
    out[...] = inner[...]
    lane = iota((ROWS, 128), 1)
    for k in range(2):
        low = left if k == 0 else pltpu.roll(left, 124, 1)
        out[k, :, 0:128] += jnp.where(lane < 2, low, 0.0)
        high = right if k == 0 else pltpu.roll(right, 124, 1)
        out[k, :, COLS - 128 : COLS] += jnp.where(lane >= 126, high, 0.0)
        out[k, 0:2, :] += above[4 * k + 2 : 4 * k + 4]
        out[k, ROWS - 2 : ROWS, :] += below[4 * k : 4 * k + 2]


def call(kernel, outs, args, scratch=(), smem=(0,), flops=0):
    return pl.pallas_call(
        kernel,
        out_shape=outs,
        in_specs=[SMEM if at in smem else VMEM for at in range(len(args))],
        out_specs=jax.tree.map(lambda _: VMEM, outs),
        scratch_shapes=list(scratch),
        compiler_params=pltpu.CompilerParams(vmem_limit_bytes=56 * 1024 * 1024),
        cost_estimate=pl.CostEstimate(flops=flops, bytes_accessed=1 << 20, transcendentals=0),
    )(*args)


def body(
    n_cross, n_band, rasters, aerial, w_in, aerial_gain, b_in, w_conv1, b_conv1, w_proj, b_proj,
    w_ctx, w_up, b_up, w_head, b_head,
):
    cells = (n_cross - 1, n_band - 1)
    place = jnp.stack([lax.axis_index("cross"), lax.axis_index("band")]).astype(jnp.int32)

    def moved(x, source):
        route = []
        for cross in range(n_cross):
            for band in range(n_band):
                c, b = source(cross, band)
                route.append(((b % n_band) * n_cross + c % n_cross, band * n_cross + cross))
        return lax.ppermute(x, ("band", "cross"), route)

    def partner(x):
        return moved(x, lambda c, b: (c, b ^ 1))

    def outer(x):
        return moved(x, lambda c, b: (c, ((b + 1) ^ 1) - 1))

    def even_pair(x):
        return moved(x, lambda c, b: (c ^ 1, b))

    def odd_pair(x):
        return moved(x, lambda c, b: (((c + 1) ^ 1) - 1, b))

    def beside(x, u):
        return moved(x, lambda c, b: (c + u * (1 - 2 * (b % 2)), b - 2 + 4 * (b % 2)))

    rows, cols, message = call(
        halo_kernel,
        [shape_of(32, COLS), shape_of(32, 128), shape_of(16, 128)],
        [rasters, aerial],
        smem=(),
    )
    near, far = partner(message), outer(message)

    gain = aerial_gain[:, None]
    kinds_8 = jnp.concatenate([w_in, gain, gain, b_in[:, None], jnp.zeros_like(gain)], axis=1)
    kinds_5 = jnp.concatenate([w_in, gain, b_in[:, None], jnp.zeros((CH, 2), F32)], axis=1)
    conv_b = b_conv1[None, :]

    def inner(half):
        return call(
            functools.partial(inner_kernel, half),
            [shape_of(HALF * CH, COLS, dtype=BF16), shape_of(CH, SPOTS // 2)],
            [rasters, aerial, kinds_8, w_conv1, conv_b],
            [
                pltpu.VMEM((256, 128), BF16),
                pltpu.VMEM((256, 960), BF16),
                pltpu.VMEM(((HALF + 2) * 96, COLS), BF16),
            ],
            smem=(),
            flops=4 * 10**9,
        )

    feat_low, sums_low = inner(0)
    even_out, odd_out = call(
        functools.partial(row_message_kernel, cells), [shape_of(8, COLS + 128)] * 2, [place, rows, near, far]
    )
    even_in, odd_in = even_pair(even_out), odd_pair(odd_out)
    feat_high, sums_high = inner(1)

    taps = w_head.reshape(2, 5, 5, CH)[:, ::-1].transpose(2, 0, 1, 3).reshape(10, 5 * CH)
    skewed = jnp.broadcast_to(jnp.pad(taps, ((0, 0), (0, 16 * CH)))[:, None, :], (10, 16, 21 * CH))
    head_w = skewed.reshape(10, 16 * 21 * CH)[:, : 16 * 20 * CH].reshape(160, 20 * CH)
    gap = jnp.zeros((10, CH), BF16)
    at = [taps[:, (4 - d) * CH : (5 - d) * CH] for d in range(5)]
    ends = [[at[0], gap, gap, gap], [at[1], at[0], gap, gap], [gap, gap, at[4], at[3]], [gap, gap, gap, at[4]]]
    rim_w = jnp.stack([jnp.concatenate(r, axis=1) for r in ends], axis=1).reshape(40, 4 * CH)
    head_w, rim_w, rows = lax.optimization_barrier((head_w, rim_w, rows))

    rim_rows, rim_cols, pooled = call(
        functools.partial(rim_kernel, cells),
        [shape_of(2 * CH, COLS, dtype=BF16), shape_of(CH, 256, dtype=BF16), shape_of(CH, SPOTS, dtype=BF16)],
        [place, rows, cols, near, far, even_in, odd_in, sums_low, sums_high, kinds_5, w_conv1, conv_b],
    )

    own = jnp.stack([pooled, partner(pooled)])
    one = beside(own, -1)
    band = beside(own, 0)
    two = beside(own, 1)
    relay = outer(one)
    maps = [own, band, partner(band), one, partner(one), two, partner(two), relay, partner(relay)]

    features = call(
        merge_kernel, shape_of(ROWS * CH, COLS, dtype=BF16), [feat_low, feat_high, rim_rows, rim_cols], smem=(),
        flops=10**9,
    )
    inner_logits, col_out, row_out = call(
        functools.partial(logits_kernel, cells),
        [shape_of(2, ROWS, COLS), shape_of(ROWS + 8, 128), shape_of(8, COLS)],
        [place, features, *maps, w_proj, b_proj[None, :], w_ctx, w_up, b_up[None, :], head_w, rim_w, b_head],
        [
            pltpu.VMEM((WIDE, 15 * WIDE), BF16),
            pltpu.VMEM((15 * WIDE, 256), BF16),
            pltpu.VMEM((POOL_ROWS * CH, 256), BF16),
            pltpu.VMEM((POOL_ROWS * CH, COLS), F32),
            pltpu.VMEM(((ROWS + 4) * CH, COLS), BF16),
        ],
        smem=(0, 18),
    )
    near, far = partner(col_out), outer(col_out)
    row_out = call(
        functools.partial(row_sum_kernel, cells), shape_of(8, COLS), [place, row_out, near, far]
    )
    return call(
        functools.partial(sum_kernel, cells),
        shape_of(2, ROWS, COLS),
        [place, inner_logits, near, far, even_pair(row_out), odd_pair(row_out)],
    )


def solution(mesh):
    sizes = dict(mesh.shape)
    return jax.shard_map(
        functools.partial(body, sizes["cross"], sizes["band"]),
        mesh=mesh,
        in_specs=(P(None, "cross", "band"), P("cross", "band")) + (P(),) * 12,
        out_specs=P(None, "cross", "band"),
        check_vma=False,
    )
```

time: 117 us -> 95 us (0.81)
  starting transfers between devices: 45.7 us -> 19.6 us
  Pallas kernels: 27.6 us -> 35.1 us
  waiting for transfers between devices: 34.7 us -> 28.7 us
  local copies, waits for them, and re-layouts: 7.76 us -> 9.29 us
    ppermute x30 -> x17, starting transfers between devices: 45.7 us -> 19.6 us  [moved(): return lax.ppermute(x, ('band', 'cross'), route)]
    pallas_call x4 -> x9, Pallas kernels: 27.6 us -> 35.1 us  [call(): pl.pallas_call(kernel, out_shape=outs, in_specs=[SMEM if at in smem else...]
    ppermute x30 -> x17, waiting for transfers between devices: 34.7 us -> 28.7 us  [moved(): return lax.ppermute(x, ('band', 'cross'), route)]
    unnamed x61 -> x43, local copies, waits for them, and re-layouts: 3.33 us -> 4.09 us
  transfers between devices with their start and end apart: 30 -> 17, of which waited for: 9 -> 7; matrix products, arithmetic and copies ran while one was open for 6% -> 7% of each run, Pallas kernels for 0% -> 13%
where the time goes in v2:
time: 95 us; the launch traced here: 94.6 us
  Pallas kernels  35.1 us (37%)
  waiting for transfers between devices  28.7 us (30%)
  starting transfers between devices  19.6 us (21%)
  local copies, waits for them, and re-layouts  9.29 us (10%)
  other arithmetic  1.67 us (2%)
    pallas_call x9, Pallas kernels, call(): pl.pallas_call(kernel, out_shape=outs, in_specs=[SMEM if at in smem else...  35.1 us
    ppermute x17, waiting for transfers between devices, moved(): return lax.ppermute(x, ('band', 'cross'), route)  28.7 us
    ppermute x17, starting transfers between devices, moved(): return lax.ppermute(x, ('band', 'cross'), route)  19.6 us
    unnamed x43, local copies, waits for them, and re-layouts  4.09 us
  transfers between devices with their start and end apart: 17, of which 7 were waited for; matrix products, arithmetic and copies ran while one was open for 7% of the time, Pallas kernels for 13%

profile of v2, /device:TPU:0, one launch (start us, length us, event | category | flops | bytes accessed | tf_op | source)
XLA Modules:
  0.0 94.6 jit_solution(6560911309054621706)
XLA Ops:
  0.0 2.0 %shard_map.138 = (f32[32,512]{1,0:T(8,128)}, f32[32,128]{1,0:T(8,128)}, f32[16,128]{1,0:T(8,128)}) custom-call(s32[4,64,512]{2,1,0:T(8,128)} %rasters.5, f32[64,512]{1,0:T(8,128)} %aerial.5), custom_call_target="tpu_custom_call" | custom-call | bytes 1048576 | tf_op jit(solution)/shard_map/pallas_call | solution.py:380
  2.0 3.5 %collective-permute-start.1 = (f32[16,128]{1,0:T(8,128)}, f32[16,128]{1,0:T(8,128)S(1)}, u32[]{:S(2)}, u32[]{:S(2)}) collective-permute-start(f32[16,128]{1,0:T(8,128)} %get-tuple-element.28), channel_id=1, source_target_pairs={{120,0},{16,8},{8,16},{32,24},{24,32},{48,40},{40,48},{64,56},{56,... | collective-permute-start | bytes 24584 | tf_op jit(solution)/shard_map/ppermute | solution.py:404
  5.4 0.8 reshape.16
  6.2 0.1 reshape.17
  6.3 0.1 fusion.1
  6.4 0.8 concatenate.20
  7.2 0.7 copy.37.kinds_w
  7.8 4.5 %shard_map.137 = (bf16[1024,512]{1,0:T(8,128)(2,1)}, f32[32,1024]{1,0:T(8,128)}) custom-call(s32[4,64,512]{2,1,0:T(8,128)} %rasters.5, f32[64,512]{1,0:T(8,128)} %aerial.5, f32[32,8]{1,0:T(8,128)} %copy.37.kinds_w, bf16[32,288]{1,0:T(8,128)(2,1)} %conv_w.5, f32[1,32]{1,0:T(1,128)} %bitcast.28), custom_call_target="tpu_custom_call" | custom-call | flops 4000000000 | bytes 1048576 | tf_op jit(solution)/shard_map/pallas_call | solution.py:380
  12.3 4.5 %shard_map.136 = (bf16[1024,512]{1,0:T(8,128)(2,1)}, f32[32,1024]{1,0:T(8,128)}) custom-call(s32[4,64,512]{2,1,0:T(8,128)} %rasters.5, f32[64,512]{1,0:T(8,128)} %aerial.5, f32[32,8]{1,0:T(8,128)} %copy.37.kinds_w, bf16[32,288]{1,0:T(8,128)(2,1)} %conv_w.5, f32[1,32]{1,0:T(1,128)} %bitcast.29), custom_call_target="tpu_custom_call" | custom-call | flops 4000000000 | bytes 1048576 | tf_op jit(solution)/shard_map/pallas_call | solution.py:380
  16.8 0.1 pad.14.clone
  17.0 0.1 pad_bitcast_fusion.1
  17.0 0.1 pad_bitcast_fusion
  17.1 0.7 pad_add_fusion.place
  17.8 0.6 copy-done.11
  18.4 1.6 %shard_map.139 = (f32[8,640]{1,0:T(8,128)}, f32[8,640]{1,0:T(8,128)}) custom-call(s32[2]{0:T(128)} %pad_add_fusion.place, f32[32,512]{1,0:T(8,128)} %get-tuple-element.26.rows, f32[16,128]{1,0:T(8,128)} %copy-done.12, f32[16,128]{1,0:T(8,128)} %copy-done.11), custom_call_target="tpu_custom_call" | custom-call | bytes 1048576 | tf_op jit(solution)/shard_map/pallas_call | solution.py:380
  20.0 2.7 %collective-permute-start.2 = (f32[8,640]{1,0:T(8,128)}, f32[8,640]{1,0:T(8,128)S(1)}, u32[]{:S(2)}, u32[]{:S(2)}) collective-permute-start(f32[8,640]{1,0:T(8,128)} %get-tuple-element.29), channel_id=1, source_target_pairs={{1,0},{9,8},{17,16},{25,24},{33,32},{41,40},{49,48},{57,56},{65,64... | collective-permute-start | bytes 61448 | tf_op jit(solution)/shard_map/ppermute | solution.py:404
  22.7 4.3 %collective-permute-start.3 = (f32[8,640]{1,0:T(8,128)}, f32[8,640]{1,0:T(8,128)S(1)}, u32[]{:S(2)}, u32[]{:S(2)}) collective-permute-start(f32[8,640]{1,0:T(8,128)} %get-tuple-element.30), channel_id=1, source_target_pairs={{7,0},{15,8},{23,16},{31,24},{39,32},{47,40},{55,48},{63,56},{71,6... | collective-permute-start | bytes 61448 | tf_op jit(solution)/shard_map/ppermute | solution.py:404
  27.0 0.7 copy.41.kinds_w
  27.7 0.6 copy.40
  28.3 0.4 reshape.18
  28.8 0.8 reshape.19.head_w
  29.6 0.7 collective-permute-done.3.odd_message
  30.3 0.6 copy-done.14
  30.9 3.2 %shard_map.140 = (bf16[64,512]{1,0:T(8,128)(2,1)}, bf16[32,256]{1,0:T(8,128)(2,1)}, bf16[32,2048]{1,0:T(8,128)(2,1)}) custom-call(s32[2]{0:T(128)} %pad_add_fusion.place, f32[32,512]{1,0:T(8,128)} %get-tuple-element.26.rows, f32[32,128]{1,0:T(8,128)} %get-tuple-element.27.cols, f32[16,128]{1,0:T(8,128)} %copy-done.12, f32[16,128]{1,0:T(8,128)} %copy-done.11, ...), custom_call_target="tpu_custom_call" | custom-call | bytes 1048576 | tf_op jit(solution)/shard_map/pallas_call | solution.py:380
  34.1 1.6 %collective-permute-done.4 = bf16[32,2048]{1,0:T(8,128)(2,1)S(1)} collective-permute-done((bf16[32,2048]{1,0:T(8,128)(2,1)}, bf16[32,2048]{1,0:T(8,128)(2,1)S(1)}, u32[]{:S(2)}, u32[]{:S(2)}) %collective-permute-start.4) | collective-permute-done | bytes 131104 | tf_op jit(solution)/shard_map/ppermute | solution.py:404
  35.7 0.9 pad_maximum_fusion.own
  36.6 0.1 collective-permute-start.7
  36.7 4.6 %collective-permute-start.9 = (bf16[2,32,2048]{2,1,0:T(8,128)(2,1)S(1)}, bf16[2,32,2048]{2,1,0:T(8,128)(2,1)S(1)}, u32[]{:S(2)}, u32[]{:S(2)}) collective-permute-start(bf16[2,32,2048]{2,1,0:T(8,128)(2,1)S(1)} %pad_maximum_fusion.own), channel_id=1, source_target_pairs={{113,0},{31,8},{1,16},{47,24},{17,32},{63,40},{33,48},{79,56},{49,... | collective-permute-start | bytes 786440 | tf_op jit(solution)/shard_map/ppermute | solution.py:404
  41.3 9.8 %collective-permute-done.7.one_m = bf16[2,32,2048]{2,1,0:T(8,128)(2,1)S(1)} collective-permute-done((bf16[2,32,2048]{2,1,0:T(8,128)(2,1)S(1)}, bf16[2,32,2048]{2,1,0:T(8,128)(2,1)S(1)}, u32[]{:S(2)}, u32[]{:S(2)}) %collective-permute-start.7) | collective-permute-done | bytes 262176 | tf_op jit(solution)/shard_map/ppermute | solution.py:404
  51.1 2.7 %collective-permute-done.9.two_m = bf16[2,32,2048]{2,1,0:T(8,128)(2,1)S(1)} collective-permute-done((bf16[2,32,2048]{2,1,0:T(8,128)(2,1)S(1)}, bf16[2,32,2048]{2,1,0:T(8,128)(2,1)S(1)}, u32[]{:S(2)}, u32[]{:S(2)}) %collective-permute-start.9) | collective-permute-done | bytes 262176 | tf_op jit(solution)/shard_map/ppermute | solution.py:404
  53.9 0.5 collective-permute-start.6
  54.4 4.6 %collective-permute-done.11.relay = bf16[2,32,2048]{2,1,0:T(8,128)(2,1)S(1)} collective-permute-done((bf16[2,32,2048]{2,1,0:T(8,128)(2,1)S(1)}, bf16[2,32,2048]{2,1,0:T(8,128)(2,1)S(1)}, u32[]{:S(2)}, u32[]{:S(2)}) %collective-permute-start.11) | collective-permute-done | bytes 262176 | tf_op jit(solution)/shard_map/ppermute | solution.py:404
  59.0 0.7 copy.42.proj_w
  59.7 3.3 %shard_map.141.features = bf16[2048,512]{1,0:T(8,128)(2,1)} custom-call(bf16[1024,512]{1,0:T(8,128)(2,1)} %get-tuple-element.23.low, bf16[1024,512]{1,0:T(8,128)(2,1)} %get-tuple-element.24.high, bf16[64,512]{1,0:T(8,128)(2,1)} %get-tuple-element.33.rim_rows, bf16[32,256]{1,0:T(8,128)(2,1)} %get-tuple-element.34.rim_cols), custom_call_target="tpu_custom_call" | custom-call | flops 1000000000 | bytes 1048576 | tf_op jit(solution)/shard_map/pallas_call | solution.py:380
  63.2 0.6 copy-done.6
  63.8 0.1 copy-done.5
  63.9 0.1 copy-done.7
  64.0 0.1 copy-done.8
  64.1 12.8 %shard_map.142 = (f32[2,64,512]{2,1,0:T(8,128)}, f32[72,128]{1,0:T(8,128)}, f32[8,512]{1,0:T(8,128)}) custom-call(s32[2]{0:T(128)} %pad_add_fusion.place, bf16[2048,512]{1,0:T(8,128)(2,1)} %shard_map.141.features, bf16[2,32,2048]{2,1,0:T(8,128)(2,1)} %copy-done, bf16[2,32,2048]{2,1,0:T(8,128)(2,1)} %copy-done.3, bf16[2,32,2048]{2,1,0:T(8,128)(2,1)} %copy-done.7, ...), custom_call_target="tpu_custom_call" | custom-call | bytes 1048576 | tf_op jit(solution)/shard_map/pallas_call | solution.py:380
  76.9 0.6 collective-permute-start.13
  77.5 5.1 %collective-permute-done.14.outer = f32[72,128]{1,0:T(8,128)S(1)} collective-permute-done((f32[72,128]{1,0:T(8,128)}, f32[72,128]{1,0:T(8,128)S(1)}, u32[]{:S(2)}, u32[]{:S(2)}) %collective-permute-start.14) | collective-permute-done | bytes 36896 | tf_op jit(solution)/shard_map/ppermute | solution.py:404
  82.6 0.6 copy-done.9
  83.2 1.4 %shard_map.143 = f32[8,512]{1,0:T(8,128)} custom-call(s32[2]{0:T(128)} %pad_add_fusion.place, f32[8,512]{1,0:T(8,128)} %get-tuple-element.40.row_out, f32[72,128]{1,0:T(8,128)} %copy-done.10, f32[72,128]{1,0:T(8,128)} %copy-done.9), custom_call_target="tpu_custom_call" | custom-call | bytes 1048576 | tf_op jit(solution)/shard_map/pallas_call | solution.py:380
  84.6 1.6 %collective-permute-start.16 = (f32[8,512]{1,0:T(8,128)}, f32[8,512]{1,0:T(8,128)S(1)}, u32[]{:S(2)}, u32[]{:S(2)}) collective-permute-start(f32[8,512]{1,0:T(8,128)} %shard_map.143), channel_id=1, source_target_pairs={{7,0},{15,8},{23,16},{31,24},{39,32},{47,40},{55,48},{63,56},{71,6... | collective-permute-start | bytes 49160 | tf_op jit(solution)/shard_map/ppermute | solution.py:404
  86.2 1.8 %collective-permute-start.15 = (f32[8,512]{1,0:T(8,128)}, f32[8,512]{1,0:T(8,128)S(1)}, u32[]{:S(2)}, u32[]{:S(2)}) collective-permute-start(f32[8,512]{1,0:T(8,128)} %shard_map.143), channel_id=1, source_target_pairs={{1,0},{9,8},{17,16},{25,24},{33,32},{41,40},{49,48},{57,56},{65,64... | collective-permute-start | bytes 49160 | tf_op jit(solution)/shard_map/ppermute | solution.py:404
  88.0 4.2 %collective-permute-done.16.odd_message = f32[8,512]{1,0:T(8,128)S(1)} collective-permute-done((f32[8,512]{1,0:T(8,128)}, f32[8,512]{1,0:T(8,128)S(1)}, u32[]{:S(2)}, u32[]{:S(2)}) %collective-permute-start.16) | collective-permute-done | bytes 16416 | tf_op jit(solution)/shard_map/ppermute | solution.py:404
  92.2 0.6 copy-done.15
  92.8 1.8 %shard_map.144 = f32[2,64,512]{2,1,0:T(8,128)} custom-call(s32[2]{0:T(128)} %pad_add_fusion.place, f32[2,64,512]{2,1,0:T(8,128)} %get-tuple-element.38.inner, f32[72,128]{1,0:T(8,128)} %copy-done.10, f32[72,128]{1,0:T(8,128)} %copy-done.9, f32[8,512]{1,0:T(8,128)} %copy-done.16, f32[8,512]{1,0:T(8,128)} %copy-done.15), custom_call_target="tpu_custom_call" | custom-call | bytes 1048576 | tf_op jit(solution)/shard_map/pallas_call | solution.py:380
  (62 shorter events, 0.3 us)
Async XLA Ops:
  2.0 15.8 %collective-permute-start.1 = (f32[16,128]{1,0:T(8,128)}, f32[16,128]{1,0:T(8,128)S(1)}, u32[]{:S(2)}, u32[]{:S(2)}) collective-permute-start(f32[16,128]{1,0:T(8,128)} %get-tuple-element.28), channel_id=1, source_target_pairs={{120,0},{16,8},{8,16},{32,24},{24,32},{48,40},{40,48},{64,56},{56,... | collective-permute-start | bytes 24584 | tf_op jit(solution)/shard_map/ppermute | solution.py:404
  5.4 12.4 %collective-permute-start = (f32[16,128]{1,0:T(8,128)}, f32[16,128]{1,0:T(8,128)S(1)}, u32[]{:S(2)}, u32[]{:S(2)}) collective-permute-start(f32[16,128]{1,0:T(8,128)} %get-tuple-element.28), channel_id=1, source_target_pairs={{8,0},{0,8},{24,16},{16,24},{40,32},{32,40},{56,48},{48,56},{72,64... | collective-permute-start | bytes 24584 | tf_op jit(solution)/shard_map/ppermute | solution.py:404
  12.3 4.6 %copy-start.18 = (f32[32,4]{0,1:T(4,128)S(1)}, f32[32,4]{0,1:T(4,128)}, u32[]{:S(2)}) copy-start(f32[32,4]{0,1:T(4,128)} %param.16) | copy-start | bytes 1540
  12.3 4.6 %copy-start.19 = (f32[32]{0:T(128)S(1)}, f32[32]{0:T(128)}, u32[]{:S(2)}) copy-start(f32[32]{0:T(128)} %param.17) | copy-start | bytes 388
  12.3 4.6 %copy-start.20 = (f32[32]{0:T(128)S(1)}, f32[32]{0:T(128)}, u32[]{:S(2)}) copy-start(f32[32]{0:T(128)} %param.18) | copy-start | bytes 388
  16.8 42.2 %copy-start.17 = (bf16[128,32]{0,1:T(8,128)(2,1)S(1)}, bf16[128,32]{0,1:T(8,128)(2,1)}, u32[]{:S(2)}) copy-start(bf16[128,32]{0,1:T(8,128)(2,1)} %param.21) | copy-start | bytes 24580
  17.8 0.6 copy-start.11
  17.8 0.6 copy-start.12
  20.0 9.6 %collective-permute-start.2 = (f32[8,640]{1,0:T(8,128)}, f32[8,640]{1,0:T(8,128)S(1)}, u32[]{:S(2)}, u32[]{:S(2)}) collective-permute-start(f32[8,640]{1,0:T(8,128)} %get-tuple-element.29), channel_id=1, source_target_pairs={{1,0},{9,8},{17,16},{25,24},{33,32},{41,40},{49,48},{57,56},{65,64... | collective-permute-start | bytes 61448 | tf_op jit(solution)/shard_map/ppermute | solution.py:404
  22.7 7.6 %collective-permute-start.3 = (f32[8,640]{1,0:T(8,128)}, f32[8,640]{1,0:T(8,128)S(1)}, u32[]{:S(2)}, u32[]{:S(2)}) collective-permute-start(f32[8,640]{1,0:T(8,128)} %get-tuple-element.30), channel_id=1, source_target_pairs={{7,0},{15,8},{23,16},{31,24},{39,32},{47,40},{55,48},{63,56},{71,6... | collective-permute-start | bytes 61448 | tf_op jit(solution)/shard_map/ppermute | solution.py:404
  29.6 0.7 copy-start.13
  30.3 0.6 copy-start.14
  34.1 1.6 %collective-permute-start.4 = (bf16[32,2048]{1,0:T(8,128)(2,1)}, bf16[32,2048]{1,0:T(8,128)(2,1)S(1)}, u32[]{:S(2)}, u32[]{:S(2)}) collective-permute-start(bf16[32,2048]{1,0:T(8,128)(2,1)} %get-tuple-element.35), channel_id=1, source_target_pairs={{8,0},{0,8},{24,16},{16,24},{40,32},{32,40},{56,48},{48,56},{72,64... | collective-permute-start | bytes 393224 | tf_op jit(solution)/shard_map/ppermute | solution.py:404
  36.6 26.4 %copy-start = (bf16[2,32,2048]{2,1,0:T(8,128)(2,1)}, bf16[2,32,2048]{2,1,0:T(8,128)(2,1)S(1)}, u32[]{:S(2)}) copy-start(bf16[2,32,2048]{2,1,0:T(8,128)(2,1)S(1)} %pad_maximum_fusion.own) | copy-start | bytes 786436
  36.6 14.5 %collective-permute-start.7 = (bf16[2,32,2048]{2,1,0:T(8,128)(2,1)S(1)}, bf16[2,32,2048]{2,1,0:T(8,128)(2,1)S(1)}, u32[]{:S(2)}, u32[]{:S(2)}) collective-permute-start(bf16[2,32,2048]{2,1,0:T(8,128)(2,1)S(1)} %pad_maximum_fusion.own), channel_id=1, source_target_pairs={{119,0},{25,8},{7,16},{41,24},{23,32},{57,40},{39,48},{73,56},{55,... | collective-permute-start | bytes 786440 | tf_op jit(solution)/shard_map/ppermute | solution.py:404
  36.7 17.1 %collective-permute-start.9 = (bf16[2,32,2048]{2,1,0:T(8,128)(2,1)S(1)}, bf16[2,32,2048]{2,1,0:T(8,128)(2,1)S(1)}, u32[]{:S(2)}, u32[]{:S(2)}) collective-permute-start(bf16[2,32,2048]{2,1,0:T(8,128)(2,1)S(1)} %pad_maximum_fusion.own), channel_id=1, source_target_pairs={{113,0},{31,8},{1,16},{47,24},{17,32},{63,40},{33,48},{79,56},{49,... | collective-permute-start | bytes 786440 | tf_op jit(solution)/shard_map/ppermute | solution.py:404
  41.3 12.6 %collective-permute-start.5 = (bf16[2,32,2048]{2,1,0:T(8,128)(2,1)S(1)}, bf16[2,32,2048]{2,1,0:T(8,128)(2,1)S(1)}, u32[]{:S(2)}, u32[]{:S(2)}) collective-permute-start(bf16[2,32,2048]{2,1,0:T(8,128)(2,1)S(1)} %pad_maximum_fusion.own), channel_id=1, source_target_pairs={{112,0},{24,8},{0,16},{40,24},{16,32},{56,40},{32,48},{72,56},{48,... | collective-permute-start | bytes 786440 | tf_op jit(solution)/shard_map/ppermute | solution.py:404
  51.1 12.0 %copy-start.1 = (bf16[2,32,2048]{2,1,0:T(8,128)(2,1)}, bf16[2,32,2048]{2,1,0:T(8,128)(2,1)S(1)}, u32[]{:S(2)}) copy-start(bf16[2,32,2048]{2,1,0:T(8,128)(2,1)S(1)} %collective-permute-done.7.one_m) | copy-start | bytes 786436
  51.1 7.9 %collective-permute-start.11 = (bf16[2,32,2048]{2,1,0:T(8,128)(2,1)S(1)}, bf16[2,32,2048]{2,1,0:T(8,128)(2,1)S(1)}, u32[]{:S(2)}, u32[]{:S(2)}) collective-permute-start(bf16[2,32,2048]{2,1,0:T(8,128)(2,1)S(1)} %collective-permute-done.7.one_m), channel_id=1, source_target_pairs={{120,0},{16,8},{8,16},{32,24},{24,32},{48,40},{40,48},{64,56},{56,... | collective-permute-start | bytes 786440 | tf_op jit(solution)/shard_map/ppermute | solution.py:404
  51.1 12.0 %collective-permute-start.8 = (bf16[2,32,2048]{2,1,0:T(8,128)(2,1)S(1)}, bf16[2,32,2048]{2,1,0:T(8,128)(2,1)S(1)}, u32[]{:S(2)}, u32[]{:S(2)}) collective-permute-start(bf16[2,32,2048]{2,1,0:T(8,128)(2,1)S(1)} %collective-permute-done.7.one_m), channel_id=1, source_target_pairs={{8,0},{0,8},{24,16},{16,24},{40,32},{32,40},{56,48},{48,56},{72,64... | collective-permute-start | bytes 786440 | tf_op jit(solution)/shard_map/ppermute | solution.py:404
  53.8 9.2 %copy-start.2 = (bf16[2,32,2048]{2,1,0:T(8,128)(2,1)}, bf16[2,32,2048]{2,1,0:T(8,128)(2,1)S(1)}, u32[]{:S(2)}) copy-start(bf16[2,32,2048]{2,1,0:T(8,128)(2,1)S(1)} %collective-permute-done.9.two_m) | copy-start | bytes 786436
  53.8 9.3 %collective-permute-start.10 = (bf16[2,32,2048]{2,1,0:T(8,128)(2,1)S(1)}, bf16[2,32,2048]{2,1,0:T(8,128)(2,1)S(1)}, u32[]{:S(2)}, u32[]{:S(2)}) collective-permute-start(bf16[2,32,2048]{2,1,0:T(8,128)(2,1)S(1)} %collective-permute-done.9.two_m), channel_id=1, source_target_pairs={{8,0},{0,8},{24,16},{16,24},{40,32},{32,40},{56,48},{48,56},{72,64... | collective-permute-start | bytes 786440 | tf_op jit(solution)/shard_map/ppermute | solution.py:404
  53.9 9.2 %copy-start.3 = (bf16[2,32,2048]{2,1,0:T(8,128)(2,1)}, bf16[2,32,2048]{2,1,0:T(8,128)(2,1)S(1)}, u32[]{:S(2)}) copy-start(bf16[2,32,2048]{2,1,0:T(8,128)(2,1)S(1)} %collective-permute-done.5.band_m) | copy-start | bytes 786436
  53.9 9.3 %collective-permute-start.6 = (bf16[2,32,2048]{2,1,0:T(8,128)(2,1)S(1)}, bf16[2,32,2048]{2,1,0:T(8,128)(2,1)S(1)}, u32[]{:S(2)}, u32[]{:S(2)}) collective-permute-start(bf16[2,32,2048]{2,1,0:T(8,128)(2,1)S(1)} %collective-permute-done.5.band_m), channel_id=1, source_target_pairs={{8,0},{0,8},{24,16},{16,24},{40,32},{32,40},{56,48},{48,56},{72,64... | collective-permute-start | bytes 786440 | tf_op jit(solution)/shard_map/ppermute | solution.py:404
  59.0 4.1 %copy-start.4 = (bf16[2,32,2048]{2,1,0:T(8,128)(2,1)}, bf16[2,32,2048]{2,1,0:T(8,128)(2,1)S(1)}, u32[]{:S(2)}) copy-start(bf16[2,32,2048]{2,1,0:T(8,128)(2,1)S(1)} %collective-permute-done.11.relay) | copy-start | bytes 786436
  59.0 4.2 %collective-permute-start.12 = (bf16[2,32,2048]{2,1,0:T(8,128)(2,1)S(1)}, bf16[2,32,2048]{2,1,0:T(8,128)(2,1)S(1)}, u32[]{:S(2)}, u32[]{:S(2)}) collective-permute-start(bf16[2,32,2048]{2,1,0:T(8,128)(2,1)S(1)} %collective-permute-done.11.relay), channel_id=1, source_target_pairs={{8,0},{0,8},{24,16},{16,24},{40,32},{32,40},{56,48},{48,56},{72,64... | collective-permute-start | bytes 786440 | tf_op jit(solution)/shard_map/ppermute | solution.py:404
  63.1 0.7 copy-start.6
  63.1 0.8 copy-start.5
  63.1 0.9 copy-start.7
  63.2 0.9 copy-start.8
  76.9 5.7 %collective-permute-start.14 = (f32[72,128]{1,0:T(8,128)}, f32[72,128]{1,0:T(8,128)S(1)}, u32[]{:S(2)}, u32[]{:S(2)}) collective-permute-start(f32[72,128]{1,0:T(8,128)} %get-tuple-element.39), channel_id=1, source_target_pairs={{120,0},{16,8},{8,16},{32,24},{24,32},{48,40},{40,48},{64,56},{56,... | collective-permute-start | bytes 110600 | tf_op jit(solution)/shard_map/ppermute | solution.py:404
  76.9 5.7 %collective-permute-start.13 = (f32[72,128]{1,0:T(8,128)}, f32[72,128]{1,0:T(8,128)S(1)}, u32[]{:S(2)}, u32[]{:S(2)}) collective-permute-start(f32[72,128]{1,0:T(8,128)} %get-tuple-element.39), channel_id=1, source_target_pairs={{8,0},{0,8},{24,16},{16,24},{40,32},{32,40},{56,48},{48,56},{72,64... | collective-permute-start | bytes 110600 | tf_op jit(solution)/shard_map/ppermute | solution.py:404
  82.6 0.6 copy-start.9
  82.6 0.6 copy-start.10
  84.6 7.6 %collective-permute-start.16 = (f32[8,512]{1,0:T(8,128)}, f32[8,512]{1,0:T(8,128)S(1)}, u32[]{:S(2)}, u32[]{:S(2)}) collective-permute-start(f32[8,512]{1,0:T(8,128)} %shard_map.143), channel_id=1, source_target_pairs={{7,0},{15,8},{23,16},{31,24},{39,32},{47,40},{55,48},{63,56},{71,6... | collective-permute-start | bytes 49160 | tf_op jit(solution)/shard_map/ppermute | solution.py:404
  86.2 6.0 %collective-permute-start.15 = (f32[8,512]{1,0:T(8,128)}, f32[8,512]{1,0:T(8,128)S(1)}, u32[]{:S(2)}, u32[]{:S(2)}) collective-permute-start(f32[8,512]{1,0:T(8,128)} %shard_map.143), channel_id=1, source_target_pairs={{1,0},{9,8},{17,16},{25,24},{33,32},{41,40},{49,48},{57,56},{65,64... | collective-permute-start | bytes 49160 | tf_op jit(solution)/shard_map/ppermute | solution.py:404
  92.2 0.6 copy-start.15
  92.2 0.6 copy-start.16

commit v3 on v2

--- a/solution.py
+++ b/solution.py
@@ -12,6 +12,7 @@
 POOL_ROWS, POOL_COLS = 16, 128
 SPOTS = POOL_ROWS * POOL_COLS
 HALF = ROWS // 2
+HBM = pl.BlockSpec(memory_space=pltpu.HBM)
 VMEM = pl.BlockSpec(memory_space=pltpu.VMEM)
 SMEM = pl.BlockSpec(memory_space=pltpu.SMEM)
 F32, BF16 = jnp.float32, jnp.bfloat16
@@ -40,11 +41,24 @@
     return jnp.sum(jnp.where(eye, row, 0.0), axis=1, keepdims=True)
 
 
-def flags(place, last_cross, last_band):
+def placed():
+    return lax.axis_index("cross"), lax.axis_index("band")
+
+
+def flags(last_cross, last_band):
+    cross, band = placed()
     one = lambda truth: truth.astype(F32)
-    return (
-        one(place[0] > 0), one(place[0] < last_cross), one(place[1] > 0), one(place[1] < last_band)
-    )
+    return one(cross > 0), one(cross < last_cross), one(band > 0), one(band < last_band)
+
+
+def kinds_of(w_in, gain, b_in, gains):
+    lane = iota((CH, KINDS), 1)
+    kinds = jnp.zeros((CH, KINDS), F32)
+    parts = [w_in[k : k + 1, :] for k in range(4)] + [gain[...]] * gains + [b_in[...]]
+    parts = [column(part) for part in parts]
+    for kind, part in enumerate(parts):
+        kinds = jnp.where(lane == kind, part, kinds)
+    return kinds
 
 
 def pool_weights():
@@ -53,7 +67,7 @@
     return jnp.where(inner, 1.0 / 16, 0.0).astype(BF16)
 
 
-def halo_kernel(rasters, aerial, rows, cols, message):
+def halo_kernel(rasters, aerial, rows, cols, message, stem_in):
     ones, none = jnp.ones((1, COLS), F32), jnp.zeros((2, COLS), F32)
     for at, y in enumerate((0, 1, ROWS - 2, ROWS - 1)):
         parts = [rasters[kind, y : y + 1, :].astype(F32) for kind in range(4)]
@@ -71,36 +85,42 @@
     turned = jnp.transpose(jnp.concatenate([packed, jnp.zeros((128 - ROWS, 128), F32)], axis=0))
     cols[...] = turned[:32]
     message[...] = jnp.concatenate([turned[:8], turned[24:32]], axis=0)
-
-
-def sides(place, partner, outer, low, high):
-    even = place[1] % 2 == 0
+    for y in range(0, ROWS, 8):
+        values = jnp.concatenate([rasters[k, y : y + 8, :] for k in range(4)], axis=0).astype(F32)
+        high, low = split(aerial[y : y + 8, :])
+        tail = jnp.concatenate([jnp.ones((8, COLS), BF16), jnp.zeros((8, COLS), BF16)], axis=0)
+        stem_in[y * 8 : y * 8 + 64, :] = jnp.concatenate([values.astype(BF16), high, low, tail], axis=0)
+
+
+def sides(partner, outer, low, high):
+    even = placed()[1] % 2 == 0
     left = jnp.where(even, outer[high], partner[high])
     right = jnp.where(even, partner[low], outer[low])
     return left, right
 
 
-def row_message_kernel(cells, place, rows, partner, outer, even_message, odd_message):
-    _, _, has_left, has_right = flags(place, *cells)
-    left, right = sides(place, partner, outer, slice(0, 8), slice(8, 16))
-    left, right = left * has_left, right * has_right
-    lane = iota((8, 128), 1)
+def row_messages(cells, rows, partner, outer):
+    _, _, has_left, has_right = flags(*cells)
+    left, right = sides(partner, outer, slice(0, 8), slice(8, 16))
+    lane = lax.broadcasted_iota(jnp.int32, (8, 128), 1)
 
     def row(at, y):
-        side = jnp.where(lane == 0, right[:, y : y + 1], jnp.where(lane == 1, left[:, y : y + 1], 0.0))
+        low, high = left[:, y : y + 1] * has_left, right[:, y : y + 1] * has_right
+        side = jnp.where(lane == 0, high, jnp.where(lane == 1, low, 0.0))
         return jnp.concatenate([rows[at * 8 : (at + 1) * 8, :], side], axis=1)
 
     low, high = row(0, 0), row(3, ROWS - 1)
-    even = place[0] % 2 == 0
-    even_message[...] = jnp.where(even, high, low)
-    odd_message[...] = jnp.where(even, low, high)
-
-
-def inner_kernel(half, rasters, aerial, kinds_w, conv_w, conv_b, features, sums, stem_w, wide_w, stem3):
+    even = placed()[0] % 2 == 0
+    return jnp.where(even, high, low), jnp.where(even, low, high)
+
+
+def inner_kernel(
+    half, stem_in, w_in, gain, b_in, conv_w, conv_b, features, sums, stem_w, wide_w, stem3
+):
     spread = jnp.where(iota((KINDS, 64), 1) // 8 == iota((KINDS, 64), 0), 1.0, 0.0).astype(BF16)
     same = iota((256, 64), 0) // CH == iota((256, 64), 1) % 8
     halves = []
-    for part in split(kinds_w[...]):
+    for part in split(kinds_of(w_in, gain, b_in, 2)):
         rows = mm(jnp.concatenate([part] * 8, axis=0), spread)
         halves.append(jnp.where(same, rows, 0.0))
     stem_w[...] = jnp.concatenate(halves, axis=1).astype(BF16)
@@ -118,10 +138,7 @@
     stem3[edge * 96 : (edge + 1) * 96, :] = jnp.zeros((96, COLS), BF16)
     for block in blocks:
         y = block * 8
-        values = jnp.concatenate([rasters[k, y : y + 8, :] for k in range(4)], axis=0).astype(F32)
-        high, low = split(aerial[y : y + 8, :])
-        tail = jnp.concatenate([jnp.ones((8, COLS), BF16), jnp.zeros((8, COLS), BF16)], axis=0)
-        x = jnp.concatenate([values.astype(BF16), high, low, tail], axis=0)
+        x = stem_in[y * 8 : y * 8 + 64, :]
         out = jnp.maximum(mm(stem_w[...], jnp.concatenate([x, x], axis=0)), 0.0)
         for r in range(8):
             at = y + r - base
@@ -147,16 +164,16 @@
 
 
 def rim_kernel(
-    cells, place, rows, cols, partner, outer, even_message, odd_message, sums_low, sums_high,
-    kinds_w, conv_w, conv_b, rim_rows, rim_cols, pooled,
+    cells, rows, cols, partner, outer, even_message, odd_message, sums_low, sums_high,
+    w_in, gain, b_in, conv_w, conv_b, rim_rows, rim_cols, pooled,
 ):
-    has_above, has_below, has_left, has_right = flags(place, *cells)
-    left, right = sides(place, partner, outer, slice(0, 8), slice(8, 16))
+    has_above, has_below, has_left, has_right = flags(*cells)
+    left, right = sides(partner, outer, slice(0, 8), slice(8, 16))
     left, right = left * has_left, right * has_right
-    even = place[0] % 2 == 0
+    even = placed()[0] % 2 == 0
     above = jnp.where(even, odd_message[...], even_message[...]) * has_above
     below = jnp.where(even, even_message[...], odd_message[...]) * has_below
-    kind_high, kind_low = split(kinds_w[...])
+    kind_high, kind_low = split(kinds_of(w_in, gain, b_in, 1))
     stem_w = jnp.concatenate([kind_high, kind_high, kind_low], axis=1)
     bias = column(conv_b[...])
 
@@ -206,23 +223,44 @@
     stacked = [pltpu.roll(s, 1, 1), s, pltpu.roll(s, 255, 1)]
     value = conv(jnp.concatenate(stacked, axis=0).astype(BF16))
     rim_cols[...] = value
-    y, at = iota((256, SPOTS), 0), iota((256, SPOTS), 1)
-    p, q = at // POOL_COLS, at % POOL_COLS
-    picked = ((y // 4 == p) & (q == 0)) | (((y - 128) // 4 == p) & (y >= 128) & (q == POOL_COLS - 1))
+    y, at = iota((256, 128), 0), iota((256, 128), 1)
+    picked = (y < ROWS) & (y // 4 == at) | (y >= 128) & (y < 128 + ROWS) & (y // 4 - 16 == at)
     col_sums = mm(value, jnp.where(picked, 1.0 / 16, 0.0).astype(BF16))
+    lane = iota((CH, POOL_COLS), 1)
     for p in range(POOL_ROWS):
         at = p * POOL_COLS
         near = sums_low if p < POOL_ROWS // 2 else sums_high
         first = at % (SPOTS // 2)
-        total = near[:, first : first + POOL_COLS] + col_sums[:, at : at + POOL_COLS]
+        last = jnp.where(lane == POOL_COLS - 1, col_sums[:, 16 + p : 17 + p], 0.0)
+        total = near[:, first : first + POOL_COLS] + jnp.where(lane == 0, col_sums[:, p : p + 1], last)
         if p == 0:
             total += row_sums[0]
         if p == POOL_ROWS - 1:
             total += row_sums[1]
-        pooled[:, at : at + POOL_COLS] = total.astype(BF16)
-
-
-def merge_kernel(low, high, rim_rows, rim_cols, features):
+        pooled[0, :, at : at + POOL_COLS] = total.astype(BF16)
+    pooled[1, :, :] = jnp.zeros((CH, SPOTS), BF16)
+
+
+def head_weights(w_head, row_y, row_count, col_y, col_count):
+    shape = (10 * row_count, col_count * CH)
+    rows = iota((10 * row_count, 2), 0) // row_count % 2 == iota((10 * row_count, 2), 1)
+    pick = jnp.where(rows, 1.0, 0.0).astype(BF16)
+    dx = iota((10 * row_count, 160), 0) // (2 * row_count) == iota((10 * row_count, 160), 1) // CH
+    repeat = iota((160, shape[1]), 0) % CH == iota((160, shape[1]), 1) % CH
+    repeat = jnp.where(repeat, 1.0, 0.0).astype(BF16)
+    dy = row_y(iota(shape, 0) % row_count) - col_y(iota(shape, 1) // CH)
+    total = jnp.zeros(shape, F32)
+    for tap in range(5):
+        taps = mm(pick, w_head[:, tap * 160 : (tap + 1) * 160])
+        taps = mm(jnp.where(dx, taps, 0.0).astype(BF16), repeat)
+        total = jnp.where(dy == tap - 2, taps, total)
+    return total.astype(BF16)
+
+
+def merge_kernel(low, high, rim_rows, rim_cols, w_head, features, head_w, rim_w):
+    head_w[...] = head_weights(w_head[...], lambda r: r, 16, lambda r: r - 2, 20)
+    outside = lambda r: jnp.where(r < 2, r - 2, ROWS - 2 + r)
+    rim_w[...] = head_weights(w_head[...], outside, 4, lambda r: jnp.where(r < 2, r, ROWS - 4 + r), 4)
     lane = iota((CH, 128), 1)
     columns = rim_cols[...].astype(F32)
     for y in range(ROWS):
@@ -249,50 +287,66 @@
 NAMES = ("own", "band", "band_p", "one", "one_p", "two", "two_p", "relay", "relay_p")
 
 
-def logits_kernel(
-    cells, place, features, own, band_m, band_p, one_m, one_p, two_m, two_p, relay, relay_p,
-    proj_w, proj_b, ctx_w, up_w, up_b, head_w, rim_w, head_b,
-    logits, col_out, row_out, weights, proj, low_up, lifted, decoded,
-):
-    arrays = dict(zip(NAMES, (own, band_m, band_p, one_m, one_p, two_m, two_p, relay, relay_p)))
+EARLY = [at for at in range(15) if MAPS[(at // 5 - 1, at % 5 - 2)][0] in NAMES[:4]]
+LATE = [at for at in range(15) if at not in EARLY]
+
+
+def context_sum(cells, which, arrays, proj_w, proj_b, ctx_w, weights, proj, finish):
     last_cross, last_band = cells
-    cross, band = place[0], place[1]
+    cross, band = placed()
     core = band % 2
     sign = 1 - 2 * core
-    maps = []
-
-    for at in range(15):
-        u, v = at // 5 - 1, at % 5 - 2
-        maps.append(MAPS[(u, v)])
-        row, col = cross + u * sign, band + v * sign
+    for k, at in enumerate(which):
+        row, col = cross + (at // 5 - 1) * sign, band + (at % 5 - 2) * sign
         inside = (row >= 0) & (row <= last_cross) & (col >= 0) & (col <= last_band)
         one = ctx_w[:, at * WIDE : (at + 1) * WIDE]
         two = ctx_w[:, (14 - at) * WIDE : (15 - at) * WIDE]
         chosen = jnp.where(core == 0, one, two)
-        weights[:, at * WIDE : (at + 1) * WIDE] = jnp.where(inside, chosen, jnp.zeros_like(chosen))
-
+        weights[:, k * WIDE : (k + 1) * WIDE] = jnp.where(inside, chosen, jnp.zeros_like(chosen))
     p_bias = jnp.broadcast_to(column(proj_b[...]), (WIDE, 256))
+
+    def part(at, carry):
+        spots = pl.ds(pl.multiple_of(at * 256, 256), 256)
+        for k, tile in enumerate(which):
+            name, half = MAPS[(tile // 5 - 1, tile % 5 - 2)]
+            out = mm(proj_w[...], arrays[name][half, :, spots])
+            proj[k * WIDE : (k + 1) * WIDE, :] = jnp.maximum(out + p_bias, 0.0).astype(BF16)
+        finish(at, spots, mm(weights[...], proj[...]))
+        return carry
+
+    lax.fori_loop(0, SPOTS // 256, part, 0, unroll=True)
+
+
+def early_kernel(cells, *refs):
+    arrays = dict(zip(NAMES[:4], refs[:4]))
+    proj_w, proj_b, ctx_w, context, weights, proj = refs[4:]
+    own = EARLY.index(7)
+
+    def finish(at, spots, total):
+        context[:, spots] = total + proj[own * WIDE : (own + 1) * WIDE, :].astype(F32)
+
+    context_sum(cells, EARLY, arrays, proj_w, proj_b, ctx_w, weights, proj, finish)
+
+
+def logits_kernel(
+    cells, features, context, one_p, two_m, two_p, relay, relay_p,
+    proj_w, proj_b, ctx_w, up_w, up_b, head_w, rim_w, head_b,
+    logits, col_out, row_out, weights, proj, low_up, lifted, decoded,
+):
+    arrays = dict(zip(NAMES[4:], (one_p, two_m, two_p, relay, relay_p)))
     u_bias = jnp.broadcast_to(column(up_b[...]), (CH, 256))
 
-    def context_part(part, carry):
-        at = pl.multiple_of(part * 256, 256)
-        for k in range(15):
-            name, half = maps[k]
-            out = mm(proj_w[...], arrays[name][half, :, pl.ds(at, 256)])
-            proj[k * WIDE : (k + 1) * WIDE, :] = jnp.maximum(out + p_bias, 0.0).astype(BF16)
-        context = mm(weights[...], proj[...]) + proj[7 * WIDE : 8 * WIDE, :].astype(F32)
-        mixed = jnp.maximum(context, 0.0).astype(BF16)
+    def finish(part, spots, total):
+        mixed = jnp.maximum(total + context[:, spots], 0.0).astype(BF16)
         up = mm(up_w[...], mixed) + u_bias
-        high = up.astype(BF16)
-        low = (up - high.astype(F32)).astype(BF16)
+        high, low = split(up)
         both = [
             jnp.concatenate([high[:, h * 128 : (h + 1) * 128], low[:, h * 128 : (h + 1) * 128]], axis=1)
             for h in range(2)
         ]
         low_up[pl.ds(pl.multiple_of(part * 64, 64), 64), :] = jnp.concatenate(both, axis=0)
-        return carry
-
-    lax.fori_loop(0, SPOTS // 256, context_part, 0)
+
+    context_sum(cells, LATE, arrays, proj_w, proj_b, ctx_w, weights, proj, finish)
 
     widen = jnp.where(
         iota((256, COLS), 0) % 128 == iota((256, COLS), 1) // 4, 1.0, 0.0
@@ -310,7 +364,7 @@
             decoded[pl.ds(pl.multiple_of(at + 64, CH), CH), :] = value
         return carry
 
-    lax.fori_loop(0, POOL_ROWS, decode, 0)
+    lax.fori_loop(0, POOL_ROWS, decode, 0, unroll=4)
 
     def gather_taps(z, count):
         total = None
@@ -335,7 +389,7 @@
         col_out[pl.ds(y, 16), :] = jnp.where(first_lanes, rim[:16], pltpu.roll(rim[16:], 4, 1))
         return carry
 
-    lax.fori_loop(0, ROWS // 16, head, 0)
+    lax.fori_loop(0, ROWS // 16, head, 0, unroll=True)
 
     ends = jnp.concatenate([decoded[64:128, :], decoded[64 * CH : 66 * CH, :]], axis=0)
     total = gather_taps(mm(rim_w[...], ends), 8)
@@ -343,27 +397,22 @@
     col_out[ROWS : ROWS + 8, :] = total[:, COLS:]
 
 
-def row_sum_kernel(cells, place, row_out, partner, outer, out):
-    _, _, has_left, has_right = flags(place, *cells)
+def row_sums(cells, row_out, partner, outer):
+    _, _, has_left, has_right = flags(*cells)
     corners = slice(ROWS, ROWS + 8)
-    left, right = sides(place, partner, outer, corners, corners)
-    lane = iota((8, 128), 1)
-    out[...] = row_out[...] + jnp.concatenate(
-        [
-            jnp.where(lane < 2, left * has_left, 0.0),
-            jnp.zeros((8, COLS - 256), F32),
-            jnp.where(lane >= 126, right * has_right, 0.0),
-        ],
-        axis=1,
-    )
-
-
-def sum_kernel(cells, place, inner, partner, outer, even_message, odd_message, out):
-    has_above, has_below, has_left, has_right = flags(place, *cells)
-    even = place[0] % 2 == 0
+    left, right = sides(partner, outer, corners, corners)
+    lane = lax.broadcasted_iota(jnp.int32, (8, 128), 1)
+    low = jnp.where(lane < 2, left * has_left, 0.0)
+    high = jnp.where(lane >= 126, right * has_right, 0.0)
+    return row_out + jnp.concatenate([low, jnp.zeros((8, COLS - 256), F32), high], axis=1)
+
+
+def sum_kernel(cells, inner, partner, outer, even_message, odd_message, out):
+    has_above, has_below, has_left, has_right = flags(*cells)
+    even = placed()[0] % 2 == 0
     above = jnp.where(even, odd_message[...], even_message[...]) * has_above
     below = jnp.where(even, even_message[...], odd_message[...]) * has_below
-    left, right = sides(place, partner, outer, slice(0, ROWS), slice(0, ROWS))
+    left, right = sides(partner, outer, slice(0, ROWS), slice(0, ROWS))
     left, right = left * has_left, right * has_right
     out[...] = inner[...]
     lane = iota((ROWS, 128), 1)
@@ -376,14 +425,31 @@
         out[k, ROWS - 2 : ROWS, :] += below[4 * k : 4 * k + 2]
 
 
-def call(kernel, outs, args, scratch=(), smem=(0,), flops=0):
+def call(kernel, outs, args, scratch=(), smem=(), hbm=(), flops=0):
+    scratch = list(scratch)
+
+    def fetching(*refs):
+        ins, rest = list(refs[: len(args)]), refs[len(args) :]
+        buffers, sems = rest[-len(hbm) - 1 : -1], rest[-1]
+        copies = [pltpu.make_async_copy(ins[at], buffers[i], sems.at[i]) for i, at in enumerate(hbm)]
+        for copy in copies:
+            copy.start()
+        for copy in copies:
+            copy.wait()
+        for at, buffer in zip(hbm, buffers):
+            ins[at] = buffer
+        kernel(*ins, *rest[: -len(hbm) - 1])
+
+    if hbm:
+        scratch += [pltpu.VMEM(args[at].shape, args[at].dtype) for at in hbm]
+        scratch += [pltpu.SemaphoreType.DMA((len(hbm),))]
     return pl.pallas_call(
-        kernel,
+        fetching if hbm else kernel,
         out_shape=outs,
-        in_specs=[SMEM if at in smem else VMEM for at in range(len(args))],
+        in_specs=[SMEM if at in smem else HBM if at in hbm else VMEM for at in range(len(args))],
         out_specs=jax.tree.map(lambda _: VMEM, outs),
-        scratch_shapes=list(scratch),
-        compiler_params=pltpu.CompilerParams(vmem_limit_bytes=56 * 1024 * 1024),
+        scratch_shapes=scratch,
+        compiler_params=pltpu.CompilerParams(vmem_limit_bytes=24 * 1024 * 1024),
         cost_estimate=pl.CostEstimate(flops=flops, bytes_accessed=1 << 20, transcendentals=0),
     )(*args)
 
@@ -393,7 +459,7 @@
     w_ctx, w_up, b_up, w_head, b_head,
 ):
     cells = (n_cross - 1, n_band - 1)
-    place = jnp.stack([lax.axis_index("cross"), lax.axis_index("band")]).astype(jnp.int32)
+    tie = lax.optimization_barrier
 
     def moved(x, source):
         route = []
@@ -418,87 +484,85 @@
     def beside(x, u):
         return moved(x, lambda c, b: (c + u * (1 - 2 * (b % 2)), b - 2 + 4 * (b % 2)))
 
-    rows, cols, message = call(
+    rows, cols, message, stem_in = call(
         halo_kernel,
-        [shape_of(32, COLS), shape_of(32, 128), shape_of(16, 128)],
+        [shape_of(32, COLS), shape_of(32, 128), shape_of(16, 128), shape_of(8 * ROWS, COLS, dtype=BF16)],
         [rasters, aerial],
-        smem=(),
+        flops=2 * 10**10,
     )
     near, far = partner(message), outer(message)
 
-    gain = aerial_gain[:, None]
-    kinds_8 = jnp.concatenate([w_in, gain, gain, b_in[:, None], jnp.zeros_like(gain)], axis=1)
-    kinds_5 = jnp.concatenate([w_in, gain, b_in[:, None], jnp.zeros((CH, 2), F32)], axis=1)
-    conv_b = b_conv1[None, :]
-
-    def inner(half):
+    stem_args = [w_in.T, aerial_gain[None, :], b_in[None, :], w_conv1, b_conv1[None, :]]
+    proj_args = [w_proj, b_proj[None, :], w_ctx]
+
+    def inner(half, stem_in):
         return call(
             functools.partial(inner_kernel, half),
             [shape_of(HALF * CH, COLS, dtype=BF16), shape_of(CH, SPOTS // 2)],
-            [rasters, aerial, kinds_8, w_conv1, conv_b],
+            [stem_in, *stem_args],
             [
                 pltpu.VMEM((256, 128), BF16),
                 pltpu.VMEM((256, 960), BF16),
                 pltpu.VMEM(((HALF + 2) * 96, COLS), BF16),
             ],
-            smem=(),
             flops=4 * 10**9,
         )
 
-    feat_low, sums_low = inner(0)
-    even_out, odd_out = call(
-        functools.partial(row_message_kernel, cells), [shape_of(8, COLS + 128)] * 2, [place, rows, near, far]
-    )
+    feat_low, sums_low = inner(0, stem_in)
+    near, far, sums_low = tie((near, far, sums_low))
+    even_out, odd_out = row_messages(cells, rows, near, far)
+    even_out, odd_out, stem_in = tie((even_out, odd_out, stem_in))
     even_in, odd_in = even_pair(even_out), odd_pair(odd_out)
-    feat_high, sums_high = inner(1)
-
-    taps = w_head.reshape(2, 5, 5, CH)[:, ::-1].transpose(2, 0, 1, 3).reshape(10, 5 * CH)
-    skewed = jnp.broadcast_to(jnp.pad(taps, ((0, 0), (0, 16 * CH)))[:, None, :], (10, 16, 21 * CH))
-    head_w = skewed.reshape(10, 16 * 21 * CH)[:, : 16 * 20 * CH].reshape(160, 20 * CH)
-    gap = jnp.zeros((10, CH), BF16)
-    at = [taps[:, (4 - d) * CH : (5 - d) * CH] for d in range(5)]
-    ends = [[at[0], gap, gap, gap], [at[1], at[0], gap, gap], [gap, gap, at[4], at[3]], [gap, gap, gap, at[4]]]
-    rim_w = jnp.stack([jnp.concatenate(r, axis=1) for r in ends], axis=1).reshape(40, 4 * CH)
-    head_w, rim_w, rows = lax.optimization_barrier((head_w, rim_w, rows))
-
-    rim_rows, rim_cols, pooled = call(
+    feat_high, sums_high = inner(1, stem_in)
+
+    rim_rows, rim_cols, own = call(
         functools.partial(rim_kernel, cells),
-        [shape_of(2 * CH, COLS, dtype=BF16), shape_of(CH, 256, dtype=BF16), shape_of(CH, SPOTS, dtype=BF16)],
-        [place, rows, cols, near, far, even_in, odd_in, sums_low, sums_high, kinds_5, w_conv1, conv_b],
-    )
-
-    own = jnp.stack([pooled, partner(pooled)])
+        [shape_of(2 * CH, COLS, dtype=BF16), shape_of(CH, 256, dtype=BF16), shape_of(2, CH, SPOTS, dtype=BF16)],
+        [rows, cols, near, far, even_in, odd_in, sums_low, sums_high, *stem_args],
+    )
+
+    own = own.at[1].set(partner(own)[0])
+    own, rim_rows = tie((own, rim_rows))
     one = beside(own, -1)
     band = beside(own, 0)
     two = beside(own, 1)
+    features, head_w, rim_w = call(
+        merge_kernel,
+        [shape_of(ROWS * CH, COLS, dtype=BF16), shape_of(160, 20 * CH, dtype=BF16), shape_of(40, 4 * CH, dtype=BF16)],
+        [feat_low, feat_high, rim_rows, rim_cols, w_head],
+    )
+    one, features = tie((one, features))
     relay = outer(one)
-    maps = [own, band, partner(band), one, partner(one), two, partner(two), relay, partner(relay)]
-
-    features = call(
-        merge_kernel, shape_of(ROWS * CH, COLS, dtype=BF16), [feat_low, feat_high, rim_rows, rim_cols], smem=(),
-        flops=10**9,
-    )
+    band_p, one_p = partner(band), partner(one)
+    context = call(
+        functools.partial(early_kernel, cells), shape_of(WIDE, SPOTS), [own, band, band_p, one, *proj_args],
+        [pltpu.VMEM((WIDE, len(EARLY) * WIDE), BF16), pltpu.VMEM((len(EARLY) * WIDE, 256), BF16)],
+    )
+    relay, two, context = tie((relay, two, context))
+    two_p, relay_p = partner(two), partner(relay)
+
     inner_logits, col_out, row_out = call(
         functools.partial(logits_kernel, cells),
         [shape_of(2, ROWS, COLS), shape_of(ROWS + 8, 128), shape_of(8, COLS)],
-        [place, features, *maps, w_proj, b_proj[None, :], w_ctx, w_up, b_up[None, :], head_w, rim_w, b_head],
         [
-            pltpu.VMEM((WIDE, 15 * WIDE), BF16),
-            pltpu.VMEM((15 * WIDE, 256), BF16),
+            features, context, one_p, two, two_p, relay, relay_p,
+            *proj_args, w_up, b_up[None, :], head_w, rim_w, b_head,
+        ],
+        [
+            pltpu.VMEM((WIDE, len(LATE) * WIDE), BF16),
+            pltpu.VMEM((len(LATE) * WIDE, 256), BF16),
             pltpu.VMEM((POOL_ROWS * CH, 256), BF16),
             pltpu.VMEM((POOL_ROWS * CH, COLS), F32),
             pltpu.VMEM(((ROWS + 4) * CH, COLS), BF16),
         ],
-        smem=(0, 18),
+        smem=(14,),
     )
     near, far = partner(col_out), outer(col_out)
-    row_out = call(
-        functools.partial(row_sum_kernel, cells), shape_of(8, COLS), [place, row_out, near, far]
-    )
+    row_out = row_sums(cells, row_out, near, far)
     return call(
         functools.partial(sum_kernel, cells),
         shape_of(2, ROWS, COLS),
-        [place, inner_logits, near, far, even_pair(row_out), odd_pair(row_out)],
+        [inner_logits, near, far, even_pair(row_out), odd_pair(row_out)],
     )
 
 

time: 95 us -> 70.6 us (0.74)
  Pallas kernels: 35.1 us -> 19.4 us
  local copies, waits for them, and re-layouts: 9.29 us -> 4.49 us
  waiting for transfers between devices: 28.7 us -> 24.7 us
  starting transfers between devices: 19.6 us -> 21.2 us
  other arithmetic: 1.67 us -> 0.33 us
    pallas_call x9 -> x8, Pallas kernels: 35.1 us -> 19.4 us  [call(): pl.pallas_call(fetching if hbm else kernel, out_shape=outs, in_specs=[SME...]
    ppermute x17, waiting for transfers between devices: 28.7 us -> 24.7 us  [moved(): return lax.ppermute(x, ('band', 'cross'), route)]
    concatenate x4 -> x1, local copies, waits for them, and re-layouts: 2.18 us -> 0.01 us  [row_sums(): jnp.concatenate([low, jnp.zeros((8, COLS - 256), F32), high], axis=1)]
    reshape x4 -> x0, local copies, waits for them, and re-layouts: 2.12 us -> none  [the longest x2 1.26 us: body(): skewed.reshape(10, 16 * 21 * CH)[:, :16 * 20 * CH].reshape(160, 20 * CH)]
    ppermute x17, starting transfers between devices: 19.6 us -> 21.2 us  [moved(): return lax.ppermute(x, ('band', 'cross'), route)]
    another operation x3 -> x0, other arithmetic: 1.6 us -> none  [the longest x1 0.93 us: body(): own = jnp.stack([pooled, partner(pooled)])]
    unnamed x43 -> x37, local copies, waits for them, and re-layouts: 4.09 us -> 3.82 us
  transfers between devices with their start and end apart: 17 -> 17, of which waited for: 7 -> 11; matrix products, arithmetic and copies ran while one was open for 7% -> 0% of each run, Pallas kernels for 13% -> 14%
where the time goes in v3:
time: 70.6 us; the launch traced here: 70.4 us
  waiting for transfers between devices  24.7 us (35%)
  starting transfers between devices  21.2 us (30%)
  Pallas kernels  19.4 us (27%)
  local copies, waits for them, and re-layouts  4.49 us (6%)
    ppermute x17, waiting for transfers between devices, moved(): return lax.ppermute(x, ('band', 'cross'), route)  24.7 us
    ppermute x17, starting transfers between devices, moved(): return lax.ppermute(x, ('band', 'cross'), route)  21.2 us
    pallas_call x8, Pallas kernels, call(): pl.pallas_call(fetching if hbm else kernel, out_shape=outs, in_specs=[SME...  19.4 us
    unnamed x37, local copies, waits for them, and re-layouts  3.82 us
  transfers between devices with their start and end apart: 17, of which 11 were waited for; matrix products, arithmetic and copies ran while one was open for 0% of the time, Pallas kernels for 14%

profile of v3, /device:TPU:0, one launch (start us, length us, event | category | flops | bytes accessed | tf_op | source)
XLA Modules:
  0.0 70.4 jit_solution(16316015925545396935)
XLA Ops:
  0.0 1.1 %copy-done.15 = s32[4,64,512]{2,1,0:T(8,128)S(1)} copy-done((s32[4,64,512]{2,1,0:T(8,128)S(1)}, s32[4,64,512]{2,1,0:T(8,128)}, u32[]{:S(2)}) %copy-start.15) | copy-done | bytes 524312
  1.1 0.9 %copy-done.16 = f32[64,512]{1,0:T(8,128)S(1)} copy-done((f32[64,512]{1,0:T(8,128)S(1)}, f32[64,512]{1,0:T(8,128)}, u32[]{:S(2)}) %copy-start.16) | copy-done | bytes 131096
  2.0 0.3 shard_map.136
  2.3 0.1 collective-permute-start
  2.4 4.1 %collective-permute-start.1 = (f32[16,128]{1,0:T(8,128)S(1)}, f32[16,128]{1,0:T(8,128)S(1)}, u32[]{:S(2)}, u32[]{:S(2)}) collective-permute-start(f32[16,128]{1,0:T(8,128)S(1)} %get-tuple-element.49), channel_id=1, source_target_pairs={{120,0},{16,8},{8,16},{32,24},{24,32},{48,40},{40,48},{64,56},{56,... | collective-permute-start | bytes 24584 | tf_op jit(solution)/shard_map/ppermute | solution.py:470
  6.6 2.5 %shard_map.137 = (bf16[1024,512]{1,0:T(8,128)(2,1)S(1)}, f32[32,1024]{1,0:T(8,128)S(1)}) custom-call(bf16[512,512]{1,0:T(8,128)(2,1)S(1)} %get-tuple-element.57.stem_in, f32[4,32]{1,0:T(4,128)S(1)} %bitcast.6, f32[1,32]{1,0:T(1,128)S(1)} %bitcast.11, f32[1,32]{1,0:T(1,128)S(1)} %bitcast.14, bf16[32,288]{1,0:T(8,128)(2,1)S(1)} %copy-done.5, f32[1,32]{1,0:T(1,128)S(1)} %bitcast.17), custom_call_target="tpu_custom_call" | custom-call | flops 4000000000 | bytes 1048576 | tf_op jit(solution)/shard_map/pallas_call | solution.py:446
  9.1 1.0 %copy-done.1 = bf16[1024,512]{1,0:T(8,128)(2,1)} copy-done((bf16[1024,512]{1,0:T(8,128)(2,1)}, bf16[1024,512]{1,0:T(8,128)(2,1)S(1)}, u32[]{:S(2)}) %copy-start.1) | copy-done | bytes 1048600
  10.1 0.0 collective-permute-done.partner
  10.1 0.0 collective-permute-done.1.outer
  10.1 0.2 multiply_reduce_fusion.2
  10.3 0.1 select_select_fusion.1
  10.4 0.0 copy-start.7
  10.4 2.8 %collective-permute-start.2 = (f32[8,640]{1,0:T(8,128)S(1)}, f32[8,640]{1,0:T(8,128)S(1)}, u32[]{:S(2)}, u32[]{:S(2)}) collective-permute-start(f32[8,640]{1,0:T(8,128)S(1)} %get-tuple-element.54), channel_id=1, source_target_pairs={{1,0},{9,8},{17,16},{25,24},{33,32},{41,40},{49,48},{57,56},{65,64... | collective-permute-start | bytes 61448 | tf_op jit(solution)/shard_map/ppermute | solution.py:470
  13.2 4.3 %collective-permute-start.3 = (f32[8,640]{1,0:T(8,128)S(1)}, f32[8,640]{1,0:T(8,128)S(1)}, u32[]{:S(2)}, u32[]{:S(2)}) collective-permute-start(f32[8,640]{1,0:T(8,128)S(1)} %get-tuple-element.55), channel_id=1, source_target_pairs={{7,0},{15,8},{23,16},{31,24},{39,32},{47,40},{55,48},{63,56},{71,6... | collective-permute-start | bytes 61448 | tf_op jit(solution)/shard_map/ppermute | solution.py:470
  17.5 2.5 %shard_map.138 = (bf16[1024,512]{1,0:T(8,128)(2,1)S(1)}, f32[32,1024]{1,0:T(8,128)S(1)}) custom-call(bf16[512,512]{1,0:T(8,128)(2,1)S(1)} %get-tuple-element.57.stem_in, f32[4,32]{1,0:T(4,128)S(1)} %bitcast.7, f32[1,32]{1,0:T(1,128)S(1)} %bitcast.12, f32[1,32]{1,0:T(1,128)S(1)} %bitcast.15, bf16[32,288]{1,0:T(8,128)(2,1)S(1)} %copy-done.5, f32[1,32]{1,0:T(1,128)S(1)} %bitcast.18), custom_call_target="tpu_custom_call" | custom-call | flops 4000000000 | bytes 1048576 | tf_op jit(solution)/shard_map/pallas_call | solution.py:446
  20.0 0.0 copy-start.17
  20.0 0.0 copy-start
  20.0 0.0 copy-start.9
  20.1 0.0 collective-permute-done.2.even_message
  20.1 0.6 collective-permute-done.3.odd_message
  20.6 2.4 %shard_map.139 = (bf16[64,512]{1,0:T(8,128)(2,1)S(1)}, bf16[32,256]{1,0:T(8,128)(2,1)S(1)}, bf16[2,32,2048]{2,1,0:T(8,128)(2,1)}) custom-call(f32[32,512]{1,0:T(8,128)S(1)} %get-tuple-element.47.rows, f32[32,128]{1,0:T(8,128)S(1)} %get-tuple-element.48.cols, f32[16,128]{1,0:T(8,128)S(1)} %collective-permute-done.partner, ...), custom_call_target="tpu_custom_call" | custom-call | bytes 1048576 | tf_op jit(solution)/shard_map/pallas_call | solution.py:446
  23.0 0.0 collective-permute-start.4
  23.0 1.7 %collective-permute-done.4 = bf16[2,32,2048]{2,1,0:T(8,128)(2,1)S(1)} collective-permute-done((bf16[2,32,2048]{2,1,0:T(8,128)(2,1)}, bf16[2,32,2048]{2,1,0:T(8,128)(2,1)S(1)}, u32[]{:S(2)}, u32[]{:S(2)}) %collective-permute-start.4) | collective-permute-done | bytes 262176 | tf_op jit(solution)/shard_map/ppermute | solution.py:470
  24.8 0.7 slice_dynamic-update-slice_fusion.refs_0_
  25.5 4.2 %collective-permute-start.7 = (bf16[2,32,2048]{2,1,0:T(8,128)(2,1)}, bf16[2,32,2048]{2,1,0:T(8,128)(2,1)S(1)}, u32[]{:S(2)}, u32[]{:S(2)}) collective-permute-start(bf16[2,32,2048]{2,1,0:T(8,128)(2,1)} %slice_dynamic-update-slice_fusion.refs_0_), channel_id=1, source_target_pairs={{113,0},{31,8},{1,16},{47,24},{17,32},{63,40},{33,48},{79,56},{49,... | collective-permute-start | bytes 786440 | tf_op jit(solution)/shard_map/ppermute | solution.py:470
  29.7 0.0 copy-start.14
  29.7 1.5 %shard_map.140 = (bf16[2048,512]{1,0:T(8,128)(2,1)S(1)}, bf16[160,640]{1,0:T(8,128)(2,1)S(1)}, bf16[40,128]{1,0:T(8,128)(2,1)S(1)}) custom-call(bf16[1024,512]{1,0:T(8,128)(2,1)S(1)} %copy-done.2, bf16[1024,512]{1,0:T(8,128)(2,1)S(1)} %get-tuple-element.63.high, bf16[64,512]{1,0:T(8,128)(2,1)S(1)} %get-tuple-element.64.rim_rows, ...), custom_call_target="tpu_custom_call" | custom-call | bytes 1048576 | tf_op jit(solution)/shard_map/pallas_call | solution.py:446
  31.1 0.7 copy-done.3
  31.8 3.3 %collective-permute-done.8.refs_1_ = bf16[2,32,2048]{2,1,0:T(8,128)(2,1)} collective-permute-done((bf16[2,32,2048]{2,1,0:T(8,128)(2,1)}, bf16[2,32,2048]{2,1,0:T(8,128)(2,1)}, u32[]{:S(2)}, u32[]{:S(2)}) %collective-permute-start.8) | collective-permute-done | bytes 262176 | tf_op jit(solution)/shard_map/ppermute | solution.py:470
  35.1 4.7 %collective-permute-done.5.refs_3_ = bf16[2,32,2048]{2,1,0:T(8,128)(2,1)S(1)} collective-permute-done((bf16[2,32,2048]{2,1,0:T(8,128)(2,1)}, bf16[2,32,2048]{2,1,0:T(8,128)(2,1)S(1)}, u32[]{:S(2)}, u32[]{:S(2)}) %collective-permute-start.5) | collective-permute-done | bytes 262176 | tf_op jit(solution)/shard_map/ppermute | solution.py:470
  39.8 0.1 copy.17.refs_4_.proj_w
  39.9 0.1 collective-permute-start.10
  40.0 0.0 collective-permute-done.9.refs_2_
  40.1 3.3 %shard_map.141.context = f32[128,2048]{1,0:T(8,128)S(1)} custom-call(bf16[2,32,2048]{2,1,0:T(8,128)(2,1)} %slice_dynamic-update-slice_fusion.refs_0_, bf16[2,32,2048]{2,1,0:T(8,128)(2,1)} %collective-permute-done.8.refs_1_, bf16[2,32,2048]{2,1,0:T(8,128)(2,1)} %collective-permute-done.9.refs_2_, bf16[2,32,2048]{2,1,0:T(8,128)(2,1)S(1)} %collective-permute-done.5.refs_3_, ...), custom_call_target="tpu_custom_call" | custom-call | bytes 1048576 | tf_op jit(solution)/shard_map/pallas_call | solution.py:446
  43.4 5.0 %collective-permute-done.6.relay = bf16[2,32,2048]{2,1,0:T(8,128)(2,1)S(1)} collective-permute-done((bf16[2,32,2048]{2,1,0:T(8,128)(2,1)S(1)}, bf16[2,32,2048]{2,1,0:T(8,128)(2,1)S(1)}, u32[]{:S(2)}, u32[]{:S(2)}) %collective-permute-start.6) | collective-permute-done | bytes 262176 | tf_op jit(solution)/shard_map/ppermute | solution.py:470
  48.4 0.5 collective-permute-start.12
  48.9 1.0 %collective-permute-done.11.two_p = bf16[2,32,2048]{2,1,0:T(8,128)(2,1)S(1)} collective-permute-done((bf16[2,32,2048]{2,1,0:T(8,128)(2,1)S(1)}, bf16[2,32,2048]{2,1,0:T(8,128)(2,1)S(1)}, u32[]{:S(2)}, u32[]{:S(2)}) %collective-permute-start.11) | collective-permute-done | bytes 262176 | tf_op jit(solution)/shard_map/ppermute | solution.py:470
  49.9 0.4 collective-permute-done.12.relay_p
  50.3 6.1 %shard_map.142 = (f32[2,64,512]{2,1,0:T(8,128)S(1)}, f32[72,128]{1,0:T(8,128)S(1)}, f32[8,512]{1,0:T(8,128)S(1)}) custom-call(bf16[2048,512]{1,0:T(8,128)(2,1)S(1)} %get-tuple-element.67.features, f32[128,2048]{1,0:T(8,128)S(1)} %shard_map.141.context, bf16[2,32,2048]{2,1,0:T(8,128)(2,1)S(1)} %collective-permute-done.10.one_p, ...), custom_call_target="tpu_custom_call" | custom-call | bytes 1048576 | tf_op jit(solution)/shard_map/pallas_call | solution.py:446
  56.4 0.2 collective-permute-start.13
  56.6 0.4 collective-permute-start.14
  57.0 0.6 collective-permute-done.13.partner
  57.6 4.4 %collective-permute-done.14.outer = f32[72,128]{1,0:T(8,128)S(1)} collective-permute-done((f32[72,128]{1,0:T(8,128)S(1)}, f32[72,128]{1,0:T(8,128)S(1)}, u32[]{:S(2)}, u32[]{:S(2)}) %collective-permute-start.14) | collective-permute-done | bytes 36896 | tf_op jit(solution)/shard_map/ppermute | solution.py:470
  62.1 0.1 collective-permute-start.15
  62.2 4.4 %collective-permute-start.16 = (f32[8,512]{1,0:T(8,128)S(1)}, f32[8,512]{1,0:T(8,128)S(1)}, u32[]{:S(2)}, u32[]{:S(2)}) collective-permute-start(f32[8,512]{1,0:T(8,128)S(1)} %maximum_add_fusion), channel_id=1, source_target_pairs={{7,0},{15,8},{23,16},{31,24},{39,32},{47,40},{55,48},{63,56},{71,6... | collective-permute-start | bytes 49160 | tf_op jit(solution)/shard_map/ppermute | solution.py:470
  66.6 0.8 %collective-permute-done.15.even_message = f32[8,512]{1,0:T(8,128)S(1)} collective-permute-done((f32[8,512]{1,0:T(8,128)S(1)}, f32[8,512]{1,0:T(8,128)S(1)}, u32[]{:S(2)}, u32[]{:S(2)}) %collective-permute-start.15) | collective-permute-done | bytes 16416 | tf_op jit(solution)/shard_map/ppermute | solution.py:470
  67.4 2.2 %collective-permute-done.16.odd_message = f32[8,512]{1,0:T(8,128)S(1)} collective-permute-done((f32[8,512]{1,0:T(8,128)S(1)}, f32[8,512]{1,0:T(8,128)S(1)}, u32[]{:S(2)}, u32[]{:S(2)}) %collective-permute-start.16) | collective-permute-done | bytes 16416 | tf_op jit(solution)/shard_map/ppermute | solution.py:470
  69.6 0.8 %shard_map.143 = f32[2,64,512]{2,1,0:T(8,128)} custom-call(f32[2,64,512]{2,1,0:T(8,128)S(1)} %get-tuple-element.74.inner, f32[72,128]{1,0:T(8,128)S(1)} %collective-permute-done.13.partner, f32[72,128]{1,0:T(8,128)S(1)} %collective-permute-done.14.outer, f32[8,512]{1,0:T(8,128)S(1)} %collective-permute-done.15.even_message, ...), custom_call_target="tpu_custom_call" | custom-call | bytes 1048576 | tf_op jit(solution)/shard_map/pallas_call | solution.py:446
  (43 shorter events, 0.1 us)
Async XLA Ops:
  0.0 6.5 %copy-start.8 = (f32[32,4]{0,1:T(4,128)S(1)}, f32[32,4]{0,1:T(4,128)}, u32[]{:S(2)}) copy-start(f32[32,4]{0,1:T(4,128)} %param.18) | copy-start | bytes 1540
  0.0 6.5 %copy-start.10 = (f32[32]{0:T(128)S(1)}, f32[32]{0:T(128)}, u32[]{:S(2)}) copy-start(f32[32]{0:T(128)} %param.19) | copy-start | bytes 388
  0.0 6.5 %copy-start.11 = (f32[32]{0:T(128)S(1)}, f32[32]{0:T(128)}, u32[]{:S(2)}) copy-start(f32[32]{0:T(128)} %param.20) | copy-start | bytes 388
  0.0 6.5 %copy-start.12 = (f32[32]{0:T(128)S(1)}, f32[32]{0:T(128)}, u32[]{:S(2)}) copy-start(f32[32]{0:T(128)} %param.22) | copy-start | bytes 388
  0.0 6.5 %copy-start.5 = (bf16[32,288]{1,0:T(8,128)(2,1)S(1)}, bf16[32,288]{1,0:T(8,128)(2,1)}, u32[]{:S(2)}) copy-start(bf16[32,288]{1,0:T(8,128)(2,1)} %conv_w.5) | copy-start | bytes 55300
  0.0 1.1 %copy-start.15 = (s32[4,64,512]{2,1,0:T(8,128)S(1)}, s32[4,64,512]{2,1,0:T(8,128)}, u32[]{:S(2)}) copy-start(s32[4,64,512]{2,1,0:T(8,128)} %rasters.1) | copy-start | bytes 1572868
  1.1 0.9 %copy-start.16 = (f32[64,512]{1,0:T(8,128)S(1)}, f32[64,512]{1,0:T(8,128)}, u32[]{:S(2)}) copy-start(f32[64,512]{1,0:T(8,128)} %aerial.1) | copy-start | bytes 393220
  2.3 7.7 %collective-permute-start = (f32[16,128]{1,0:T(8,128)S(1)}, f32[16,128]{1,0:T(8,128)S(1)}, u32[]{:S(2)}, u32[]{:S(2)}) collective-permute-start(f32[16,128]{1,0:T(8,128)S(1)} %get-tuple-element.49), channel_id=1, source_target_pairs={{8,0},{0,8},{24,16},{16,24},{40,32},{32,40},{56,48},{48,56},{72,64... | collective-permute-start | bytes 24584 | tf_op jit(solution)/shard_map/ppermute | solution.py:470
  2.4 7.7 %collective-permute-start.1 = (f32[16,128]{1,0:T(8,128)S(1)}, f32[16,128]{1,0:T(8,128)S(1)}, u32[]{:S(2)}, u32[]{:S(2)}) collective-permute-start(f32[16,128]{1,0:T(8,128)S(1)} %get-tuple-element.49), channel_id=1, source_target_pairs={{120,0},{16,8},{8,16},{32,24},{24,32},{48,40},{40,48},{64,56},{56,... | collective-permute-start | bytes 24584 | tf_op jit(solution)/shard_map/ppermute | solution.py:470
  9.1 1.0 %copy-start.1 = (bf16[1024,512]{1,0:T(8,128)(2,1)}, bf16[1024,512]{1,0:T(8,128)(2,1)S(1)}, u32[]{:S(2)}) copy-start(bf16[1024,512]{1,0:T(8,128)(2,1)S(1)} %get-tuple-element.62.low) | copy-start | bytes 3145732
  10.4 19.3 %copy-start.2 = (bf16[1024,512]{1,0:T(8,128)(2,1)S(1)}, bf16[1024,512]{1,0:T(8,128)(2,1)}, u32[]{:S(2)}) copy-start(bf16[1024,512]{1,0:T(8,128)(2,1)} %copy-done.1) | copy-start | bytes 3145732
  10.4 19.2 %copy-start.7 = (bf16[2,800]{1,0:T(2,128)(2,1)S(1)}, bf16[2,800]{1,0:T(2,128)(2,1)}, u32[]{:S(2)}) copy-start(bf16[2,800]{1,0:T(2,128)(2,1)} %w_head.1) | copy-start | bytes 9604
  10.4 9.6 %collective-permute-start.2 = (f32[8,640]{1,0:T(8,128)S(1)}, f32[8,640]{1,0:T(8,128)S(1)}, u32[]{:S(2)}, u32[]{:S(2)}) collective-permute-start(f32[8,640]{1,0:T(8,128)S(1)} %get-tuple-element.54), channel_id=1, source_target_pairs={{1,0},{9,8},{17,16},{25,24},{33,32},{41,40},{49,48},{57,56},{65,64... | collective-permute-start | bytes 61448 | tf_op jit(solution)/shard_map/ppermute | solution.py:470
  13.2 7.4 %collective-permute-start.3 = (f32[8,640]{1,0:T(8,128)S(1)}, f32[8,640]{1,0:T(8,128)S(1)}, u32[]{:S(2)}, u32[]{:S(2)}) collective-permute-start(f32[8,640]{1,0:T(8,128)S(1)} %get-tuple-element.55), channel_id=1, source_target_pairs={{7,0},{15,8},{23,16},{31,24},{39,32},{47,40},{55,48},{63,56},{71,6... | collective-permute-start | bytes 61448 | tf_op jit(solution)/shard_map/ppermute | solution.py:470
  20.0 19.8 %copy-start.17 = (bf16[128,32]{0,1:T(8,128)(2,1)S(1)}, bf16[128,32]{0,1:T(8,128)(2,1)}, u32[]{:S(2)}) copy-start(bf16[128,32]{0,1:T(8,128)(2,1)} %param.23) | copy-start | bytes 24580
  20.0 20.0 %copy-start = (bf16[128,1920]{1,0:T(8,128)(2,1)S(1)}, bf16[128,1920]{1,0:T(8,128)(2,1)}, u32[]{:S(2)}) copy-start(bf16[128,1920]{1,0:T(8,128)(2,1)} %ctx_w.1) | copy-start | bytes 1474564
  20.0 20.0 %copy-start.9 = (f32[128]{0:T(128)S(1)}, f32[128]{0:T(128)}, u32[]{:S(2)}) copy-start(f32[128]{0:T(128)} %param.24) | copy-start | bytes 1540
  23.0 1.7 %collective-permute-start.4 = (bf16[2,32,2048]{2,1,0:T(8,128)(2,1)}, bf16[2,32,2048]{2,1,0:T(8,128)(2,1)S(1)}, u32[]{:S(2)}, u32[]{:S(2)}) collective-permute-start(bf16[2,32,2048]{2,1,0:T(8,128)(2,1)} %get-tuple-element.59), channel_id=1, source_target_pairs={{8,0},{0,8},{24,16},{16,24},{40,32},{32,40},{56,48},{48,56},{72,64... | collective-permute-start | bytes 786440 | tf_op jit(solution)/shard_map/ppermute | solution.py:470
  25.4 9.6 %collective-permute-start.8 = (bf16[2,32,2048]{2,1,0:T(8,128)(2,1)}, bf16[2,32,2048]{2,1,0:T(8,128)(2,1)}, u32[]{:S(2)}, u32[]{:S(2)}) collective-permute-start(bf16[2,32,2048]{2,1,0:T(8,128)(2,1)} %slice_dynamic-update-slice_fusion.refs_0_), channel_id=1, source_target_pairs={{112,0},{24,8},{0,16},{40,24},{16,32},{56,40},{32,48},{72,56},{48,... | collective-permute-start | bytes 786440 | tf_op jit(solution)/shard_map/ppermute | solution.py:470
  25.5 14.4 %collective-permute-start.5 = (bf16[2,32,2048]{2,1,0:T(8,128)(2,1)}, bf16[2,32,2048]{2,1,0:T(8,128)(2,1)S(1)}, u32[]{:S(2)}, u32[]{:S(2)}) collective-permute-start(bf16[2,32,2048]{2,1,0:T(8,128)(2,1)} %slice_dynamic-update-slice_fusion.refs_0_), channel_id=1, source_target_pairs={{119,0},{25,8},{7,16},{41,24},{23,32},{57,40},{39,48},{73,56},{55,... | collective-permute-start | bytes 786440 | tf_op jit(solution)/shard_map/ppermute | solution.py:470
  25.5 17.9 %collective-permute-start.7 = (bf16[2,32,2048]{2,1,0:T(8,128)(2,1)}, bf16[2,32,2048]{2,1,0:T(8,128)(2,1)S(1)}, u32[]{:S(2)}, u32[]{:S(2)}) collective-permute-start(bf16[2,32,2048]{2,1,0:T(8,128)(2,1)} %slice_dynamic-update-slice_fusion.refs_0_), channel_id=1, source_target_pairs={{113,0},{31,8},{1,16},{47,24},{17,32},{63,40},{33,48},{79,56},{49,... | collective-permute-start | bytes 786440 | tf_op jit(solution)/shard_map/ppermute | solution.py:470
  29.7 20.6 %copy-start.6 = (bf16[32,128]{1,0:T(8,128)(2,1)S(1)}, bf16[32,128]{1,0:T(8,128)(2,1)}, u32[]{:S(2)}) copy-start(bf16[32,128]{1,0:T(8,128)(2,1)} %up_w.1) | copy-start | bytes 24580
  29.7 20.6 %copy-start.13 = (f32[32]{0:T(128)S(1)}, f32[32]{0:T(128)}, u32[]{:S(2)}) copy-start(f32[32]{0:T(128)} %param.27) | copy-start | bytes 388
  29.7 20.6 %copy-start.14 = (f32[2]{0:T(128)S(1)}, f32[2]{0:T(128)}, u32[]{:S(2)}) copy-start(f32[2]{0:T(128)} %head_b.1) | copy-start | bytes 28
  31.1 0.7 copy-start.3
  35.1 4.9 %collective-permute-start.9 = (bf16[2,32,2048]{2,1,0:T(8,128)(2,1)}, bf16[2,32,2048]{2,1,0:T(8,128)(2,1)}, u32[]{:S(2)}, u32[]{:S(2)}) collective-permute-start(bf16[2,32,2048]{2,1,0:T(8,128)(2,1)} %collective-permute-done.8.refs_1_), channel_id=1, source_target_pairs={{8,0},{0,8},{24,16},{16,24},{40,32},{32,40},{56,48},{48,56},{72,64... | collective-permute-start | bytes 786440 | tf_op jit(solution)/shard_map/ppermute | solution.py:470
  39.8 8.6 %collective-permute-start.6 = (bf16[2,32,2048]{2,1,0:T(8,128)(2,1)S(1)}, bf16[2,32,2048]{2,1,0:T(8,128)(2,1)S(1)}, u32[]{:S(2)}, u32[]{:S(2)}) collective-permute-start(bf16[2,32,2048]{2,1,0:T(8,128)(2,1)S(1)} %collective-permute-done.5.refs_3_), channel_id=1, source_target_pairs={{120,0},{16,8},{8,16},{32,24},{24,32},{48,40},{40,48},{64,56},{56,... | collective-permute-start | bytes 786440 | tf_op jit(solution)/shard_map/ppermute | solution.py:470
  39.9 10.4 %copy-start.4 = (bf16[160,640]{1,0:T(8,128)(2,1)S(1)}, bf16[160,640]{1,0:T(8,128)(2,1)}, u32[]{:S(2)}) copy-start(bf16[160,640]{1,0:T(8,128)(2,1)} %copy-done.3) | copy-start | bytes 614404
  39.9 8.9 %collective-permute-start.10 = (bf16[2,32,2048]{2,1,0:T(8,128)(2,1)S(1)}, bf16[2,32,2048]{2,1,0:T(8,128)(2,1)S(1)}, u32[]{:S(2)}, u32[]{:S(2)}) collective-permute-start(bf16[2,32,2048]{2,1,0:T(8,128)(2,1)S(1)} %collective-permute-done.5.refs_3_), channel_id=1, source_target_pairs={{8,0},{0,8},{24,16},{16,24},{40,32},{32,40},{56,48},{48,56},{72,64... | collective-permute-start | bytes 786440 | tf_op jit(solution)/shard_map/ppermute | solution.py:470
  48.4 1.5 %collective-permute-start.11 = (bf16[2,32,2048]{2,1,0:T(8,128)(2,1)S(1)}, bf16[2,32,2048]{2,1,0:T(8,128)(2,1)S(1)}, u32[]{:S(2)}, u32[]{:S(2)}) collective-permute-start(bf16[2,32,2048]{2,1,0:T(8,128)(2,1)S(1)} %collective-permute-done.7.two_m), channel_id=1, source_target_pairs={{8,0},{0,8},{24,16},{16,24},{40,32},{32,40},{56,48},{48,56},{72,64... | collective-permute-start | bytes 786440 | tf_op jit(solution)/shard_map/ppermute | solution.py:470
  48.4 1.9 %collective-permute-start.12 = (bf16[2,32,2048]{2,1,0:T(8,128)(2,1)S(1)}, bf16[2,32,2048]{2,1,0:T(8,128)(2,1)S(1)}, u32[]{:S(2)}, u32[]{:S(2)}) collective-permute-start(bf16[2,32,2048]{2,1,0:T(8,128)(2,1)S(1)} %collective-permute-done.6.relay), channel_id=1, source_target_pairs={{8,0},{0,8},{24,16},{16,24},{40,32},{32,40},{56,48},{48,56},{72,64... | collective-permute-start | bytes 786440 | tf_op jit(solution)/shard_map/ppermute | solution.py:470
  56.4 1.3 %collective-permute-start.13 = (f32[72,128]{1,0:T(8,128)S(1)}, f32[72,128]{1,0:T(8,128)S(1)}, u32[]{:S(2)}, u32[]{:S(2)}) collective-permute-start(f32[72,128]{1,0:T(8,128)S(1)} %get-tuple-element.75), channel_id=1, source_target_pairs={{8,0},{0,8},{24,16},{16,24},{40,32},{32,40},{56,48},{48,56},{72,64... | collective-permute-start | bytes 110600 | tf_op jit(solution)/shard_map/ppermute | solution.py:470
  56.6 5.5 %collective-permute-start.14 = (f32[72,128]{1,0:T(8,128)S(1)}, f32[72,128]{1,0:T(8,128)S(1)}, u32[]{:S(2)}, u32[]{:S(2)}) collective-permute-start(f32[72,128]{1,0:T(8,128)S(1)} %get-tuple-element.75), channel_id=1, source_target_pairs={{120,0},{16,8},{8,16},{32,24},{24,32},{48,40},{40,48},{64,56},{56,... | collective-permute-start | bytes 110600 | tf_op jit(solution)/shard_map/ppermute | solution.py:470
  62.1 5.3 %collective-permute-start.15 = (f32[8,512]{1,0:T(8,128)S(1)}, f32[8,512]{1,0:T(8,128)S(1)}, u32[]{:S(2)}, u32[]{:S(2)}) collective-permute-start(f32[8,512]{1,0:T(8,128)S(1)} %maximum_add_fusion), channel_id=1, source_target_pairs={{1,0},{9,8},{17,16},{25,24},{33,32},{41,40},{49,48},{57,56},{65,64... | collective-permute-start | bytes 49160 | tf_op jit(solution)/shard_map/ppermute | solution.py:470
  62.2 7.4 %collective-permute-start.16 = (f32[8,512]{1,0:T(8,128)S(1)}, f32[8,512]{1,0:T(8,128)S(1)}, u32[]{:S(2)}, u32[]{:S(2)}) collective-permute-start(f32[8,512]{1,0:T(8,128)S(1)} %maximum_add_fusion), channel_id=1, source_target_pairs={{7,0},{15,8},{23,16},{31,24},{39,32},{47,40},{55,48},{63,56},{71,6... | collective-permute-start | bytes 49160 | tf_op jit(solution)/shard_map/ppermute | solution.py:470

commit v4 on v3

--- a/solution.py
+++ b/solution.py
@@ -11,7 +11,7 @@
 CH, WIDE, KINDS = 32, 128, 8
 POOL_ROWS, POOL_COLS = 16, 128
 SPOTS = POOL_ROWS * POOL_COLS
-HALF = ROWS // 2
+FIRST = 16
 HBM = pl.BlockSpec(memory_space=pltpu.HBM)
 VMEM = pl.BlockSpec(memory_space=pltpu.VMEM)
 SMEM = pl.BlockSpec(memory_space=pltpu.SMEM)
@@ -115,13 +115,13 @@
 
 
 def inner_kernel(
-    half, stem_in, w_in, gain, b_in, conv_w, conv_b, features, sums, stem_w, wide_w, stem3
+    part, stem_in, w_in, gain, b_in, conv_w, conv_b, features, sums, stem_w, wide_w, stem3
 ):
     spread = jnp.where(iota((KINDS, 64), 1) // 8 == iota((KINDS, 64), 0), 1.0, 0.0).astype(BF16)
     same = iota((256, 64), 0) // CH == iota((256, 64), 1) % 8
     halves = []
-    for part in split(kinds_of(w_in, gain, b_in, 2)):
-        rows = mm(jnp.concatenate([part] * 8, axis=0), spread)
+    for piece in split(kinds_of(w_in, gain, b_in, 2)):
+        rows = mm(jnp.concatenate([piece] * 8, axis=0), spread)
         halves.append(jnp.where(same, rows, 0.0))
     stem_w[...] = jnp.concatenate(halves, axis=1).astype(BF16)
     wide_w[...] = jnp.zeros(wide_w.shape, BF16)
@@ -132,9 +132,10 @@
     bias = jnp.broadcast_to(column(conv_b[...]), (CH, COLS))
     bias = jnp.concatenate([bias] * 8, axis=0)
 
-    blocks = range(5) if half == 0 else range(3, 8)
-    base = half * HALF - 1
-    edge = 0 if half == 0 else HALF + 1
+    start, count = (0, FIRST) if part == 0 else (FIRST, ROWS - FIRST)
+    blocks = range(max(start // 8 - 1, 0), min((start + count) // 8 + 1, ROWS // 8))
+    base = start - 1
+    edge = 0 if part == 0 else count + 1
     stem3[edge * 96 : (edge + 1) * 96, :] = jnp.zeros((96, COLS), BF16)
     for block in blocks:
         y = block * 8
@@ -142,22 +143,22 @@
         out = jnp.maximum(mm(stem_w[...], jnp.concatenate([x, x], axis=0)), 0.0)
         for r in range(8):
             at = y + r - base
-            if at < 0 or at > HALF + 1:
+            if at < 0 or at > count + 1:
                 continue
             s = out[r * CH : (r + 1) * CH, :]
             parts = [pltpu.roll(s, 1, 1), s, pltpu.roll(s, COLS - 1, 1)]
             stem3[at * 96 : (at + 1) * 96, :] = jnp.concatenate(parts, axis=0).astype(BF16)
 
-    for block in range(HALF // 8):
+    for block in range(count // 8):
         out = mm(wide_w[...], stem3[block * 768 : block * 768 + 960, :])
         value = jnp.maximum(out + bias, 0.0).astype(BF16)
         features[block * 256 : (block + 1) * 256, :] = value
         means = mm(value, pool_w)
         for p in range(2):
             rows = [means[p * 128 + r * 32 : p * 128 + (r + 1) * 32, :] for r in range(4)]
-            if half == 0 and block == 0 and p == 0:
+            if part == 0 and block == 0 and p == 0:
                 rows = rows[1:]
-            if half == 1 and block == HALF // 8 - 1 and p == 1:
+            if part == 1 and block == count // 8 - 1 and p == 1:
                 rows = rows[:3]
             at = (block * 2 + p) * POOL_COLS
             sums[:, at : at + POOL_COLS] = sum(rows[1:], rows[0])
@@ -165,7 +166,7 @@
 
 def rim_kernel(
     cells, rows, cols, partner, outer, even_message, odd_message, sums_low, sums_high,
-    w_in, gain, b_in, conv_w, conv_b, rim_rows, rim_cols, pooled,
+    w_in, gain, b_in, conv_w, conv_b, rim_rows, rim_cols, pooled, own,
 ):
     has_above, has_below, has_left, has_right = flags(*cells)
     left, right = sides(partner, outer, slice(0, 8), slice(8, 16))
@@ -229,16 +230,17 @@
     lane = iota((CH, POOL_COLS), 1)
     for p in range(POOL_ROWS):
         at = p * POOL_COLS
-        near = sums_low if p < POOL_ROWS // 2 else sums_high
-        first = at % (SPOTS // 2)
+        near = sums_low if p < FIRST // 4 else sums_high
+        first = at if p < FIRST // 4 else at - FIRST // 4 * POOL_COLS
         last = jnp.where(lane == POOL_COLS - 1, col_sums[:, 16 + p : 17 + p], 0.0)
         total = near[:, first : first + POOL_COLS] + jnp.where(lane == 0, col_sums[:, p : p + 1], last)
         if p == 0:
             total += row_sums[0]
         if p == POOL_ROWS - 1:
             total += row_sums[1]
-        pooled[0, :, at : at + POOL_COLS] = total.astype(BF16)
-    pooled[1, :, :] = jnp.zeros((CH, SPOTS), BF16)
+        pooled[:, at : at + POOL_COLS] = total.astype(BF16)
+        own[0, :, at : at + POOL_COLS] = total.astype(BF16)
+    own[1, :, :] = jnp.zeros((CH, SPOTS), BF16)
 
 
 def head_weights(w_head, row_y, row_count, col_y, col_count):
@@ -257,38 +259,13 @@
     return total.astype(BF16)
 
 
-def merge_kernel(low, high, rim_rows, rim_cols, w_head, features, head_w, rim_w):
-    head_w[...] = head_weights(w_head[...], lambda r: r, 16, lambda r: r - 2, 20)
-    outside = lambda r: jnp.where(r < 2, r - 2, ROWS - 2 + r)
-    rim_w[...] = head_weights(w_head[...], outside, 4, lambda r: jnp.where(r < 2, r, ROWS - 4 + r), 4)
-    lane = iota((CH, 128), 1)
-    columns = rim_cols[...].astype(F32)
-    for y in range(ROWS):
-        if y == 0:
-            f = rim_rows[0:CH, :]
-        elif y == ROWS - 1:
-            f = rim_rows[CH : 2 * CH, :]
-        else:
-            source = low if y < HALF else high
-            at = y % HALF * CH
-            f = source[at : at + CH, :]
-        f = f.astype(F32)
-        first = jnp.where(lane == 0, columns[:, y : y + 1], f[:, :128])
-        last = jnp.where(lane == 127, columns[:, 128 + y : 129 + y], f[:, COLS - 128 :])
-        f = jnp.concatenate([first, f[:, 128 : COLS - 128], last], axis=1)
-        features[y * CH : (y + 1) * CH, :] = f.astype(BF16)
-
-
 MAPS = {
     (0, -2): ("band", 0), (0, -1): ("band", 1), (0, 0): ("own", 0), (0, 1): ("own", 1), (0, 2): ("band_p", 1),
     (-1, -2): ("one", 0), (-1, -1): ("one", 1), (-1, 0): ("relay_p", 0), (-1, 1): ("relay_p", 1), (-1, 2): ("two_p", 1),
     (1, -2): ("two", 0), (1, -1): ("two", 1), (1, 0): ("relay", 1), (1, 1): ("relay", 0), (1, 2): ("one_p", 1),
 }
-NAMES = ("own", "band", "band_p", "one", "one_p", "two", "two_p", "relay", "relay_p")
-
-
-EARLY = [at for at in range(15) if MAPS[(at // 5 - 1, at % 5 - 2)][0] in NAMES[:4]]
-LATE = [at for at in range(15) if at not in EARLY]
+PHASES = (("own", "one", "one_p", "band"), ("two", "two_p", "relay", "relay_p", "band_p"))
+TILES = [[at for at in range(15) if MAPS[(at // 5 - 1, at % 5 - 2)][0] in names] for names in PHASES]
 
 
 def context_sum(cells, which, arrays, proj_w, proj_b, ctx_w, weights, proj, finish):
@@ -304,12 +281,13 @@
         chosen = jnp.where(core == 0, one, two)
         weights[:, k * WIDE : (k + 1) * WIDE] = jnp.where(inside, chosen, jnp.zeros_like(chosen))
     p_bias = jnp.broadcast_to(column(proj_b[...]), (WIDE, 256))
+    proj_w = jnp.transpose(proj_w[...].astype(F32)).astype(BF16)
 
     def part(at, carry):
         spots = pl.ds(pl.multiple_of(at * 256, 256), 256)
         for k, tile in enumerate(which):
             name, half = MAPS[(tile // 5 - 1, tile % 5 - 2)]
-            out = mm(proj_w[...], arrays[name][half, :, spots])
+            out = mm(proj_w, arrays[name][half, :, spots])
             proj[k * WIDE : (k + 1) * WIDE, :] = jnp.maximum(out + p_bias, 0.0).astype(BF16)
         finish(at, spots, mm(weights[...], proj[...]))
         return carry
@@ -318,27 +296,31 @@
 
 
 def early_kernel(cells, *refs):
-    arrays = dict(zip(NAMES[:4], refs[:4]))
-    proj_w, proj_b, ctx_w, context, weights, proj = refs[4:]
-    own = EARLY.index(7)
+    count = len(PHASES[0])
+    arrays = dict(zip(PHASES[0], refs[:count]))
+    proj_w, proj_b, ctx_w, w_head, up_b, context, head_w, rim_w, up_bias, weights, proj = refs[count:]
+    up_bias[...] = jnp.broadcast_to(column(up_b[...]), (CH, 256))
+    head_w[...] = head_weights(w_head[...], lambda r: r, 16, lambda r: r - 2, 20)
+    outside = lambda r: jnp.where(r < 2, r - 2, ROWS - 2 + r)
+    rim_w[...] = head_weights(w_head[...], outside, 4, lambda r: jnp.where(r < 2, r, ROWS - 4 + r), 4)
+    own = TILES[0].index(7)
 
     def finish(at, spots, total):
         context[:, spots] = total + proj[own * WIDE : (own + 1) * WIDE, :].astype(F32)
 
-    context_sum(cells, EARLY, arrays, proj_w, proj_b, ctx_w, weights, proj, finish)
+    context_sum(cells, TILES[0], arrays, proj_w, proj_b, ctx_w, weights, proj, finish)
 
 
 def logits_kernel(
-    cells, features, context, one_p, two_m, two_p, relay, relay_p,
+    cells, low, high, rim_rows, rim_cols, context, two, two_p, relay, relay_p, band_p,
     proj_w, proj_b, ctx_w, up_w, up_b, head_w, rim_w, head_b,
     logits, col_out, row_out, weights, proj, low_up, lifted, decoded,
 ):
-    arrays = dict(zip(NAMES[4:], (one_p, two_m, two_p, relay, relay_p)))
-    u_bias = jnp.broadcast_to(column(up_b[...]), (CH, 256))
+    arrays = dict(zip(PHASES[1], (two, two_p, relay, relay_p, band_p)))
 
     def finish(part, spots, total):
         mixed = jnp.maximum(total + context[:, spots], 0.0).astype(BF16)
-        up = mm(up_w[...], mixed) + u_bias
+        up = mm(up_w[...], mixed) + up_b[...]
         high, low = split(up)
         both = [
             jnp.concatenate([high[:, h * 128 : (h + 1) * 128], low[:, h * 128 : (h + 1) * 128]], axis=1)
@@ -346,7 +328,7 @@
         ]
         low_up[pl.ds(pl.multiple_of(part * 64, 64), 64), :] = jnp.concatenate(both, axis=0)
 
-    context_sum(cells, LATE, arrays, proj_w, proj_b, ctx_w, weights, proj, finish)
+    context_sum(cells, TILES[1], arrays, proj_w, proj_b, ctx_w, weights, proj, finish)
 
     widen = jnp.where(
         iota((256, COLS), 0) % 128 == iota((256, COLS), 1) // 4, 1.0, 0.0
@@ -356,15 +338,22 @@
     decoded[0:64, :] = jnp.zeros((64, COLS), BF16)
     decoded[66 * CH :, :] = jnp.zeros((64, COLS), BF16)
 
-    def decode(p, carry):
-        up = lifted[pl.ds(pl.multiple_of(p * CH, CH), CH), :]
-        for r in range(4):
-            at = pl.multiple_of((4 * p + r) * CH, CH)
-            value = jnp.maximum(features[pl.ds(at, CH), :].astype(F32) + up, 0.0).astype(BF16)
-            decoded[pl.ds(pl.multiple_of(at + 64, CH), CH), :] = value
-        return carry
-
-    lax.fori_loop(0, POOL_ROWS, decode, 0, unroll=4)
+    lane = iota((CH, 128), 1)
+    columns = rim_cols[...].astype(F32)
+    for y in range(ROWS):
+        if y == 0:
+            f = rim_rows[0:CH, :]
+        elif y == ROWS - 1:
+            f = rim_rows[CH : 2 * CH, :]
+        else:
+            at = (y if y < FIRST else y - FIRST) * CH
+            f = (low if y < FIRST else high)[at : at + CH, :]
+        f = f.astype(F32)
+        first = jnp.where(lane == 0, columns[:, y : y + 1], f[:, :128])
+        last = jnp.where(lane == 127, columns[:, 128 + y : 129 + y], f[:, COLS - 128 :])
+        f = jnp.concatenate([first, f[:, 128 : COLS - 128], last], axis=1)
+        value = f + lifted[y // 4 * CH : (y // 4 + 1) * CH, :]
+        decoded[(y + 2) * CH : (y + 3) * CH, :] = jnp.maximum(value, 0.0).astype(BF16)
 
     def gather_taps(z, count):
         total = None
@@ -488,22 +477,23 @@
         halo_kernel,
         [shape_of(32, COLS), shape_of(32, 128), shape_of(16, 128), shape_of(8 * ROWS, COLS, dtype=BF16)],
         [rasters, aerial],
-        flops=2 * 10**10,
+        flops=8 * 10**10,
     )
     near, far = partner(message), outer(message)
 
     stem_args = [w_in.T, aerial_gain[None, :], b_in[None, :], w_conv1, b_conv1[None, :]]
-    proj_args = [w_proj, b_proj[None, :], w_ctx]
-
-    def inner(half, stem_in):
+    proj_args = [w_proj.T, b_proj[None, :], w_ctx]
+
+    def inner(part, stem_in):
+        count = FIRST if part == 0 else ROWS - FIRST
         return call(
-            functools.partial(inner_kernel, half),
-            [shape_of(HALF * CH, COLS, dtype=BF16), shape_of(CH, SPOTS // 2)],
+            functools.partial(inner_kernel, part),
+            [shape_of(count * CH, COLS, dtype=BF16), shape_of(CH, count // 4 * POOL_COLS)],
             [stem_in, *stem_args],
             [
                 pltpu.VMEM((256, 128), BF16),
                 pltpu.VMEM((256, 960), BF16),
-                pltpu.VMEM(((HALF + 2) * 96, COLS), BF16),
+                pltpu.VMEM(((count + 2) * 96, COLS), BF16),
             ],
             flops=4 * 10**9,
         )
@@ -515,47 +505,51 @@
     even_in, odd_in = even_pair(even_out), odd_pair(odd_out)
     feat_high, sums_high = inner(1, stem_in)
 
-    rim_rows, rim_cols, own = call(
+    rim_rows, rim_cols, pooled, own = call(
         functools.partial(rim_kernel, cells),
-        [shape_of(2 * CH, COLS, dtype=BF16), shape_of(CH, 256, dtype=BF16), shape_of(2, CH, SPOTS, dtype=BF16)],
+        [
+            shape_of(2 * CH, COLS, dtype=BF16), shape_of(CH, 256, dtype=BF16), shape_of(CH, SPOTS, dtype=BF16),
+            shape_of(2, CH, SPOTS, dtype=BF16),
+        ],
         [rows, cols, near, far, even_in, odd_in, sums_low, sums_high, *stem_args],
     )
 
-    own = own.at[1].set(partner(own)[0])
-    own, rim_rows = tie((own, rim_rows))
-    one = beside(own, -1)
-    band = beside(own, 0)
-    two = beside(own, 1)
-    features, head_w, rim_w = call(
-        merge_kernel,
-        [shape_of(ROWS * CH, COLS, dtype=BF16), shape_of(160, 20 * CH, dtype=BF16), shape_of(40, 4 * CH, dtype=BF16)],
-        [feat_low, feat_high, rim_rows, rim_cols, w_head],
-    )
-    one, features = tie((one, features))
-    relay = outer(one)
-    band_p, one_p = partner(band), partner(one)
-    context = call(
-        functools.partial(early_kernel, cells), shape_of(WIDE, SPOTS), [own, band, band_p, one, *proj_args],
-        [pltpu.VMEM((WIDE, len(EARLY) * WIDE), BF16), pltpu.VMEM((len(EARLY) * WIDE, 256), BF16)],
+    own = own.at[1].set(partner(pooled))
+    one, band = beside(own, -1), beside(own, 0)
+    own, one = tie((own, one))
+    relay, two = outer(one), beside(own, 1)
+    sent = dict(own=own, one=one, band=band, one_p=partner(one))
+
+    def context_call(kernel, phase, outs, args, scratch=(), **more):
+        count = len(TILES[phase]) * WIDE
+        buffers = [pltpu.VMEM((WIDE, count), BF16), pltpu.VMEM((count, 256), BF16)]
+        return call(functools.partial(kernel, cells), outs, args, buffers + list(scratch), **more)
+
+    context, head_w, rim_w, up_bias = context_call(
+        early_kernel, 0,
+        [
+            shape_of(WIDE, SPOTS), shape_of(160, 20 * CH, dtype=BF16), shape_of(40, 4 * CH, dtype=BF16),
+            shape_of(CH, 256),
+        ],
+        [*(sent[name] for name in PHASES[0]), *proj_args, w_head, b_up[None, :]],
     )
     relay, two, context = tie((relay, two, context))
-    two_p, relay_p = partner(two), partner(relay)
-
-    inner_logits, col_out, row_out = call(
-        functools.partial(logits_kernel, cells),
+    relay_p, two_p = partner(relay), partner(two)
+    band_p = partner(band)
+
+    inner_logits, col_out, row_out = context_call(
+        logits_kernel, 1,
         [shape_of(2, ROWS, COLS), shape_of(ROWS + 8, 128), shape_of(8, COLS)],
         [
-            features, context, one_p, two, two_p, relay, relay_p,
-            *proj_args, w_up, b_up[None, :], head_w, rim_w, b_head,
+            feat_low, feat_high, rim_rows, rim_cols, context, two, two_p, relay, relay_p, band_p,
+            *proj_args, w_up, up_bias, head_w, rim_w, b_head,
         ],
         [
-            pltpu.VMEM((WIDE, len(LATE) * WIDE), BF16),
-            pltpu.VMEM((len(LATE) * WIDE, 256), BF16),
             pltpu.VMEM((POOL_ROWS * CH, 256), BF16),
             pltpu.VMEM((POOL_ROWS * CH, COLS), F32),
             pltpu.VMEM(((ROWS + 4) * CH, COLS), BF16),
         ],
-        smem=(14,),
+        smem=(18,),
     )
     near, far = partner(col_out), outer(col_out)
     row_out = row_sums(cells, row_out, near, far)

time: 70.6 us -> 69.2 us (0.980)
  waiting for transfers between devices: 24.7 us -> 29.6 us
  Pallas kernels: 19.4 us -> 16.3 us
  local copies, waits for them, and re-layouts: 4.49 us -> 2.09 us
  starting transfers between devices: 21.2 us -> 20.4 us
    ppermute x17, waiting for transfers between devices: 24.7 us -> 29.6 us  [moved(): return lax.ppermute(x, ('band', 'cross'), route)]
    pallas_call x8 -> x7, Pallas kernels: 19.4 us -> 16.3 us  [call(): pl.pallas_call(fetching if hbm else kernel, out_shape=outs, in_specs=[SME...]
    unnamed x37 -> x28, local copies, waits for them, and re-layouts: 3.82 us -> 2.07 us
    ppermute x17, starting transfers between devices: 21.2 us -> 20.4 us  [moved(): return lax.ppermute(x, ('band', 'cross'), route)]
  transfers between devices with their start and end apart: 17 -> 17, of which waited for: 11 -> 8; matrix products, arithmetic and copies ran while one was open for 0% -> 0% of each run, Pallas kernels for 14% -> 12%
where the time goes in v4:
time: 69.2 us; the launch traced here: 69 us
  waiting for transfers between devices  29.6 us (43%)
  starting transfers between devices  20.4 us (29%)
  Pallas kernels  16.3 us (24%)
  local copies, waits for them, and re-layouts  2.09 us (3%)
    ppermute x17, waiting for transfers between devices, moved(): return lax.ppermute(x, ('band', 'cross'), route)  29.6 us
    ppermute x17, starting transfers between devices, moved(): return lax.ppermute(x, ('band', 'cross'), route)  20.4 us
    pallas_call x7, Pallas kernels, call(): pl.pallas_call(fetching if hbm else kernel, out_shape=outs, in_specs=[SME...  16.3 us
    unnamed x28, local copies, waits for them, and re-layouts  2.07 us
  transfers between devices with their start and end apart: 17, of which 8 were waited for; matrix products, arithmetic and copies ran while one was open for 0% of the time, Pallas kernels for 12%

profile of v4, /device:TPU:0, one launch (start us, length us, event | category | flops | bytes accessed | tf_op | source)
XLA Modules:
  0.0 69.0 jit_solution(10768054517200324147)
XLA Ops:
  0.0 1.1 %copy-done.12 = s32[4,64,512]{2,1,0:T(8,128)S(1)} copy-done((s32[4,64,512]{2,1,0:T(8,128)S(1)}, s32[4,64,512]{2,1,0:T(8,128)}, u32[]{:S(2)}) %copy-start.12) | copy-done | bytes 524312
  1.1 0.9 %copy-done.13 = f32[64,512]{1,0:T(8,128)S(1)} copy-done((f32[64,512]{1,0:T(8,128)S(1)}, f32[64,512]{1,0:T(8,128)}, u32[]{:S(2)}) %copy-start.13) | copy-done | bytes 131096
  2.0 0.3 shard_map.136
  2.3 0.1 collective-permute-start
  2.4 4.1 %collective-permute-start.1 = (f32[16,128]{1,0:T(8,128)S(1)}, f32[16,128]{1,0:T(8,128)S(1)}, u32[]{:S(2)}, u32[]{:S(2)}) collective-permute-start(f32[16,128]{1,0:T(8,128)S(1)} %get-tuple-element.50), channel_id=1, source_target_pairs={{120,0},{16,8},{8,16},{32,24},{24,32},{48,40},{40,48},{64,56},{56,... | collective-permute-start | bytes 24584 | tf_op jit(solution)/shard_map/ppermute | solution.py:459
  6.6 1.5 %shard_map.137 = (bf16[512,512]{1,0:T(8,128)(2,1)S(1)}, f32[32,512]{1,0:T(8,128)S(1)}) custom-call(bf16[512,512]{1,0:T(8,128)(2,1)S(1)} %get-tuple-element.54.stem_in, f32[4,32]{1,0:T(4,128)S(1)} %bitcast.11, f32[1,32]{1,0:T(1,128)S(1)} %bitcast.16, f32[1,32]{1,0:T(1,128)S(1)} %bitcast.19, bf16[32,288]{1,0:T(8,128)(2,1)S(1)} %copy-done.2, f32[1,32]{1,0:T(1,128)S(1)} %bitcast.22), custom_call_target="tpu_custom_call" | custom-call | flops 4000000000 | bytes 1048576 | tf_op jit(solution)/shard_map/pallas_call | solution.py:435
  8.1 0.0 collective-permute-done.partner
  8.1 0.0 collective-permute-done.1.outer
  8.2 0.2 multiply_reduce_fusion.2
  8.4 0.1 select_select_fusion.1
  8.5 0.0 copy-start
  8.5 0.0 copy-start.1
  8.5 0.0 copy-start.4
  8.5 0.0 copy-start.6
  8.5 0.0 copy-start.10
  8.5 2.8 %collective-permute-start.2 = (f32[8,640]{1,0:T(8,128)S(1)}, f32[8,640]{1,0:T(8,128)S(1)}, u32[]{:S(2)}, u32[]{:S(2)}) collective-permute-start(f32[8,640]{1,0:T(8,128)S(1)} %get-tuple-element.57), channel_id=1, source_target_pairs={{1,0},{9,8},{17,16},{25,24},{33,32},{41,40},{49,48},{57,56},{65,64... | collective-permute-start | bytes 61448 | tf_op jit(solution)/shard_map/ppermute | solution.py:459
  11.3 4.3 %collective-permute-start.3 = (f32[8,640]{1,0:T(8,128)S(1)}, f32[8,640]{1,0:T(8,128)S(1)}, u32[]{:S(2)}, u32[]{:S(2)}) collective-permute-start(f32[8,640]{1,0:T(8,128)S(1)} %get-tuple-element.58), channel_id=1, source_target_pairs={{7,0},{15,8},{23,16},{31,24},{39,32},{47,40},{55,48},{63,56},{71,6... | collective-permute-start | bytes 61448 | tf_op jit(solution)/shard_map/ppermute | solution.py:459
  15.6 3.6 %shard_map.138 = (bf16[1536,512]{1,0:T(8,128)(2,1)S(1)}, f32[32,1536]{1,0:T(8,128)S(1)}) custom-call(bf16[512,512]{1,0:T(8,128)(2,1)S(1)} %get-tuple-element.54.stem_in, f32[4,32]{1,0:T(4,128)S(1)} %bitcast.12, f32[1,32]{1,0:T(1,128)S(1)} %bitcast.17, f32[1,32]{1,0:T(1,128)S(1)} %bitcast.20, bf16[32,288]{1,0:T(8,128)(2,1)S(1)} %copy-done.2, f32[1,32]{1,0:T(1,128)S(1)} %bitcast.23), custom_call_target="tpu_custom_call" | custom-call | flops 4000000000 | bytes 1048576 | tf_op jit(solution)/shard_map/pallas_call | solution.py:435
  19.2 0.0 copy-start.3
  19.2 0.0 copy-start.11
  19.2 0.0 collective-permute-done.2.even_message
  19.3 0.0 collective-permute-done.3.odd_message
  19.3 1.7 %shard_map.139 = (bf16[64,512]{1,0:T(8,128)(2,1)S(1)}, bf16[32,256]{1,0:T(8,128)(2,1)S(1)}, bf16[32,2048]{1,0:T(8,128)(2,1)S(1)}, bf16[2,32,2048]{2,1,0:T(8,128)(2,1)S(1)}) custom-call(f32[32,512]{1,0:T(8,128)S(1)} %get-tuple-element.49.rows, f32[32,128]{1,0:T(8,128)S(1)} %get-tuple-element.56.cols, f32[16,128]{1,0:T(8,128)S(1)} %collective-permute-done.partner, ...), custom_call_target="tpu_custom_call" | custom-call | bytes 1048576 | tf_op jit(solution)/shard_map/pallas_call | solution.py:435
  21.0 0.1 collective-permute-start.4
  21.1 1.3 %collective-permute-done.4 = bf16[32,2048]{1,0:T(8,128)(2,1)S(1)} collective-permute-done((bf16[32,2048]{1,0:T(8,128)(2,1)S(1)}, bf16[32,2048]{1,0:T(8,128)(2,1)S(1)}, u32[]{:S(2)}, u32[]{:S(2)}) %collective-permute-start.4) | collective-permute-done | bytes 131104 | tf_op jit(solution)/shard_map/ppermute | solution.py:459
  22.4 0.1 collective-permute-start.5
  22.5 0.2 collective-permute-start.9
  22.7 13.6 %collective-permute-done.5.refs_1_ = bf16[2,32,2048]{2,1,0:T(8,128)(2,1)S(1)} collective-permute-done((bf16[2,32,2048]{2,1,0:T(8,128)(2,1)S(1)}, bf16[2,32,2048]{2,1,0:T(8,128)(2,1)S(1)}, u32[]{:S(2)}, u32[]{:S(2)}) %collective-permute-start.5) | collective-permute-done | bytes 262176 | tf_op jit(solution)/shard_map/ppermute | solution.py:459
  36.3 0.0 collective-permute-start.8
  36.3 1.7 %collective-permute-start.7 = (bf16[2,32,2048]{2,1,0:T(8,128)(2,1)S(1)}, bf16[2,32,2048]{2,1,0:T(8,128)(2,1)S(1)}, u32[]{:S(2)}, u32[]{:S(2)}) collective-permute-start(bf16[2,32,2048]{2,1,0:T(8,128)(2,1)S(1)} %bitcast_dynamic-update-slice_fusion.refs_0_), channel_id=1, source_target_pairs={{113,0},{31,8},{1,16},{47,24},{17,32},{63,40},{33,48},{79,56},{49,... | collective-permute-start | bytes 786440 | tf_op jit(solution)/shard_map/ppermute | solution.py:459
  38.0 0.0 collective-permute-done.9.refs_3_
  38.0 0.0 collective-permute-start.12
  38.0 0.0 collective-permute-done.8.refs_2_
  38.1 3.3 %shard_map.140 = (f32[128,2048]{1,0:T(8,128)S(1)}, bf16[160,640]{1,0:T(8,128)(2,1)S(1)}, bf16[40,128]{1,0:T(8,128)(2,1)S(1)}, f32[32,256]{1,0:T(8,128)S(1)}) custom-call(bf16[2,32,2048]{2,1,0:T(8,128)(2,1)S(1)} %bitcast_dynamic-update-slice_fusion.refs_0_, bf16[2,32,2048]{2,1,0:T(8,128)(2,1)S(1)} %collective-permute-done.5.refs_1_, ...), custom_call_target="tpu_custom_call" | custom-call | bytes 1048576 | tf_op jit(solution)/shard_map/pallas_call | solution.py:435
  41.4 6.6 %collective-permute-done.6.relay = bf16[2,32,2048]{2,1,0:T(8,128)(2,1)S(1)} collective-permute-done((bf16[2,32,2048]{2,1,0:T(8,128)(2,1)S(1)}, bf16[2,32,2048]{2,1,0:T(8,128)(2,1)S(1)}, u32[]{:S(2)}, u32[]{:S(2)}) %collective-permute-start.6) | collective-permute-done | bytes 262176 | tf_op jit(solution)/shard_map/ppermute | solution.py:459
  47.9 0.5 collective-permute-start.11
  48.4 0.0 collective-permute-done.12.band_p
  48.4 1.0 %collective-permute-done.10.two_p = bf16[2,32,2048]{2,1,0:T(8,128)(2,1)S(1)} collective-permute-done((bf16[2,32,2048]{2,1,0:T(8,128)(2,1)S(1)}, bf16[2,32,2048]{2,1,0:T(8,128)(2,1)S(1)}, u32[]{:S(2)}, u32[]{:S(2)}) %collective-permute-start.10) | collective-permute-done | bytes 262176 | tf_op jit(solution)/shard_map/ppermute | solution.py:459
  49.5 0.4 collective-permute-done.11.relay_p
  49.9 5.1 %shard_map.141 = (f32[2,64,512]{2,1,0:T(8,128)S(1)}, f32[72,128]{1,0:T(8,128)S(1)}, f32[8,512]{1,0:T(8,128)S(1)}) custom-call(bf16[512,512]{1,0:T(8,128)(2,1)S(1)} %get-tuple-element.48.low, bf16[1536,512]{1,0:T(8,128)(2,1)S(1)} %get-tuple-element.55.high, bf16[64,512]{1,0:T(8,128)(2,1)S(1)} %get-tuple-element.61.rim_rows, ...), custom_call_target="tpu_custom_call" | custom-call | bytes 1048576 | tf_op jit(solution)/shard_map/pallas_call | solution.py:435
  55.0 0.2 collective-permute-start.13
  55.2 1.9 %collective-permute-start.14 = (f32[72,128]{1,0:T(8,128)S(1)}, f32[72,128]{1,0:T(8,128)S(1)}, u32[]{:S(2)}, u32[]{:S(2)}) collective-permute-start(f32[72,128]{1,0:T(8,128)S(1)} %get-tuple-element.75), channel_id=1, source_target_pairs={{120,0},{16,8},{8,16},{32,24},{24,32},{48,40},{40,48},{64,56},{56,... | collective-permute-start | bytes 110600 | tf_op jit(solution)/shard_map/ppermute | solution.py:459
  57.1 3.6 %collective-permute-done.14.outer = f32[72,128]{1,0:T(8,128)S(1)} collective-permute-done((f32[72,128]{1,0:T(8,128)S(1)}, f32[72,128]{1,0:T(8,128)S(1)}, u32[]{:S(2)}, u32[]{:S(2)}) %collective-permute-start.14) | collective-permute-done | bytes 36896 | tf_op jit(solution)/shard_map/ppermute | solution.py:459
  60.7 0.1 collective-permute-start.15
  60.8 4.3 %collective-permute-start.16 = (f32[8,512]{1,0:T(8,128)S(1)}, f32[8,512]{1,0:T(8,128)S(1)}, u32[]{:S(2)}, u32[]{:S(2)}) collective-permute-start(f32[8,512]{1,0:T(8,128)S(1)} %maximum_add_fusion), channel_id=1, source_target_pairs={{7,0},{15,8},{23,16},{31,24},{39,32},{47,40},{55,48},{63,56},{71,6... | collective-permute-start | bytes 49160 | tf_op jit(solution)/shard_map/ppermute | solution.py:459
  65.1 0.9 %collective-permute-done.15.even_message = f32[8,512]{1,0:T(8,128)S(1)} collective-permute-done((f32[8,512]{1,0:T(8,128)S(1)}, f32[8,512]{1,0:T(8,128)S(1)}, u32[]{:S(2)}, u32[]{:S(2)}) %collective-permute-start.15) | collective-permute-done | bytes 16416 | tf_op jit(solution)/shard_map/ppermute | solution.py:459
  66.0 2.2 %collective-permute-done.16.odd_message = f32[8,512]{1,0:T(8,128)S(1)} collective-permute-done((f32[8,512]{1,0:T(8,128)S(1)}, f32[8,512]{1,0:T(8,128)S(1)}, u32[]{:S(2)}, u32[]{:S(2)}) %collective-permute-start.16) | collective-permute-done | bytes 16416 | tf_op jit(solution)/shard_map/ppermute | solution.py:459
  68.2 0.8 %shard_map.142 = f32[2,64,512]{2,1,0:T(8,128)} custom-call(f32[2,64,512]{2,1,0:T(8,128)S(1)} %get-tuple-element.74.inner, f32[72,128]{1,0:T(8,128)S(1)} %collective-permute-done.13.partner, f32[72,128]{1,0:T(8,128)S(1)} %collective-permute-done.14.outer, f32[8,512]{1,0:T(8,128)S(1)} %collective-permute-done.15.even_message, ...), custom_call_target="tpu_custom_call" | custom-call | bytes 1048576 | tf_op jit(solution)/shard_map/pallas_call | solution.py:435
  (33 shorter events, 0.1 us)
Async XLA Ops:
  0.0 6.5 %copy-start.5 = (f32[32,4]{0,1:T(4,128)S(1)}, f32[32,4]{0,1:T(4,128)}, u32[]{:S(2)}) copy-start(f32[32,4]{0,1:T(4,128)} %param.18) | copy-start | bytes 1540
  0.0 6.5 %copy-start.7 = (f32[32]{0:T(128)S(1)}, f32[32]{0:T(128)}, u32[]{:S(2)}) copy-start(f32[32]{0:T(128)} %param.19) | copy-start | bytes 388
  0.0 6.5 %copy-start.8 = (f32[32]{0:T(128)S(1)}, f32[32]{0:T(128)}, u32[]{:S(2)}) copy-start(f32[32]{0:T(128)} %param.20) | copy-start | bytes 388
  0.0 6.5 %copy-start.9 = (f32[32]{0:T(128)S(1)}, f32[32]{0:T(128)}, u32[]{:S(2)}) copy-start(f32[32]{0:T(128)} %param.22) | copy-start | bytes 388
  0.0 6.5 %copy-start.2 = (bf16[32,288]{1,0:T(8,128)(2,1)S(1)}, bf16[32,288]{1,0:T(8,128)(2,1)}, u32[]{:S(2)}) copy-start(bf16[32,288]{1,0:T(8,128)(2,1)} %conv_w.5) | copy-start | bytes 55300
  0.0 1.1 %copy-start.12 = (s32[4,64,512]{2,1,0:T(8,128)S(1)}, s32[4,64,512]{2,1,0:T(8,128)}, u32[]{:S(2)}) copy-start(s32[4,64,512]{2,1,0:T(8,128)} %rasters.1) | copy-start | bytes 1572868
  1.1 0.9 %copy-start.13 = (f32[64,512]{1,0:T(8,128)S(1)}, f32[64,512]{1,0:T(8,128)}, u32[]{:S(2)}) copy-start(f32[64,512]{1,0:T(8,128)} %aerial.1) | copy-start | bytes 393220
  2.3 5.8 %collective-permute-start = (f32[16,128]{1,0:T(8,128)S(1)}, f32[16,128]{1,0:T(8,128)S(1)}, u32[]{:S(2)}, u32[]{:S(2)}) collective-permute-start(f32[16,128]{1,0:T(8,128)S(1)} %get-tuple-element.50), channel_id=1, source_target_pairs={{8,0},{0,8},{24,16},{16,24},{40,32},{32,40},{56,48},{48,56},{72,64... | collective-permute-start | bytes 24584 | tf_op jit(solution)/shard_map/ppermute | solution.py:459
  2.4 5.8 %collective-permute-start.1 = (f32[16,128]{1,0:T(8,128)S(1)}, f32[16,128]{1,0:T(8,128)S(1)}, u32[]{:S(2)}, u32[]{:S(2)}) collective-permute-start(f32[16,128]{1,0:T(8,128)S(1)} %get-tuple-element.50), channel_id=1, source_target_pairs={{120,0},{16,8},{8,16},{32,24},{24,32},{48,40},{40,48},{64,56},{56,... | collective-permute-start | bytes 24584 | tf_op jit(solution)/shard_map/ppermute | solution.py:459
  8.5 29.6 %copy-start = (bf16[128,1920]{1,0:T(8,128)(2,1)S(1)}, bf16[128,1920]{1,0:T(8,128)(2,1)}, u32[]{:S(2)}) copy-start(bf16[128,1920]{1,0:T(8,128)(2,1)} %ctx_w.1) | copy-start | bytes 1474564
  8.5 29.5 %copy-start.1 = (bf16[128,32]{0,1:T(8,128)(2,1)S(1)}, bf16[128,32]{0,1:T(8,128)(2,1)}, u32[]{:S(2)}) copy-start(bf16[128,32]{0,1:T(8,128)(2,1)} %param.23) | copy-start | bytes 24580
  8.5 29.5 %copy-start.4 = (bf16[2,800]{1,0:T(2,128)(2,1)S(1)}, bf16[2,800]{1,0:T(2,128)(2,1)}, u32[]{:S(2)}) copy-start(bf16[2,800]{1,0:T(2,128)(2,1)} %refs_7_.1) | copy-start | bytes 9604
  8.5 29.5 %copy-start.6 = (f32[128]{0:T(128)S(1)}, f32[128]{0:T(128)}, u32[]{:S(2)}) copy-start(f32[128]{0:T(128)} %param.24) | copy-start | bytes 1540
  8.5 29.5 %copy-start.10 = (f32[32]{0:T(128)S(1)}, f32[32]{0:T(128)}, u32[]{:S(2)}) copy-start(f32[32]{0:T(128)} %param.27) | copy-start | bytes 388
  8.5 10.7 %collective-permute-start.2 = (f32[8,640]{1,0:T(8,128)S(1)}, f32[8,640]{1,0:T(8,128)S(1)}, u32[]{:S(2)}, u32[]{:S(2)}) collective-permute-start(f32[8,640]{1,0:T(8,128)S(1)} %get-tuple-element.57), channel_id=1, source_target_pairs={{1,0},{9,8},{17,16},{25,24},{33,32},{41,40},{49,48},{57,56},{65,64... | collective-permute-start | bytes 61448 | tf_op jit(solution)/shard_map/ppermute | solution.py:459
  11.3 7.9 %collective-permute-start.3 = (f32[8,640]{1,0:T(8,128)S(1)}, f32[8,640]{1,0:T(8,128)S(1)}, u32[]{:S(2)}, u32[]{:S(2)}) collective-permute-start(f32[8,640]{1,0:T(8,128)S(1)} %get-tuple-element.58), channel_id=1, source_target_pairs={{7,0},{15,8},{23,16},{31,24},{39,32},{47,40},{55,48},{63,56},{71,6... | collective-permute-start | bytes 61448 | tf_op jit(solution)/shard_map/ppermute | solution.py:459
  19.2 30.6 %copy-start.3 = (bf16[32,128]{1,0:T(8,128)(2,1)S(1)}, bf16[32,128]{1,0:T(8,128)(2,1)}, u32[]{:S(2)}) copy-start(bf16[32,128]{1,0:T(8,128)(2,1)} %up_w.1) | copy-start | bytes 24580
  19.2 30.6 %copy-start.11 = (f32[2]{0:T(128)S(1)}, f32[2]{0:T(128)}, u32[]{:S(2)}) copy-start(f32[2]{0:T(128)} %head_b.1) | copy-start | bytes 28
  21.0 1.4 %collective-permute-start.4 = (bf16[32,2048]{1,0:T(8,128)(2,1)S(1)}, bf16[32,2048]{1,0:T(8,128)(2,1)S(1)}, u32[]{:S(2)}, u32[]{:S(2)}) collective-permute-start(bf16[32,2048]{1,0:T(8,128)(2,1)S(1)} %get-tuple-element.64), channel_id=1, source_target_pairs={{8,0},{0,8},{24,16},{16,24},{40,32},{32,40},{56,48},{48,56},{72,64... | collective-permute-start | bytes 393224 | tf_op jit(solution)/shard_map/ppermute | solution.py:459
  22.4 13.9 %collective-permute-start.5 = (bf16[2,32,2048]{2,1,0:T(8,128)(2,1)S(1)}, bf16[2,32,2048]{2,1,0:T(8,128)(2,1)S(1)}, u32[]{:S(2)}, u32[]{:S(2)}) collective-permute-start(bf16[2,32,2048]{2,1,0:T(8,128)(2,1)S(1)} %bitcast_dynamic-update-slice_fusion.refs_0_), channel_id=1, source_target_pairs={{119,0},{25,8},{7,16},{41,24},{23,32},{57,40},{39,48},{73,56},{55,... | collective-permute-start | bytes 786440 | tf_op jit(solution)/shard_map/ppermute | solution.py:459
  22.5 15.5 %collective-permute-start.9 = (bf16[2,32,2048]{2,1,0:T(8,128)(2,1)S(1)}, bf16[2,32,2048]{2,1,0:T(8,128)(2,1)S(1)}, u32[]{:S(2)}, u32[]{:S(2)}) collective-permute-start(bf16[2,32,2048]{2,1,0:T(8,128)(2,1)S(1)} %bitcast_dynamic-update-slice_fusion.refs_0_), channel_id=1, source_target_pairs={{112,0},{24,8},{0,16},{40,24},{16,32},{56,40},{32,48},{72,56},{48,... | collective-permute-start | bytes 786440 | tf_op jit(solution)/shard_map/ppermute | solution.py:459
  36.3 1.7 %collective-permute-start.8 = (bf16[2,32,2048]{2,1,0:T(8,128)(2,1)S(1)}, bf16[2,32,2048]{2,1,0:T(8,128)(2,1)S(1)}, u32[]{:S(2)}, u32[]{:S(2)}) collective-permute-start(bf16[2,32,2048]{2,1,0:T(8,128)(2,1)S(1)} %collective-permute-done.5.refs_1_), channel_id=1, source_target_pairs={{8,0},{0,8},{24,16},{16,24},{40,32},{32,40},{56,48},{48,56},{72,64... | collective-permute-start | bytes 786440 | tf_op jit(solution)/shard_map/ppermute | solution.py:459
  36.3 11.6 %collective-permute-start.6 = (bf16[2,32,2048]{2,1,0:T(8,128)(2,1)S(1)}, bf16[2,32,2048]{2,1,0:T(8,128)(2,1)S(1)}, u32[]{:S(2)}, u32[]{:S(2)}) collective-permute-start(bf16[2,32,2048]{2,1,0:T(8,128)(2,1)S(1)} %collective-permute-done.5.refs_1_), channel_id=1, source_target_pairs={{120,0},{16,8},{8,16},{32,24},{24,32},{48,40},{40,48},{64,56},{56,... | collective-permute-start | bytes 786440 | tf_op jit(solution)/shard_map/ppermute | solution.py:459
  36.3 11.6 %collective-permute-start.7 = (bf16[2,32,2048]{2,1,0:T(8,128)(2,1)S(1)}, bf16[2,32,2048]{2,1,0:T(8,128)(2,1)S(1)}, u32[]{:S(2)}, u32[]{:S(2)}) collective-permute-start(bf16[2,32,2048]{2,1,0:T(8,128)(2,1)S(1)} %bitcast_dynamic-update-slice_fusion.refs_0_), channel_id=1, source_target_pairs={{113,0},{31,8},{1,16},{47,24},{17,32},{63,40},{33,48},{79,56},{49,... | collective-permute-start | bytes 786440 | tf_op jit(solution)/shard_map/ppermute | solution.py:459
  38.0 10.4 %collective-permute-start.12 = (bf16[2,32,2048]{2,1,0:T(8,128)(2,1)S(1)}, bf16[2,32,2048]{2,1,0:T(8,128)(2,1)S(1)}, u32[]{:S(2)}, u32[]{:S(2)}) collective-permute-start(bf16[2,32,2048]{2,1,0:T(8,128)(2,1)S(1)} %collective-permute-done.9.refs_3_), channel_id=1, source_target_pairs={{8,0},{0,8},{24,16},{16,24},{40,32},{32,40},{56,48},{48,56},{72,64... | collective-permute-start | bytes 786440 | tf_op jit(solution)/shard_map/ppermute | solution.py:459
  47.9 1.5 %collective-permute-start.10 = (bf16[2,32,2048]{2,1,0:T(8,128)(2,1)S(1)}, bf16[2,32,2048]{2,1,0:T(8,128)(2,1)S(1)}, u32[]{:S(2)}, u32[]{:S(2)}) collective-permute-start(bf16[2,32,2048]{2,1,0:T(8,128)(2,1)S(1)} %collective-permute-done.7.two), channel_id=1, source_target_pairs={{8,0},{0,8},{24,16},{16,24},{40,32},{32,40},{56,48},{48,56},{72,64... | collective-permute-start | bytes 786440 | tf_op jit(solution)/shard_map/ppermute | solution.py:459
  47.9 1.9 %collective-permute-start.11 = (bf16[2,32,2048]{2,1,0:T(8,128)(2,1)S(1)}, bf16[2,32,2048]{2,1,0:T(8,128)(2,1)S(1)}, u32[]{:S(2)}, u32[]{:S(2)}) collective-permute-start(bf16[2,32,2048]{2,1,0:T(8,128)(2,1)S(1)} %collective-permute-done.6.relay), channel_id=1, source_target_pairs={{8,0},{0,8},{24,16},{16,24},{40,32},{32,40},{56,48},{48,56},{72,64... | collective-permute-start | bytes 786440 | tf_op jit(solution)/shard_map/ppermute | solution.py:459
  55.0 2.1 %collective-permute-start.13 = (f32[72,128]{1,0:T(8,128)S(1)}, f32[72,128]{1,0:T(8,128)S(1)}, u32[]{:S(2)}, u32[]{:S(2)}) collective-permute-start(f32[72,128]{1,0:T(8,128)S(1)} %get-tuple-element.75), channel_id=1, source_target_pairs={{8,0},{0,8},{24,16},{16,24},{40,32},{32,40},{56,48},{48,56},{72,64... | collective-permute-start | bytes 110600 | tf_op jit(solution)/shard_map/ppermute | solution.py:459
  55.2 5.5 %collective-permute-start.14 = (f32[72,128]{1,0:T(8,128)S(1)}, f32[72,128]{1,0:T(8,128)S(1)}, u32[]{:S(2)}, u32[]{:S(2)}) collective-permute-start(f32[72,128]{1,0:T(8,128)S(1)} %get-tuple-element.75), channel_id=1, source_target_pairs={{120,0},{16,8},{8,16},{32,24},{24,32},{48,40},{40,48},{64,56},{56,... | collective-permute-start | bytes 110600 | tf_op jit(solution)/shard_map/ppermute | solution.py:459
  60.7 5.3 %collective-permute-start.15 = (f32[8,512]{1,0:T(8,128)S(1)}, f32[8,512]{1,0:T(8,128)S(1)}, u32[]{:S(2)}, u32[]{:S(2)}) collective-permute-start(f32[8,512]{1,0:T(8,128)S(1)} %maximum_add_fusion), channel_id=1, source_target_pairs={{1,0},{9,8},{17,16},{25,24},{33,32},{41,40},{49,48},{57,56},{65,64... | collective-permute-start | bytes 49160 | tf_op jit(solution)/shard_map/ppermute | solution.py:459
  60.8 7.4 %collective-permute-start.16 = (f32[8,512]{1,0:T(8,128)S(1)}, f32[8,512]{1,0:T(8,128)S(1)}, u32[]{:S(2)}, u32[]{:S(2)}) collective-permute-start(f32[8,512]{1,0:T(8,128)S(1)} %maximum_add_fusion), channel_id=1, source_target_pairs={{7,0},{15,8},{23,16},{31,24},{39,32},{47,40},{55,48},{63,56},{71,6... | collective-permute-start | bytes 49160 | tf_op jit(solution)/shard_map/ppermute | solution.py:459

commit v5 on v4

--- a/solution.py
+++ b/solution.py
@@ -264,7 +264,7 @@
     (-1, -2): ("one", 0), (-1, -1): ("one", 1), (-1, 0): ("relay_p", 0), (-1, 1): ("relay_p", 1), (-1, 2): ("two_p", 1),
     (1, -2): ("two", 0), (1, -1): ("two", 1), (1, 0): ("relay", 1), (1, 1): ("relay", 0), (1, 2): ("one_p", 1),
 }
-PHASES = (("own", "one", "one_p", "band"), ("two", "two_p", "relay", "relay_p", "band_p"))
+PHASES = (("own", "one", "band"), ("two", "two_p", "relay", "relay_p", "band_p", "one_p"))
 TILES = [[at for at in range(15) if MAPS[(at // 5 - 1, at % 5 - 2)][0] in names] for names in PHASES]
 
 
@@ -312,11 +312,11 @@
 
 
 def logits_kernel(
-    cells, low, high, rim_rows, rim_cols, context, two, two_p, relay, relay_p, band_p,
+    cells, low, high, rim_rows, rim_cols, context, two, two_p, relay, relay_p, band_p, one_p,
     proj_w, proj_b, ctx_w, up_w, up_b, head_w, rim_w, head_b,
     logits, col_out, row_out, weights, proj, low_up, lifted, decoded,
 ):
-    arrays = dict(zip(PHASES[1], (two, two_p, relay, relay_p, band_p)))
+    arrays = dict(zip(PHASES[1], (two, two_p, relay, relay_p, band_p, one_p)))
 
     def finish(part, spots, total):
         mixed = jnp.maximum(total + context[:, spots], 0.0).astype(BF16)
@@ -516,9 +516,8 @@
 
     own = own.at[1].set(partner(pooled))
     one, band = beside(own, -1), beside(own, 0)
-    own, one = tie((own, one))
     relay, two = outer(one), beside(own, 1)
-    sent = dict(own=own, one=one, band=band, one_p=partner(one))
+    sent = dict(own=own, one=one, band=band)
 
     def context_call(kernel, phase, outs, args, scratch=(), **more):
         count = len(TILES[phase]) * WIDE
@@ -535,13 +534,13 @@
     )
     relay, two, context = tie((relay, two, context))
     relay_p, two_p = partner(relay), partner(two)
-    band_p = partner(band)
+    band_p, one_p = partner(band), partner(one)
 
     inner_logits, col_out, row_out = context_call(
         logits_kernel, 1,
         [shape_of(2, ROWS, COLS), shape_of(ROWS + 8, 128), shape_of(8, COLS)],
         [
-            feat_low, feat_high, rim_rows, rim_cols, context, two, two_p, relay, relay_p, band_p,
+            feat_low, feat_high, rim_rows, rim_cols, context, two, two_p, relay, relay_p, band_p, one_p,
             *proj_args, w_up, up_bias, head_w, rim_w, b_head,
         ],
         [
@@ -549,7 +548,7 @@
             pltpu.VMEM((POOL_ROWS * CH, COLS), F32),
             pltpu.VMEM(((ROWS + 4) * CH, COLS), BF16),
         ],
-        smem=(18,),
+        smem=(19,),
     )
     near, far = partner(col_out), outer(col_out)
     row_out = row_sums(cells, row_out, near, far)

time: 69.2 us -> 66.5 us (0.961)
  waiting for transfers between devices: 29.6 us -> 25.1 us
  starting transfers between devices: 20.4 us -> 22 us
    ppermute x17, waiting for transfers between devices: 29.6 us -> 25.1 us  [moved(): return lax.ppermute(x, ('band', 'cross'), route)]
    ppermute x17, starting transfers between devices: 20.4 us -> 22 us  [moved(): return lax.ppermute(x, ('band', 'cross'), route)]
  transfers between devices with their start and end apart: 17 -> 17, of which waited for: 8 -> 9; matrix products, arithmetic and copies ran while one was open for 0% -> 0% of each run, Pallas kernels for 12% -> 13%
where the time goes in v5:
time: 66.5 us; the launch traced here: 66.4 us
  waiting for transfers between devices  25.1 us (38%)
  starting transfers between devices  22 us (33%)
  Pallas kernels  16.6 us (25%)
  local copies, waits for them, and re-layouts  2.09 us (3%)
    ppermute x17, waiting for transfers between devices, moved(): return lax.ppermute(x, ('band', 'cross'), route)  25.1 us
    ppermute x17, starting transfers between devices, moved(): return lax.ppermute(x, ('band', 'cross'), route)  22 us
    pallas_call x7, Pallas kernels, call(): pl.pallas_call(fetching if hbm else kernel, out_shape=outs, in_specs=[SME...  16.6 us
    unnamed x28, local copies, waits for them, and re-layouts  2.07 us
  transfers between devices with their start and end apart: 17, of which 9 were waited for; matrix products, arithmetic and copies ran while one was open for 0% of the time, Pallas kernels for 13%

profile of v5, /device:TPU:0, one launch (start us, length us, event | category | flops | bytes accessed | tf_op | source)
XLA Modules:
  0.0 66.4 jit_solution(2112439607791758146)
XLA Ops:
  0.0 1.1 %copy-done.12 = s32[4,64,512]{2,1,0:T(8,128)S(1)} copy-done((s32[4,64,512]{2,1,0:T(8,128)S(1)}, s32[4,64,512]{2,1,0:T(8,128)}, u32[]{:S(2)}) %copy-start.12) | copy-done | bytes 524312
  1.1 0.9 %copy-done.13 = f32[64,512]{1,0:T(8,128)S(1)} copy-done((f32[64,512]{1,0:T(8,128)S(1)}, f32[64,512]{1,0:T(8,128)}, u32[]{:S(2)}) %copy-start.13) | copy-done | bytes 131096
  2.0 0.3 shard_map.136
  2.3 0.1 collective-permute-start
  2.4 4.1 %collective-permute-start.1 = (f32[16,128]{1,0:T(8,128)S(1)}, f32[16,128]{1,0:T(8,128)S(1)}, u32[]{:S(2)}, u32[]{:S(2)}) collective-permute-start(f32[16,128]{1,0:T(8,128)S(1)} %get-tuple-element.48), channel_id=1, source_target_pairs={{120,0},{16,8},{8,16},{32,24},{24,32},{48,40},{40,48},{64,56},{56,... | collective-permute-start | bytes 24584 | tf_op jit(solution)/shard_map/ppermute | solution.py:459
  6.6 1.5 %shard_map.137 = (bf16[512,512]{1,0:T(8,128)(2,1)S(1)}, f32[32,512]{1,0:T(8,128)S(1)}) custom-call(bf16[512,512]{1,0:T(8,128)(2,1)S(1)} %get-tuple-element.52.stem_in, f32[4,32]{1,0:T(4,128)S(1)} %bitcast.11, f32[1,32]{1,0:T(1,128)S(1)} %bitcast.16, f32[1,32]{1,0:T(1,128)S(1)} %bitcast.19, bf16[32,288]{1,0:T(8,128)(2,1)S(1)} %copy-done.2, f32[1,32]{1,0:T(1,128)S(1)} %bitcast.22), custom_call_target="tpu_custom_call" | custom-call | flops 4000000000 | bytes 1048576 | tf_op jit(solution)/shard_map/pallas_call | solution.py:435
  8.1 0.0 collective-permute-done.partner
  8.1 0.0 collective-permute-done.1.outer
  8.2 0.2 multiply_reduce_fusion.2
  8.4 0.1 select_select_fusion.1
  8.5 0.0 copy-start
  8.5 0.0 copy-start.1
  8.5 0.0 copy-start.4
  8.5 0.0 copy-start.6
  8.5 0.0 copy-start.10
  8.5 2.8 %collective-permute-start.2 = (f32[8,640]{1,0:T(8,128)S(1)}, f32[8,640]{1,0:T(8,128)S(1)}, u32[]{:S(2)}, u32[]{:S(2)}) collective-permute-start(f32[8,640]{1,0:T(8,128)S(1)} %get-tuple-element.55), channel_id=1, source_target_pairs={{1,0},{9,8},{17,16},{25,24},{33,32},{41,40},{49,48},{57,56},{65,64... | collective-permute-start | bytes 61448 | tf_op jit(solution)/shard_map/ppermute | solution.py:459
  11.3 4.3 %collective-permute-start.3 = (f32[8,640]{1,0:T(8,128)S(1)}, f32[8,640]{1,0:T(8,128)S(1)}, u32[]{:S(2)}, u32[]{:S(2)}) collective-permute-start(f32[8,640]{1,0:T(8,128)S(1)} %get-tuple-element.56), channel_id=1, source_target_pairs={{7,0},{15,8},{23,16},{31,24},{39,32},{47,40},{55,48},{63,56},{71,6... | collective-permute-start | bytes 61448 | tf_op jit(solution)/shard_map/ppermute | solution.py:459
  15.6 3.6 %shard_map.138 = (bf16[1536,512]{1,0:T(8,128)(2,1)S(1)}, f32[32,1536]{1,0:T(8,128)S(1)}) custom-call(bf16[512,512]{1,0:T(8,128)(2,1)S(1)} %get-tuple-element.52.stem_in, f32[4,32]{1,0:T(4,128)S(1)} %bitcast.12, f32[1,32]{1,0:T(1,128)S(1)} %bitcast.17, f32[1,32]{1,0:T(1,128)S(1)} %bitcast.20, bf16[32,288]{1,0:T(8,128)(2,1)S(1)} %copy-done.2, f32[1,32]{1,0:T(1,128)S(1)} %bitcast.23), custom_call_target="tpu_custom_call" | custom-call | flops 4000000000 | bytes 1048576 | tf_op jit(solution)/shard_map/pallas_call | solution.py:435
  19.2 0.0 copy-start.3
  19.2 0.0 copy-start.11
  19.2 0.0 collective-permute-done.2.even_message
  19.3 1.7 %shard_map.139 = (bf16[64,512]{1,0:T(8,128)(2,1)S(1)}, bf16[32,256]{1,0:T(8,128)(2,1)S(1)}, bf16[32,2048]{1,0:T(8,128)(2,1)S(1)}, bf16[2,32,2048]{2,1,0:T(8,128)(2,1)S(1)}) custom-call(f32[32,512]{1,0:T(8,128)S(1)} %get-tuple-element.47.rows, f32[32,128]{1,0:T(8,128)S(1)} %get-tuple-element.54.cols, f32[16,128]{1,0:T(8,128)S(1)} %collective-permute-done.partner, ...), custom_call_target="tpu_custom_call" | custom-call | bytes 1048576 | tf_op jit(solution)/shard_map/pallas_call | solution.py:435
  21.0 0.1 collective-permute-start.4
  21.1 1.3 %collective-permute-done.4 = bf16[32,2048]{1,0:T(8,128)(2,1)S(1)} collective-permute-done((bf16[32,2048]{1,0:T(8,128)(2,1)S(1)}, bf16[32,2048]{1,0:T(8,128)(2,1)S(1)}, u32[]{:S(2)}, u32[]{:S(2)}) %collective-permute-start.4) | collective-permute-done | bytes 131104 | tf_op jit(solution)/shard_map/ppermute | solution.py:459
  22.4 0.1 collective-permute-start.5
  22.5 0.2 collective-permute-start.8
  22.7 4.9 %collective-permute-start.7 = (bf16[2,32,2048]{2,1,0:T(8,128)(2,1)S(1)}, bf16[2,32,2048]{2,1,0:T(8,128)(2,1)S(1)}, u32[]{:S(2)}, u32[]{:S(2)}) collective-permute-start(bf16[2,32,2048]{2,1,0:T(8,128)(2,1)S(1)} %bitcast_dynamic-update-slice_fusion.refs_0_), channel_id=1, source_target_pairs={{113,0},{31,8},{1,16},{47,24},{17,32},{63,40},{33,48},{79,56},{49,... | collective-permute-start | bytes 786440 | tf_op jit(solution)/shard_map/ppermute | solution.py:459
  27.6 9.6 %collective-permute-done.5.refs_1_ = bf16[2,32,2048]{2,1,0:T(8,128)(2,1)S(1)} collective-permute-done((bf16[2,32,2048]{2,1,0:T(8,128)(2,1)S(1)}, bf16[2,32,2048]{2,1,0:T(8,128)(2,1)S(1)}, u32[]{:S(2)}, u32[]{:S(2)}) %collective-permute-start.5) | collective-permute-done | bytes 262176 | tf_op jit(solution)/shard_map/ppermute | solution.py:459
  37.2 0.0 collective-permute-start.12
  37.2 0.0 collective-permute-done.8.refs_2_
  37.2 0.5 collective-permute-start.11
  37.7 3.3 %shard_map.140 = (f32[128,2048]{1,0:T(8,128)S(1)}, bf16[160,640]{1,0:T(8,128)(2,1)S(1)}, bf16[40,128]{1,0:T(8,128)(2,1)S(1)}, f32[32,256]{1,0:T(8,128)S(1)}) custom-call(bf16[2,32,2048]{2,1,0:T(8,128)(2,1)S(1)} %bitcast_dynamic-update-slice_fusion.refs_0_, bf16[2,32,2048]{2,1,0:T(8,128)(2,1)S(1)} %collective-permute-done.5.refs_1_, ...), custom_call_target="tpu_custom_call" | custom-call | bytes 1048576 | tf_op jit(solution)/shard_map/pallas_call | solution.py:435
  41.0 0.0 collective-permute-done.7.two
  41.0 4.1 %collective-permute-done.6.relay = bf16[2,32,2048]{2,1,0:T(8,128)(2,1)S(1)} collective-permute-done((bf16[2,32,2048]{2,1,0:T(8,128)(2,1)S(1)}, bf16[2,32,2048]{2,1,0:T(8,128)(2,1)S(1)}, u32[]{:S(2)}, u32[]{:S(2)}) %collective-permute-start.6) | collective-permute-done | bytes 262176 | tf_op jit(solution)/shard_map/ppermute | solution.py:459
  45.1 0.0 collective-permute-start.10
  45.1 0.5 collective-permute-start.9
  45.6 0.0 collective-permute-done.11.band_p
  45.6 1.0 %collective-permute-done.10.relay_p = bf16[2,32,2048]{2,1,0:T(8,128)(2,1)S(1)} collective-permute-done((bf16[2,32,2048]{2,1,0:T(8,128)(2,1)S(1)}, bf16[2,32,2048]{2,1,0:T(8,128)(2,1)S(1)}, u32[]{:S(2)}, u32[]{:S(2)}) %collective-permute-start.10) | collective-permute-done | bytes 262176 | tf_op jit(solution)/shard_map/ppermute | solution.py:459
  46.6 0.4 collective-permute-done.9.two_p
  47.0 5.4 %shard_map.141 = (f32[2,64,512]{2,1,0:T(8,128)S(1)}, f32[72,128]{1,0:T(8,128)S(1)}, f32[8,512]{1,0:T(8,128)S(1)}) custom-call(bf16[512,512]{1,0:T(8,128)(2,1)S(1)} %get-tuple-element.46.low, bf16[1536,512]{1,0:T(8,128)(2,1)S(1)} %get-tuple-element.53.high, bf16[64,512]{1,0:T(8,128)(2,1)S(1)} %get-tuple-element.59.rim_rows, ...), custom_call_target="tpu_custom_call" | custom-call | bytes 1048576 | tf_op jit(solution)/shard_map/pallas_call | solution.py:435
  52.3 0.2 collective-permute-start.13
  52.6 1.0 %collective-permute-done.13.partner = f32[72,128]{1,0:T(8,128)S(1)} collective-permute-done((f32[72,128]{1,0:T(8,128)S(1)}, f32[72,128]{1,0:T(8,128)S(1)}, u32[]{:S(2)}, u32[]{:S(2)}) %collective-permute-start.13) | collective-permute-done | bytes 36896 | tf_op jit(solution)/shard_map/ppermute | solution.py:459
  53.6 4.4 %collective-permute-done.14.outer = f32[72,128]{1,0:T(8,128)S(1)} collective-permute-done((f32[72,128]{1,0:T(8,128)S(1)}, f32[72,128]{1,0:T(8,128)S(1)}, u32[]{:S(2)}, u32[]{:S(2)}) %collective-permute-start.14) | collective-permute-done | bytes 36896 | tf_op jit(solution)/shard_map/ppermute | solution.py:459
  58.1 0.1 collective-permute-start.15
  58.2 4.2 %collective-permute-start.16 = (f32[8,512]{1,0:T(8,128)S(1)}, f32[8,512]{1,0:T(8,128)S(1)}, u32[]{:S(2)}, u32[]{:S(2)}) collective-permute-start(f32[8,512]{1,0:T(8,128)S(1)} %maximum_add_fusion), channel_id=1, source_target_pairs={{7,0},{15,8},{23,16},{31,24},{39,32},{47,40},{55,48},{63,56},{71,6... | collective-permute-start | bytes 49160 | tf_op jit(solution)/shard_map/ppermute | solution.py:459
  62.3 1.1 %collective-permute-done.15.even_message = f32[8,512]{1,0:T(8,128)S(1)} collective-permute-done((f32[8,512]{1,0:T(8,128)S(1)}, f32[8,512]{1,0:T(8,128)S(1)}, u32[]{:S(2)}, u32[]{:S(2)}) %collective-permute-start.15) | collective-permute-done | bytes 16416 | tf_op jit(solution)/shard_map/ppermute | solution.py:459
  63.4 2.2 %collective-permute-done.16.odd_message = f32[8,512]{1,0:T(8,128)S(1)} collective-permute-done((f32[8,512]{1,0:T(8,128)S(1)}, f32[8,512]{1,0:T(8,128)S(1)}, u32[]{:S(2)}, u32[]{:S(2)}) %collective-permute-start.16) | collective-permute-done | bytes 16416 | tf_op jit(solution)/shard_map/ppermute | solution.py:459
  65.6 0.8 %shard_map.142 = f32[2,64,512]{2,1,0:T(8,128)} custom-call(f32[2,64,512]{2,1,0:T(8,128)S(1)} %get-tuple-element.70.inner, f32[72,128]{1,0:T(8,128)S(1)} %collective-permute-done.13.partner, f32[72,128]{1,0:T(8,128)S(1)} %collective-permute-done.14.outer, f32[8,512]{1,0:T(8,128)S(1)} %collective-permute-done.15.even_message, ...), custom_call_target="tpu_custom_call" | custom-call | bytes 1048576 | tf_op jit(solution)/shard_map/pallas_call | solution.py:435
  (33 shorter events, 0.1 us)
Async XLA Ops:
  0.0 6.5 %copy-start.5 = (f32[32,4]{0,1:T(4,128)S(1)}, f32[32,4]{0,1:T(4,128)}, u32[]{:S(2)}) copy-start(f32[32,4]{0,1:T(4,128)} %param.18) | copy-start | bytes 1540
  0.0 6.5 %copy-start.7 = (f32[32]{0:T(128)S(1)}, f32[32]{0:T(128)}, u32[]{:S(2)}) copy-start(f32[32]{0:T(128)} %param.19) | copy-start | bytes 388
  0.0 6.5 %copy-start.8 = (f32[32]{0:T(128)S(1)}, f32[32]{0:T(128)}, u32[]{:S(2)}) copy-start(f32[32]{0:T(128)} %param.20) | copy-start | bytes 388
  0.0 6.5 %copy-start.9 = (f32[32]{0:T(128)S(1)}, f32[32]{0:T(128)}, u32[]{:S(2)}) copy-start(f32[32]{0:T(128)} %param.22) | copy-start | bytes 388
  0.0 6.5 %copy-start.2 = (bf16[32,288]{1,0:T(8,128)(2,1)S(1)}, bf16[32,288]{1,0:T(8,128)(2,1)}, u32[]{:S(2)}) copy-start(bf16[32,288]{1,0:T(8,128)(2,1)} %conv_w.5) | copy-start | bytes 55300
  0.0 1.1 %copy-start.12 = (s32[4,64,512]{2,1,0:T(8,128)S(1)}, s32[4,64,512]{2,1,0:T(8,128)}, u32[]{:S(2)}) copy-start(s32[4,64,512]{2,1,0:T(8,128)} %rasters.1) | copy-start | bytes 1572868
  1.1 0.9 %copy-start.13 = (f32[64,512]{1,0:T(8,128)S(1)}, f32[64,512]{1,0:T(8,128)}, u32[]{:S(2)}) copy-start(f32[64,512]{1,0:T(8,128)} %aerial.1) | copy-start | bytes 393220
  2.3 5.8 %collective-permute-start = (f32[16,128]{1,0:T(8,128)S(1)}, f32[16,128]{1,0:T(8,128)S(1)}, u32[]{:S(2)}, u32[]{:S(2)}) collective-permute-start(f32[16,128]{1,0:T(8,128)S(1)} %get-tuple-element.48), channel_id=1, source_target_pairs={{8,0},{0,8},{24,16},{16,24},{40,32},{32,40},{56,48},{48,56},{72,64... | collective-permute-start | bytes 24584 | tf_op jit(solution)/shard_map/ppermute | solution.py:459
  2.4 5.8 %collective-permute-start.1 = (f32[16,128]{1,0:T(8,128)S(1)}, f32[16,128]{1,0:T(8,128)S(1)}, u32[]{:S(2)}, u32[]{:S(2)}) collective-permute-start(f32[16,128]{1,0:T(8,128)S(1)} %get-tuple-element.48), channel_id=1, source_target_pairs={{120,0},{16,8},{8,16},{32,24},{24,32},{48,40},{40,48},{64,56},{56,... | collective-permute-start | bytes 24584 | tf_op jit(solution)/shard_map/ppermute | solution.py:459
  8.5 29.2 %copy-start = (bf16[128,1920]{1,0:T(8,128)(2,1)S(1)}, bf16[128,1920]{1,0:T(8,128)(2,1)}, u32[]{:S(2)}) copy-start(bf16[128,1920]{1,0:T(8,128)(2,1)} %ctx_w.1) | copy-start | bytes 1474564
  8.5 29.2 %copy-start.1 = (bf16[128,32]{0,1:T(8,128)(2,1)S(1)}, bf16[128,32]{0,1:T(8,128)(2,1)}, u32[]{:S(2)}) copy-start(bf16[128,32]{0,1:T(8,128)(2,1)} %param.23) | copy-start | bytes 24580
  8.5 29.2 %copy-start.4 = (bf16[2,800]{1,0:T(2,128)(2,1)S(1)}, bf16[2,800]{1,0:T(2,128)(2,1)}, u32[]{:S(2)}) copy-start(bf16[2,800]{1,0:T(2,128)(2,1)} %refs_6_.1) | copy-start | bytes 9604
  8.5 29.2 %copy-start.6 = (f32[128]{0:T(128)S(1)}, f32[128]{0:T(128)}, u32[]{:S(2)}) copy-start(f32[128]{0:T(128)} %param.24) | copy-start | bytes 1540
  8.5 29.2 %copy-start.10 = (f32[32]{0:T(128)S(1)}, f32[32]{0:T(128)}, u32[]{:S(2)}) copy-start(f32[32]{0:T(128)} %param.27) | copy-start | bytes 388
  8.5 10.7 %collective-permute-start.2 = (f32[8,640]{1,0:T(8,128)S(1)}, f32[8,640]{1,0:T(8,128)S(1)}, u32[]{:S(2)}, u32[]{:S(2)}) collective-permute-start(f32[8,640]{1,0:T(8,128)S(1)} %get-tuple-element.55), channel_id=1, source_target_pairs={{1,0},{9,8},{17,16},{25,24},{33,32},{41,40},{49,48},{57,56},{65,64... | collective-permute-start | bytes 61448 | tf_op jit(solution)/shard_map/ppermute | solution.py:459
  11.3 7.9 %collective-permute-start.3 = (f32[8,640]{1,0:T(8,128)S(1)}, f32[8,640]{1,0:T(8,128)S(1)}, u32[]{:S(2)}, u32[]{:S(2)}) collective-permute-start(f32[8,640]{1,0:T(8,128)S(1)} %get-tuple-element.56), channel_id=1, source_target_pairs={{7,0},{15,8},{23,16},{31,24},{39,32},{47,40},{55,48},{63,56},{71,6... | collective-permute-start | bytes 61448 | tf_op jit(solution)/shard_map/ppermute | solution.py:459
  19.2 27.7 %copy-start.3 = (bf16[32,128]{1,0:T(8,128)(2,1)S(1)}, bf16[32,128]{1,0:T(8,128)(2,1)}, u32[]{:S(2)}) copy-start(bf16[32,128]{1,0:T(8,128)(2,1)} %up_w.1) | copy-start | bytes 24580
  19.2 27.7 %copy-start.11 = (f32[2]{0:T(128)S(1)}, f32[2]{0:T(128)}, u32[]{:S(2)}) copy-start(f32[2]{0:T(128)} %head_b.1) | copy-start | bytes 28
  21.0 1.4 %collective-permute-start.4 = (bf16[32,2048]{1,0:T(8,128)(2,1)S(1)}, bf16[32,2048]{1,0:T(8,128)(2,1)S(1)}, u32[]{:S(2)}, u32[]{:S(2)}) collective-permute-start(bf16[32,2048]{1,0:T(8,128)(2,1)S(1)} %get-tuple-element.62), channel_id=1, source_target_pairs={{8,0},{0,8},{24,16},{16,24},{40,32},{32,40},{56,48},{48,56},{72,64... | collective-permute-start | bytes 393224 | tf_op jit(solution)/shard_map/ppermute | solution.py:459
  22.4 14.7 %collective-permute-start.5 = (bf16[2,32,2048]{2,1,0:T(8,128)(2,1)S(1)}, bf16[2,32,2048]{2,1,0:T(8,128)(2,1)S(1)}, u32[]{:S(2)}, u32[]{:S(2)}) collective-permute-start(bf16[2,32,2048]{2,1,0:T(8,128)(2,1)S(1)} %bitcast_dynamic-update-slice_fusion.refs_0_), channel_id=1, source_target_pairs={{119,0},{25,8},{7,16},{41,24},{23,32},{57,40},{39,48},{73,56},{55,... | collective-permute-start | bytes 786440 | tf_op jit(solution)/shard_map/ppermute | solution.py:459
  22.5 14.7 %collective-permute-start.8 = (bf16[2,32,2048]{2,1,0:T(8,128)(2,1)S(1)}, bf16[2,32,2048]{2,1,0:T(8,128)(2,1)S(1)}, u32[]{:S(2)}, u32[]{:S(2)}) collective-permute-start(bf16[2,32,2048]{2,1,0:T(8,128)(2,1)S(1)} %bitcast_dynamic-update-slice_fusion.refs_0_), channel_id=1, source_target_pairs={{112,0},{24,8},{0,16},{40,24},{16,32},{56,40},{32,48},{72,56},{48,... | collective-permute-start | bytes 786440 | tf_op jit(solution)/shard_map/ppermute | solution.py:459
  22.7 18.3 %collective-permute-start.7 = (bf16[2,32,2048]{2,1,0:T(8,128)(2,1)S(1)}, bf16[2,32,2048]{2,1,0:T(8,128)(2,1)S(1)}, u32[]{:S(2)}, u32[]{:S(2)}) collective-permute-start(bf16[2,32,2048]{2,1,0:T(8,128)(2,1)S(1)} %bitcast_dynamic-update-slice_fusion.refs_0_), channel_id=1, source_target_pairs={{113,0},{31,8},{1,16},{47,24},{17,32},{63,40},{33,48},{79,56},{49,... | collective-permute-start | bytes 786440 | tf_op jit(solution)/shard_map/ppermute | solution.py:459
  37.1 7.9 %collective-permute-start.6 = (bf16[2,32,2048]{2,1,0:T(8,128)(2,1)S(1)}, bf16[2,32,2048]{2,1,0:T(8,128)(2,1)S(1)}, u32[]{:S(2)}, u32[]{:S(2)}) collective-permute-start(bf16[2,32,2048]{2,1,0:T(8,128)(2,1)S(1)} %collective-permute-done.5.refs_1_), channel_id=1, source_target_pairs={{120,0},{16,8},{8,16},{32,24},{24,32},{48,40},{40,48},{64,56},{56,... | collective-permute-start | bytes 786440 | tf_op jit(solution)/shard_map/ppermute | solution.py:459
  37.2 8.4 %collective-permute-start.12 = (bf16[2,32,2048]{2,1,0:T(8,128)(2,1)S(1)}, bf16[2,32,2048]{2,1,0:T(8,128)(2,1)S(1)}, u32[]{:S(2)}, u32[]{:S(2)}) collective-permute-start(bf16[2,32,2048]{2,1,0:T(8,128)(2,1)S(1)} %collective-permute-done.5.refs_1_), channel_id=1, source_target_pairs={{8,0},{0,8},{24,16},{16,24},{40,32},{32,40},{56,48},{48,56},{72,64... | collective-permute-start | bytes 786440 | tf_op jit(solution)/shard_map/ppermute | solution.py:459
  37.2 8.4 %collective-permute-start.11 = (bf16[2,32,2048]{2,1,0:T(8,128)(2,1)S(1)}, bf16[2,32,2048]{2,1,0:T(8,128)(2,1)S(1)}, u32[]{:S(2)}, u32[]{:S(2)}) collective-permute-start(bf16[2,32,2048]{2,1,0:T(8,128)(2,1)S(1)} %collective-permute-done.8.refs_2_), channel_id=1, source_target_pairs={{8,0},{0,8},{24,16},{16,24},{40,32},{32,40},{56,48},{48,56},{72,64... | collective-permute-start | bytes 786440 | tf_op jit(solution)/shard_map/ppermute | solution.py:459
  45.1 1.5 %collective-permute-start.10 = (bf16[2,32,2048]{2,1,0:T(8,128)(2,1)S(1)}, bf16[2,32,2048]{2,1,0:T(8,128)(2,1)S(1)}, u32[]{:S(2)}, u32[]{:S(2)}) collective-permute-start(bf16[2,32,2048]{2,1,0:T(8,128)(2,1)S(1)} %collective-permute-done.6.relay), channel_id=1, source_target_pairs={{8,0},{0,8},{24,16},{16,24},{40,32},{32,40},{56,48},{48,56},{72,64... | collective-permute-start | bytes 786440 | tf_op jit(solution)/shard_map/ppermute | solution.py:459
  45.1 1.9 %collective-permute-start.9 = (bf16[2,32,2048]{2,1,0:T(8,128)(2,1)S(1)}, bf16[2,32,2048]{2,1,0:T(8,128)(2,1)S(1)}, u32[]{:S(2)}, u32[]{:S(2)}) collective-permute-start(bf16[2,32,2048]{2,1,0:T(8,128)(2,1)S(1)} %collective-permute-done.7.two), channel_id=1, source_target_pairs={{8,0},{0,8},{24,16},{16,24},{40,32},{32,40},{56,48},{48,56},{72,64... | collective-permute-start | bytes 786440 | tf_op jit(solution)/shard_map/ppermute | solution.py:459
  52.3 1.3 %collective-permute-start.13 = (f32[72,128]{1,0:T(8,128)S(1)}, f32[72,128]{1,0:T(8,128)S(1)}, u32[]{:S(2)}, u32[]{:S(2)}) collective-permute-start(f32[72,128]{1,0:T(8,128)S(1)} %get-tuple-element.71), channel_id=1, source_target_pairs={{8,0},{0,8},{24,16},{16,24},{40,32},{32,40},{56,48},{48,56},{72,64... | collective-permute-start | bytes 110600 | tf_op jit(solution)/shard_map/ppermute | solution.py:459
  52.5 5.5 %collective-permute-start.14 = (f32[72,128]{1,0:T(8,128)S(1)}, f32[72,128]{1,0:T(8,128)S(1)}, u32[]{:S(2)}, u32[]{:S(2)}) collective-permute-start(f32[72,128]{1,0:T(8,128)S(1)} %get-tuple-element.71), channel_id=1, source_target_pairs={{120,0},{16,8},{8,16},{32,24},{24,32},{48,40},{40,48},{64,56},{56,... | collective-permute-start | bytes 110600 | tf_op jit(solution)/shard_map/ppermute | solution.py:459
  58.1 5.3 %collective-permute-start.15 = (f32[8,512]{1,0:T(8,128)S(1)}, f32[8,512]{1,0:T(8,128)S(1)}, u32[]{:S(2)}, u32[]{:S(2)}) collective-permute-start(f32[8,512]{1,0:T(8,128)S(1)} %maximum_add_fusion), channel_id=1, source_target_pairs={{1,0},{9,8},{17,16},{25,24},{33,32},{41,40},{49,48},{57,56},{65,64... | collective-permute-start | bytes 49160 | tf_op jit(solution)/shard_map/ppermute | solution.py:459
  58.2 7.4 %collective-permute-start.16 = (f32[8,512]{1,0:T(8,128)S(1)}, f32[8,512]{1,0:T(8,128)S(1)}, u32[]{:S(2)}, u32[]{:S(2)}) collective-permute-start(f32[8,512]{1,0:T(8,128)S(1)} %maximum_add_fusion), channel_id=1, source_target_pairs={{7,0},{15,8},{23,16},{31,24},{39,32},{47,40},{55,48},{63,56},{71,6... | collective-permute-start | bytes 49160 | tf_op jit(solution)/shard_map/ppermute | solution.py:459

commit v6 on v5

--- a/solution.py
+++ b/solution.py
@@ -283,16 +283,18 @@
     p_bias = jnp.broadcast_to(column(proj_b[...]), (WIDE, 256))
     proj_w = jnp.transpose(proj_w[...].astype(F32)).astype(BF16)
 
-    def part(at, carry):
-        spots = pl.ds(pl.multiple_of(at * 256, 256), 256)
+    def project(spots):
         for k, tile in enumerate(which):
             name, half = MAPS[(tile // 5 - 1, tile % 5 - 2)]
             out = mm(proj_w, arrays[name][half, :, spots])
-            proj[k * WIDE : (k + 1) * WIDE, :] = jnp.maximum(out + p_bias, 0.0).astype(BF16)
-        finish(at, spots, mm(weights[...], proj[...]))
-        return carry
-
-    lax.fori_loop(0, SPOTS // 256, part, 0, unroll=True)
+            proj[k * WIDE : (k + 1) * WIDE, spots] = jnp.maximum(out + p_bias, 0.0).astype(BF16)
+
+    spots = [slice(at * 256, (at + 1) * 256) for at in range(SPOTS // 256)]
+    project(spots[0])
+    for at, spot in enumerate(spots):
+        if at + 1 < len(spots):
+            project(spots[at + 1])
+        finish(at, spot, mm(weights[...], proj[:, spot]))
 
 
 def early_kernel(cells, *refs):
@@ -306,7 +308,7 @@
     own = TILES[0].index(7)
 
     def finish(at, spots, total):
-        context[:, spots] = total + proj[own * WIDE : (own + 1) * WIDE, :].astype(F32)
+        context[:, spots] = total + proj[own * WIDE : (own + 1) * WIDE, spots].astype(F32)
 
     context_sum(cells, TILES[0], arrays, proj_w, proj_b, ctx_w, weights, proj, finish)
 
@@ -326,7 +328,7 @@
             jnp.concatenate([high[:, h * 128 : (h + 1) * 128], low[:, h * 128 : (h + 1) * 128]], axis=1)
             for h in range(2)
         ]
-        low_up[pl.ds(pl.multiple_of(part * 64, 64), 64), :] = jnp.concatenate(both, axis=0)
+        low_up[part * 64 : (part + 1) * 64, :] = jnp.concatenate(both, axis=0)
 
     context_sum(cells, TILES[1], arrays, proj_w, proj_b, ctx_w, weights, proj, finish)
 
@@ -521,7 +523,7 @@
 
     def context_call(kernel, phase, outs, args, scratch=(), **more):
         count = len(TILES[phase]) * WIDE
-        buffers = [pltpu.VMEM((WIDE, count), BF16), pltpu.VMEM((count, 256), BF16)]
+        buffers = [pltpu.VMEM((WIDE, count), BF16), pltpu.VMEM((count, SPOTS), BF16)]
         return call(functools.partial(kernel, cells), outs, args, buffers + list(scratch), **more)
 
     context, head_w, rim_w, up_bias = context_call(

time: 66.5 us -> 65.8 us (0.989)
  Pallas kernels: 16.6 us -> 15.3 us
    pallas_call x7, Pallas kernels: 16.6 us -> 15.3 us  [call(): pl.pallas_call(fetching if hbm else kernel, out_shape=outs, in_specs=[SME...]
  transfers between devices with their start and end apart: 17 -> 17, of which waited for: 9 -> 9; matrix products, arithmetic and copies ran while one was open for 0% -> 0% of each run, Pallas kernels for 13% -> 12%
where the time goes in v6:
time: 65.8 us; the launch traced here: 65.7 us
  waiting for transfers between devices  25.7 us (39%)
  starting transfers between devices  22 us (33%)
  Pallas kernels  15.3 us (23%)
  local copies, waits for them, and re-layouts  2.09 us (3%)
    ppermute x17, waiting for transfers between devices, moved(): return lax.ppermute(x, ('band', 'cross'), route)  25.7 us
    ppermute x17, starting transfers between devices, moved(): return lax.ppermute(x, ('band', 'cross'), route)  22 us
    pallas_call x7, Pallas kernels, call(): pl.pallas_call(fetching if hbm else kernel, out_shape=outs, in_specs=[SME...  15.3 us
    unnamed x28, local copies, waits for them, and re-layouts  2.07 us
  transfers between devices with their start and end apart: 17, of which 9 were waited for; matrix products, arithmetic and copies ran while one was open for 0% of the time, Pallas kernels for 12%

profile of v6, /device:TPU:0, one launch (start us, length us, event | category | flops | bytes accessed | tf_op | source)
XLA Modules:
  0.0 65.7 jit_solution(17577049432379788363)
XLA Ops:
  0.0 1.1 %copy-done.12 = s32[4,64,512]{2,1,0:T(8,128)S(1)} copy-done((s32[4,64,512]{2,1,0:T(8,128)S(1)}, s32[4,64,512]{2,1,0:T(8,128)}, u32[]{:S(2)}) %copy-start.12) | copy-done | bytes 524312
  1.1 0.9 %copy-done.13 = f32[64,512]{1,0:T(8,128)S(1)} copy-done((f32[64,512]{1,0:T(8,128)S(1)}, f32[64,512]{1,0:T(8,128)}, u32[]{:S(2)}) %copy-start.13) | copy-done | bytes 131096
  2.0 0.3 shard_map.136
  2.3 0.1 collective-permute-start
  2.4 4.1 %collective-permute-start.1 = (f32[16,128]{1,0:T(8,128)S(1)}, f32[16,128]{1,0:T(8,128)S(1)}, u32[]{:S(2)}, u32[]{:S(2)}) collective-permute-start(f32[16,128]{1,0:T(8,128)S(1)} %get-tuple-element.48), channel_id=1, source_target_pairs={{120,0},{16,8},{8,16},{32,24},{24,32},{48,40},{40,48},{64,56},{56,... | collective-permute-start | bytes 24584 | tf_op jit(solution)/shard_map/ppermute | solution.py:461
  6.6 1.5 %shard_map.137 = (bf16[512,512]{1,0:T(8,128)(2,1)S(1)}, f32[32,512]{1,0:T(8,128)S(1)}) custom-call(bf16[512,512]{1,0:T(8,128)(2,1)S(1)} %get-tuple-element.52.stem_in, f32[4,32]{1,0:T(4,128)S(1)} %bitcast.11, f32[1,32]{1,0:T(1,128)S(1)} %bitcast.16, f32[1,32]{1,0:T(1,128)S(1)} %bitcast.19, bf16[32,288]{1,0:T(8,128)(2,1)S(1)} %copy-done.2, f32[1,32]{1,0:T(1,128)S(1)} %bitcast.22), custom_call_target="tpu_custom_call" | custom-call | flops 4000000000 | bytes 1048576 | tf_op jit(solution)/shard_map/pallas_call | solution.py:437
  8.1 0.0 collective-permute-done.1.outer
  8.2 0.2 multiply_reduce_fusion.2
  8.4 0.1 select_select_fusion.1
  8.5 0.0 copy-start
  8.5 0.0 copy-start.1
  8.5 0.0 copy-start.4
  8.5 0.0 copy-start.6
  8.5 0.0 copy-start.10
  8.5 2.8 %collective-permute-start.2 = (f32[8,640]{1,0:T(8,128)S(1)}, f32[8,640]{1,0:T(8,128)S(1)}, u32[]{:S(2)}, u32[]{:S(2)}) collective-permute-start(f32[8,640]{1,0:T(8,128)S(1)} %get-tuple-element.55), channel_id=1, source_target_pairs={{1,0},{9,8},{17,16},{25,24},{33,32},{41,40},{49,48},{57,56},{65,64... | collective-permute-start | bytes 61448 | tf_op jit(solution)/shard_map/ppermute | solution.py:461
  11.3 4.3 %collective-permute-start.3 = (f32[8,640]{1,0:T(8,128)S(1)}, f32[8,640]{1,0:T(8,128)S(1)}, u32[]{:S(2)}, u32[]{:S(2)}) collective-permute-start(f32[8,640]{1,0:T(8,128)S(1)} %get-tuple-element.56), channel_id=1, source_target_pairs={{7,0},{15,8},{23,16},{31,24},{39,32},{47,40},{55,48},{63,56},{71,6... | collective-permute-start | bytes 61448 | tf_op jit(solution)/shard_map/ppermute | solution.py:461
  15.6 3.6 %shard_map.138 = (bf16[1536,512]{1,0:T(8,128)(2,1)S(1)}, f32[32,1536]{1,0:T(8,128)S(1)}) custom-call(bf16[512,512]{1,0:T(8,128)(2,1)S(1)} %get-tuple-element.52.stem_in, f32[4,32]{1,0:T(4,128)S(1)} %bitcast.12, f32[1,32]{1,0:T(1,128)S(1)} %bitcast.17, f32[1,32]{1,0:T(1,128)S(1)} %bitcast.20, bf16[32,288]{1,0:T(8,128)(2,1)S(1)} %copy-done.2, f32[1,32]{1,0:T(1,128)S(1)} %bitcast.23), custom_call_target="tpu_custom_call" | custom-call | flops 4000000000 | bytes 1048576 | tf_op jit(solution)/shard_map/pallas_call | solution.py:437
  19.2 0.0 copy-start.3
  19.2 0.0 copy-start.11
  19.2 0.0 collective-permute-done.2.even_message
  19.3 0.0 collective-permute-done.3.odd_message
  19.3 1.7 %shard_map.139 = (bf16[64,512]{1,0:T(8,128)(2,1)S(1)}, bf16[32,256]{1,0:T(8,128)(2,1)S(1)}, bf16[32,2048]{1,0:T(8,128)(2,1)S(1)}, bf16[2,32,2048]{2,1,0:T(8,128)(2,1)S(1)}) custom-call(f32[32,512]{1,0:T(8,128)S(1)} %get-tuple-element.47.rows, f32[32,128]{1,0:T(8,128)S(1)} %get-tuple-element.54.cols, f32[16,128]{1,0:T(8,128)S(1)} %collective-permute-done.partner, ...), custom_call_target="tpu_custom_call" | custom-call | bytes 1048576 | tf_op jit(solution)/shard_map/pallas_call | solution.py:437
  21.0 0.1 collective-permute-start.4
  21.1 1.3 %collective-permute-done.4 = bf16[32,2048]{1,0:T(8,128)(2,1)S(1)} collective-permute-done((bf16[32,2048]{1,0:T(8,128)(2,1)S(1)}, bf16[32,2048]{1,0:T(8,128)(2,1)S(1)}, u32[]{:S(2)}, u32[]{:S(2)}) %collective-permute-start.4) | collective-permute-done | bytes 131104 | tf_op jit(solution)/shard_map/ppermute | solution.py:461
  22.4 0.1 collective-permute-start.5
  22.5 0.2 collective-permute-start.8
  22.7 4.9 %collective-permute-start.7 = (bf16[2,32,2048]{2,1,0:T(8,128)(2,1)S(1)}, bf16[2,32,2048]{2,1,0:T(8,128)(2,1)S(1)}, u32[]{:S(2)}, u32[]{:S(2)}) collective-permute-start(bf16[2,32,2048]{2,1,0:T(8,128)(2,1)S(1)} %bitcast_dynamic-update-slice_fusion.refs_0_), channel_id=1, source_target_pairs={{113,0},{31,8},{1,16},{47,24},{17,32},{63,40},{33,48},{79,56},{49,... | collective-permute-start | bytes 786440 | tf_op jit(solution)/shard_map/ppermute | solution.py:461
  27.6 9.6 %collective-permute-done.5.refs_1_ = bf16[2,32,2048]{2,1,0:T(8,128)(2,1)S(1)} collective-permute-done((bf16[2,32,2048]{2,1,0:T(8,128)(2,1)S(1)}, bf16[2,32,2048]{2,1,0:T(8,128)(2,1)S(1)}, u32[]{:S(2)}, u32[]{:S(2)}) %collective-permute-start.5) | collective-permute-done | bytes 262176 | tf_op jit(solution)/shard_map/ppermute | solution.py:461
  37.1 0.0 collective-permute-start.6
  37.2 0.0 collective-permute-start.12
  37.2 0.0 collective-permute-done.8.refs_2_
  37.2 0.5 collective-permute-start.11
  37.7 2.7 %shard_map.140 = (f32[128,2048]{1,0:T(8,128)S(1)}, bf16[160,640]{1,0:T(8,128)(2,1)S(1)}, bf16[40,128]{1,0:T(8,128)(2,1)S(1)}, f32[32,256]{1,0:T(8,128)S(1)}) custom-call(bf16[2,32,2048]{2,1,0:T(8,128)(2,1)S(1)} %bitcast_dynamic-update-slice_fusion.refs_0_, bf16[2,32,2048]{2,1,0:T(8,128)(2,1)S(1)} %collective-permute-done.5.refs_1_, ...), custom_call_target="tpu_custom_call" | custom-call | bytes 1048576 | tf_op jit(solution)/shard_map/pallas_call | solution.py:437
  40.4 0.0 collective-permute-done.7.two
  40.4 4.6 %collective-permute-done.6.relay = bf16[2,32,2048]{2,1,0:T(8,128)(2,1)S(1)} collective-permute-done((bf16[2,32,2048]{2,1,0:T(8,128)(2,1)S(1)}, bf16[2,32,2048]{2,1,0:T(8,128)(2,1)S(1)}, u32[]{:S(2)}, u32[]{:S(2)}) %collective-permute-start.6) | collective-permute-done | bytes 262176 | tf_op jit(solution)/shard_map/ppermute | solution.py:461
  45.1 0.5 collective-permute-start.9
  45.6 1.0 %collective-permute-done.10.relay_p = bf16[2,32,2048]{2,1,0:T(8,128)(2,1)S(1)} collective-permute-done((bf16[2,32,2048]{2,1,0:T(8,128)(2,1)S(1)}, bf16[2,32,2048]{2,1,0:T(8,128)(2,1)S(1)}, u32[]{:S(2)}, u32[]{:S(2)}) %collective-permute-start.10) | collective-permute-done | bytes 262176 | tf_op jit(solution)/shard_map/ppermute | solution.py:461
  46.6 0.4 collective-permute-done.9.two_p
  47.0 4.6 %shard_map.141 = (f32[2,64,512]{2,1,0:T(8,128)S(1)}, f32[72,128]{1,0:T(8,128)S(1)}, f32[8,512]{1,0:T(8,128)S(1)}) custom-call(bf16[512,512]{1,0:T(8,128)(2,1)S(1)} %get-tuple-element.46.low, bf16[1536,512]{1,0:T(8,128)(2,1)S(1)} %get-tuple-element.53.high, bf16[64,512]{1,0:T(8,128)(2,1)S(1)} %get-tuple-element.59.rim_rows, ...), custom_call_target="tpu_custom_call" | custom-call | bytes 1048576 | tf_op jit(solution)/shard_map/pallas_call | solution.py:437
  51.6 0.2 collective-permute-start.13
  51.8 0.0 collective-permute-start.14
  51.8 1.0 %collective-permute-done.13.partner = f32[72,128]{1,0:T(8,128)S(1)} collective-permute-done((f32[72,128]{1,0:T(8,128)S(1)}, f32[72,128]{1,0:T(8,128)S(1)}, u32[]{:S(2)}, u32[]{:S(2)}) %collective-permute-start.13) | collective-permute-done | bytes 36896 | tf_op jit(solution)/shard_map/ppermute | solution.py:461
  52.9 4.4 %collective-permute-done.14.outer = f32[72,128]{1,0:T(8,128)S(1)} collective-permute-done((f32[72,128]{1,0:T(8,128)S(1)}, f32[72,128]{1,0:T(8,128)S(1)}, u32[]{:S(2)}, u32[]{:S(2)}) %collective-permute-start.14) | collective-permute-done | bytes 36896 | tf_op jit(solution)/shard_map/ppermute | solution.py:461
  57.3 0.1 collective-permute-start.15
  57.4 4.1 %collective-permute-start.16 = (f32[8,512]{1,0:T(8,128)S(1)}, f32[8,512]{1,0:T(8,128)S(1)}, u32[]{:S(2)}, u32[]{:S(2)}) collective-permute-start(f32[8,512]{1,0:T(8,128)S(1)} %maximum_add_fusion), channel_id=1, source_target_pairs={{7,0},{15,8},{23,16},{31,24},{39,32},{47,40},{55,48},{63,56},{71,6... | collective-permute-start | bytes 49160 | tf_op jit(solution)/shard_map/ppermute | solution.py:461
  61.6 1.1 %collective-permute-done.15.even_message = f32[8,512]{1,0:T(8,128)S(1)} collective-permute-done((f32[8,512]{1,0:T(8,128)S(1)}, f32[8,512]{1,0:T(8,128)S(1)}, u32[]{:S(2)}, u32[]{:S(2)}) %collective-permute-start.15) | collective-permute-done | bytes 16416 | tf_op jit(solution)/shard_map/ppermute | solution.py:461
  62.6 2.2 %collective-permute-done.16.odd_message = f32[8,512]{1,0:T(8,128)S(1)} collective-permute-done((f32[8,512]{1,0:T(8,128)S(1)}, f32[8,512]{1,0:T(8,128)S(1)}, u32[]{:S(2)}, u32[]{:S(2)}) %collective-permute-start.16) | collective-permute-done | bytes 16416 | tf_op jit(solution)/shard_map/ppermute | solution.py:461
  64.8 0.8 %shard_map.142 = f32[2,64,512]{2,1,0:T(8,128)} custom-call(f32[2,64,512]{2,1,0:T(8,128)S(1)} %get-tuple-element.70.inner, f32[72,128]{1,0:T(8,128)S(1)} %collective-permute-done.13.partner, f32[72,128]{1,0:T(8,128)S(1)} %collective-permute-done.14.outer, f32[8,512]{1,0:T(8,128)S(1)} %collective-permute-done.15.even_message, ...), custom_call_target="tpu_custom_call" | custom-call | bytes 1048576 | tf_op jit(solution)/shard_map/pallas_call | solution.py:437
  (33 shorter events, 0.1 us)
Async XLA Ops:
  0.0 6.5 %copy-start.5 = (f32[32,4]{0,1:T(4,128)S(1)}, f32[32,4]{0,1:T(4,128)}, u32[]{:S(2)}) copy-start(f32[32,4]{0,1:T(4,128)} %param.18) | copy-start | bytes 1540
  0.0 6.5 %copy-start.7 = (f32[32]{0:T(128)S(1)}, f32[32]{0:T(128)}, u32[]{:S(2)}) copy-start(f32[32]{0:T(128)} %param.19) | copy-start | bytes 388
  0.0 6.5 %copy-start.8 = (f32[32]{0:T(128)S(1)}, f32[32]{0:T(128)}, u32[]{:S(2)}) copy-start(f32[32]{0:T(128)} %param.20) | copy-start | bytes 388
  0.0 6.5 %copy-start.9 = (f32[32]{0:T(128)S(1)}, f32[32]{0:T(128)}, u32[]{:S(2)}) copy-start(f32[32]{0:T(128)} %param.22) | copy-start | bytes 388
  0.0 6.5 %copy-start.2 = (bf16[32,288]{1,0:T(8,128)(2,1)S(1)}, bf16[32,288]{1,0:T(8,128)(2,1)}, u32[]{:S(2)}) copy-start(bf16[32,288]{1,0:T(8,128)(2,1)} %conv_w.5) | copy-start | bytes 55300
  0.0 1.1 %copy-start.12 = (s32[4,64,512]{2,1,0:T(8,128)S(1)}, s32[4,64,512]{2,1,0:T(8,128)}, u32[]{:S(2)}) copy-start(s32[4,64,512]{2,1,0:T(8,128)} %rasters.1) | copy-start | bytes 1572868
  1.1 0.9 %copy-start.13 = (f32[64,512]{1,0:T(8,128)S(1)}, f32[64,512]{1,0:T(8,128)}, u32[]{:S(2)}) copy-start(f32[64,512]{1,0:T(8,128)} %aerial.1) | copy-start | bytes 393220
  2.3 5.8 %collective-permute-start = (f32[16,128]{1,0:T(8,128)S(1)}, f32[16,128]{1,0:T(8,128)S(1)}, u32[]{:S(2)}, u32[]{:S(2)}) collective-permute-start(f32[16,128]{1,0:T(8,128)S(1)} %get-tuple-element.48), channel_id=1, source_target_pairs={{8,0},{0,8},{24,16},{16,24},{40,32},{32,40},{56,48},{48,56},{72,64... | collective-permute-start | bytes 24584 | tf_op jit(solution)/shard_map/ppermute | solution.py:461
  2.4 5.8 %collective-permute-start.1 = (f32[16,128]{1,0:T(8,128)S(1)}, f32[16,128]{1,0:T(8,128)S(1)}, u32[]{:S(2)}, u32[]{:S(2)}) collective-permute-start(f32[16,128]{1,0:T(8,128)S(1)} %get-tuple-element.48), channel_id=1, source_target_pairs={{120,0},{16,8},{8,16},{32,24},{24,32},{48,40},{40,48},{64,56},{56,... | collective-permute-start | bytes 24584 | tf_op jit(solution)/shard_map/ppermute | solution.py:461
  8.5 29.2 %copy-start = (bf16[128,1920]{1,0:T(8,128)(2,1)S(1)}, bf16[128,1920]{1,0:T(8,128)(2,1)}, u32[]{:S(2)}) copy-start(bf16[128,1920]{1,0:T(8,128)(2,1)} %ctx_w.1) | copy-start | bytes 1474564
  8.5 29.2 %copy-start.1 = (bf16[128,32]{0,1:T(8,128)(2,1)S(1)}, bf16[128,32]{0,1:T(8,128)(2,1)}, u32[]{:S(2)}) copy-start(bf16[128,32]{0,1:T(8,128)(2,1)} %param.23) | copy-start | bytes 24580
  8.5 29.2 %copy-start.4 = (bf16[2,800]{1,0:T(2,128)(2,1)S(1)}, bf16[2,800]{1,0:T(2,128)(2,1)}, u32[]{:S(2)}) copy-start(bf16[2,800]{1,0:T(2,128)(2,1)} %refs_6_.1) | copy-start | bytes 9604
  8.5 29.2 %copy-start.6 = (f32[128]{0:T(128)S(1)}, f32[128]{0:T(128)}, u32[]{:S(2)}) copy-start(f32[128]{0:T(128)} %param.24) | copy-start | bytes 1540
  8.5 29.2 %copy-start.10 = (f32[32]{0:T(128)S(1)}, f32[32]{0:T(128)}, u32[]{:S(2)}) copy-start(f32[32]{0:T(128)} %param.27) | copy-start | bytes 388
  8.5 10.7 %collective-permute-start.2 = (f32[8,640]{1,0:T(8,128)S(1)}, f32[8,640]{1,0:T(8,128)S(1)}, u32[]{:S(2)}, u32[]{:S(2)}) collective-permute-start(f32[8,640]{1,0:T(8,128)S(1)} %get-tuple-element.55), channel_id=1, source_target_pairs={{1,0},{9,8},{17,16},{25,24},{33,32},{41,40},{49,48},{57,56},{65,64... | collective-permute-start | bytes 61448 | tf_op jit(solution)/shard_map/ppermute | solution.py:461
  11.3 7.9 %collective-permute-start.3 = (f32[8,640]{1,0:T(8,128)S(1)}, f32[8,640]{1,0:T(8,128)S(1)}, u32[]{:S(2)}, u32[]{:S(2)}) collective-permute-start(f32[8,640]{1,0:T(8,128)S(1)} %get-tuple-element.56), channel_id=1, source_target_pairs={{7,0},{15,8},{23,16},{31,24},{39,32},{47,40},{55,48},{63,56},{71,6... | collective-permute-start | bytes 61448 | tf_op jit(solution)/shard_map/ppermute | solution.py:461
  19.2 27.7 %copy-start.3 = (bf16[32,128]{1,0:T(8,128)(2,1)S(1)}, bf16[32,128]{1,0:T(8,128)(2,1)}, u32[]{:S(2)}) copy-start(bf16[32,128]{1,0:T(8,128)(2,1)} %up_w.1) | copy-start | bytes 24580
  19.2 27.7 %copy-start.11 = (f32[2]{0:T(128)S(1)}, f32[2]{0:T(128)}, u32[]{:S(2)}) copy-start(f32[2]{0:T(128)} %head_b.1) | copy-start | bytes 28
  21.0 1.4 %collective-permute-start.4 = (bf16[32,2048]{1,0:T(8,128)(2,1)S(1)}, bf16[32,2048]{1,0:T(8,128)(2,1)S(1)}, u32[]{:S(2)}, u32[]{:S(2)}) collective-permute-start(bf16[32,2048]{1,0:T(8,128)(2,1)S(1)} %get-tuple-element.62), channel_id=1, source_target_pairs={{8,0},{0,8},{24,16},{16,24},{40,32},{32,40},{56,48},{48,56},{72,64... | collective-permute-start | bytes 393224 | tf_op jit(solution)/shard_map/ppermute | solution.py:461
  22.4 14.7 %collective-permute-start.5 = (bf16[2,32,2048]{2,1,0:T(8,128)(2,1)S(1)}, bf16[2,32,2048]{2,1,0:T(8,128)(2,1)S(1)}, u32[]{:S(2)}, u32[]{:S(2)}) collective-permute-start(bf16[2,32,2048]{2,1,0:T(8,128)(2,1)S(1)} %bitcast_dynamic-update-slice_fusion.refs_0_), channel_id=1, source_target_pairs={{119,0},{25,8},{7,16},{41,24},{23,32},{57,40},{39,48},{73,56},{55,... | collective-permute-start | bytes 786440 | tf_op jit(solution)/shard_map/ppermute | solution.py:461
  22.5 14.7 %collective-permute-start.8 = (bf16[2,32,2048]{2,1,0:T(8,128)(2,1)S(1)}, bf16[2,32,2048]{2,1,0:T(8,128)(2,1)S(1)}, u32[]{:S(2)}, u32[]{:S(2)}) collective-permute-start(bf16[2,32,2048]{2,1,0:T(8,128)(2,1)S(1)} %bitcast_dynamic-update-slice_fusion.refs_0_), channel_id=1, source_target_pairs={{112,0},{24,8},{0,16},{40,24},{16,32},{56,40},{32,48},{72,56},{48,... | collective-permute-start | bytes 786440 | tf_op jit(solution)/shard_map/ppermute | solution.py:461
  22.7 17.7 %collective-permute-start.7 = (bf16[2,32,2048]{2,1,0:T(8,128)(2,1)S(1)}, bf16[2,32,2048]{2,1,0:T(8,128)(2,1)S(1)}, u32[]{:S(2)}, u32[]{:S(2)}) collective-permute-start(bf16[2,32,2048]{2,1,0:T(8,128)(2,1)S(1)} %bitcast_dynamic-update-slice_fusion.refs_0_), channel_id=1, source_target_pairs={{113,0},{31,8},{1,16},{47,24},{17,32},{63,40},{33,48},{79,56},{49,... | collective-permute-start | bytes 786440 | tf_op jit(solution)/shard_map/ppermute | solution.py:461
  37.1 7.9 %collective-permute-start.6 = (bf16[2,32,2048]{2,1,0:T(8,128)(2,1)S(1)}, bf16[2,32,2048]{2,1,0:T(8,128)(2,1)S(1)}, u32[]{:S(2)}, u32[]{:S(2)}) collective-permute-start(bf16[2,32,2048]{2,1,0:T(8,128)(2,1)S(1)} %collective-permute-done.5.refs_1_), channel_id=1, source_target_pairs={{120,0},{16,8},{8,16},{32,24},{24,32},{48,40},{40,48},{64,56},{56,... | collective-permute-start | bytes 786440 | tf_op jit(solution)/shard_map/ppermute | solution.py:461
  37.2 8.4 %collective-permute-start.12 = (bf16[2,32,2048]{2,1,0:T(8,128)(2,1)S(1)}, bf16[2,32,2048]{2,1,0:T(8,128)(2,1)S(1)}, u32[]{:S(2)}, u32[]{:S(2)}) collective-permute-start(bf16[2,32,2048]{2,1,0:T(8,128)(2,1)S(1)} %collective-permute-done.5.refs_1_), channel_id=1, source_target_pairs={{8,0},{0,8},{24,16},{16,24},{40,32},{32,40},{56,48},{48,56},{72,64... | collective-permute-start | bytes 786440 | tf_op jit(solution)/shard_map/ppermute | solution.py:461
  37.2 8.4 %collective-permute-start.11 = (bf16[2,32,2048]{2,1,0:T(8,128)(2,1)S(1)}, bf16[2,32,2048]{2,1,0:T(8,128)(2,1)S(1)}, u32[]{:S(2)}, u32[]{:S(2)}) collective-permute-start(bf16[2,32,2048]{2,1,0:T(8,128)(2,1)S(1)} %collective-permute-done.8.refs_2_), channel_id=1, source_target_pairs={{8,0},{0,8},{24,16},{16,24},{40,32},{32,40},{56,48},{48,56},{72,64... | collective-permute-start | bytes 786440 | tf_op jit(solution)/shard_map/ppermute | solution.py:461
  45.1 1.5 %collective-permute-start.10 = (bf16[2,32,2048]{2,1,0:T(8,128)(2,1)S(1)}, bf16[2,32,2048]{2,1,0:T(8,128)(2,1)S(1)}, u32[]{:S(2)}, u32[]{:S(2)}) collective-permute-start(bf16[2,32,2048]{2,1,0:T(8,128)(2,1)S(1)} %collective-permute-done.6.relay), channel_id=1, source_target_pairs={{8,0},{0,8},{24,16},{16,24},{40,32},{32,40},{56,48},{48,56},{72,64... | collective-permute-start | bytes 786440 | tf_op jit(solution)/shard_map/ppermute | solution.py:461
  45.1 1.9 %collective-permute-start.9 = (bf16[2,32,2048]{2,1,0:T(8,128)(2,1)S(1)}, bf16[2,32,2048]{2,1,0:T(8,128)(2,1)S(1)}, u32[]{:S(2)}, u32[]{:S(2)}) collective-permute-start(bf16[2,32,2048]{2,1,0:T(8,128)(2,1)S(1)} %collective-permute-done.7.two), channel_id=1, source_target_pairs={{8,0},{0,8},{24,16},{16,24},{40,32},{32,40},{56,48},{48,56},{72,64... | collective-permute-start | bytes 786440 | tf_op jit(solution)/shard_map/ppermute | solution.py:461
  51.6 1.3 %collective-permute-start.13 = (f32[72,128]{1,0:T(8,128)S(1)}, f32[72,128]{1,0:T(8,128)S(1)}, u32[]{:S(2)}, u32[]{:S(2)}) collective-permute-start(f32[72,128]{1,0:T(8,128)S(1)} %get-tuple-element.71), channel_id=1, source_target_pairs={{8,0},{0,8},{24,16},{16,24},{40,32},{32,40},{56,48},{48,56},{72,64... | collective-permute-start | bytes 110600 | tf_op jit(solution)/shard_map/ppermute | solution.py:461
  51.8 5.5 %collective-permute-start.14 = (f32[72,128]{1,0:T(8,128)S(1)}, f32[72,128]{1,0:T(8,128)S(1)}, u32[]{:S(2)}, u32[]{:S(2)}) collective-permute-start(f32[72,128]{1,0:T(8,128)S(1)} %get-tuple-element.71), channel_id=1, source_target_pairs={{120,0},{16,8},{8,16},{32,24},{24,32},{48,40},{40,48},{64,56},{56,... | collective-permute-start | bytes 110600 | tf_op jit(solution)/shard_map/ppermute | solution.py:461
  57.3 5.3 %collective-permute-start.15 = (f32[8,512]{1,0:T(8,128)S(1)}, f32[8,512]{1,0:T(8,128)S(1)}, u32[]{:S(2)}, u32[]{:S(2)}) collective-permute-start(f32[8,512]{1,0:T(8,128)S(1)} %maximum_add_fusion), channel_id=1, source_target_pairs={{1,0},{9,8},{17,16},{25,24},{33,32},{41,40},{49,48},{57,56},{65,64... | collective-permute-start | bytes 49160 | tf_op jit(solution)/shard_map/ppermute | solution.py:461
  57.4 7.4 %collective-permute-start.16 = (f32[8,512]{1,0:T(8,128)S(1)}, f32[8,512]{1,0:T(8,128)S(1)}, u32[]{:S(2)}, u32[]{:S(2)}) collective-permute-start(f32[8,512]{1,0:T(8,128)S(1)} %maximum_add_fusion), channel_id=1, source_target_pairs={{7,0},{15,8},{23,16},{31,24},{39,32},{47,40},{55,48},{63,56},{71,6... | collective-permute-start | bytes 49160 | tf_op jit(solution)/shard_map/ppermute | solution.py:461

commit v7 on v6

--- a/solution.py
+++ b/solution.py
@@ -11,7 +11,7 @@
 CH, WIDE, KINDS = 32, 128, 8
 POOL_ROWS, POOL_COLS = 16, 128
 SPOTS = POOL_ROWS * POOL_COLS
-FIRST = 16
+FIRST = 8
 HBM = pl.BlockSpec(memory_space=pltpu.HBM)
 VMEM = pl.BlockSpec(memory_space=pltpu.VMEM)
 SMEM = pl.BlockSpec(memory_space=pltpu.SMEM)
@@ -534,7 +534,7 @@
         ],
         [*(sent[name] for name in PHASES[0]), *proj_args, w_head, b_up[None, :]],
     )
-    relay, two, context = tie((relay, two, context))
+    relay, context = tie((relay, context))
     relay_p, two_p = partner(relay), partner(two)
     band_p, one_p = partner(band), partner(one)
 

time: 65.8 us -> 65.3 us (level)
  transfers between devices with their start and end apart: 17 -> 17, of which waited for: 9 -> 10; matrix products, arithmetic and copies ran while one was open for 0% -> 0% of each run, Pallas kernels for 12% -> 12%
where the time goes in v7:
time: 65.3 us; the launch traced here: 65.2 us
  waiting for transfers between devices  25.3 us (39%)
  starting transfers between devices  21.8 us (33%)
  Pallas kernels  15.3 us (23%)
  local copies, waits for them, and re-layouts  2.09 us (3%)
    ppermute x17, waiting for transfers between devices, moved(): return lax.ppermute(x, ('band', 'cross'), route)  25.3 us
    ppermute x17, starting transfers between devices, moved(): return lax.ppermute(x, ('band', 'cross'), route)  21.8 us
    pallas_call x7, Pallas kernels, call(): pl.pallas_call(fetching if hbm else kernel, out_shape=outs, in_specs=[SME...  15.3 us
    unnamed x28, local copies, waits for them, and re-layouts  2.07 us
  transfers between devices with their start and end apart: 17, of which 10 were waited for; matrix products, arithmetic and copies ran while one was open for 0% of the time, Pallas kernels for 12%

profile of v7, /device:TPU:0, one launch (start us, length us, event | category | flops | bytes accessed | tf_op | source)
XLA Modules:
  0.0 65.2 jit_solution(18278963761350327348)
XLA Ops:
  0.0 1.1 %copy-done.12 = s32[4,64,512]{2,1,0:T(8,128)S(1)} copy-done((s32[4,64,512]{2,1,0:T(8,128)S(1)}, s32[4,64,512]{2,1,0:T(8,128)}, u32[]{:S(2)}) %copy-start.12) | copy-done | bytes 524312
  1.1 0.9 %copy-done.13 = f32[64,512]{1,0:T(8,128)S(1)} copy-done((f32[64,512]{1,0:T(8,128)S(1)}, f32[64,512]{1,0:T(8,128)}, u32[]{:S(2)}) %copy-start.13) | copy-done | bytes 131096
  2.0 0.3 shard_map.136
  2.3 0.1 collective-permute-start
  2.4 4.1 %collective-permute-start.1 = (f32[16,128]{1,0:T(8,128)S(1)}, f32[16,128]{1,0:T(8,128)S(1)}, u32[]{:S(2)}, u32[]{:S(2)}) collective-permute-start(f32[16,128]{1,0:T(8,128)S(1)} %get-tuple-element.47), channel_id=1, source_target_pairs={{120,0},{16,8},{8,16},{32,24},{24,32},{48,40},{40,48},{64,56},{56,... | collective-permute-start | bytes 24584 | tf_op jit(solution)/shard_map/ppermute | solution.py:461
  6.6 1.1 %shard_map.137 = (bf16[256,512]{1,0:T(8,128)(2,1)S(1)}, f32[32,256]{1,0:T(8,128)S(1)}) custom-call(bf16[512,512]{1,0:T(8,128)(2,1)S(1)} %get-tuple-element.51.stem_in, f32[4,32]{1,0:T(4,128)S(1)} %bitcast.11, f32[1,32]{1,0:T(1,128)S(1)} %bitcast.16, f32[1,32]{1,0:T(1,128)S(1)} %bitcast.19, bf16[32,288]{1,0:T(8,128)(2,1)S(1)} %copy-done.2, f32[1,32]{1,0:T(1,128)S(1)} %bitcast.22), custom_call_target="tpu_custom_call" | custom-call | flops 4000000000 | bytes 1048576 | tf_op jit(solution)/shard_map/pallas_call | solution.py:437
  7.7 0.0 collective-permute-done.partner
  7.7 0.2 collective-permute-done.1.outer
  7.9 0.2 multiply_reduce_fusion.2
  8.1 0.1 select_select_fusion.1
  8.2 0.0 copy-start
  8.2 0.0 copy-start.1
  8.2 0.0 copy-start.4
  8.2 0.0 copy-start.6
  8.2 0.0 copy-start.10
  8.3 3.0 %collective-permute-start.2 = (f32[8,640]{1,0:T(8,128)S(1)}, f32[8,640]{1,0:T(8,128)S(1)}, u32[]{:S(2)}, u32[]{:S(2)}) collective-permute-start(f32[8,640]{1,0:T(8,128)S(1)} %get-tuple-element.54), channel_id=1, source_target_pairs={{1,0},{9,8},{17,16},{25,24},{33,32},{41,40},{49,48},{57,56},{65,64... | collective-permute-start | bytes 61448 | tf_op jit(solution)/shard_map/ppermute | solution.py:461
  11.2 4.1 %collective-permute-start.3 = (f32[8,640]{1,0:T(8,128)S(1)}, f32[8,640]{1,0:T(8,128)S(1)}, u32[]{:S(2)}, u32[]{:S(2)}) collective-permute-start(f32[8,640]{1,0:T(8,128)S(1)} %get-tuple-element.55), channel_id=1, source_target_pairs={{7,0},{15,8},{23,16},{31,24},{39,32},{47,40},{55,48},{63,56},{71,6... | collective-permute-start | bytes 61448 | tf_op jit(solution)/shard_map/ppermute | solution.py:461
  15.3 4.1 %shard_map.138 = (bf16[1792,512]{1,0:T(8,128)(2,1)S(1)}, f32[32,1792]{1,0:T(8,128)S(1)}) custom-call(bf16[512,512]{1,0:T(8,128)(2,1)S(1)} %get-tuple-element.51.stem_in, f32[4,32]{1,0:T(4,128)S(1)} %bitcast.12, f32[1,32]{1,0:T(1,128)S(1)} %bitcast.17, f32[1,32]{1,0:T(1,128)S(1)} %bitcast.20, bf16[32,288]{1,0:T(8,128)(2,1)S(1)} %copy-done.2, f32[1,32]{1,0:T(1,128)S(1)} %bitcast.23), custom_call_target="tpu_custom_call" | custom-call | flops 4000000000 | bytes 1048576 | tf_op jit(solution)/shard_map/pallas_call | solution.py:437
  19.4 0.0 copy-start.3
  19.4 0.0 copy-start.11
  19.4 0.0 collective-permute-done.2.even_message
  19.5 1.7 %shard_map.139 = (bf16[64,512]{1,0:T(8,128)(2,1)S(1)}, bf16[32,256]{1,0:T(8,128)(2,1)S(1)}, bf16[32,2048]{1,0:T(8,128)(2,1)S(1)}, bf16[2,32,2048]{2,1,0:T(8,128)(2,1)S(1)}) custom-call(f32[32,512]{1,0:T(8,128)S(1)} %get-tuple-element.46.rows, f32[32,128]{1,0:T(8,128)S(1)} %get-tuple-element.53.cols, f32[16,128]{1,0:T(8,128)S(1)} %collective-permute-done.partner, ...), custom_call_target="tpu_custom_call" | custom-call | bytes 1048576 | tf_op jit(solution)/shard_map/pallas_call | solution.py:437
  21.2 0.1 collective-permute-start.4
  21.3 1.3 %collective-permute-done.4 = bf16[32,2048]{1,0:T(8,128)(2,1)S(1)} collective-permute-done((bf16[32,2048]{1,0:T(8,128)(2,1)S(1)}, bf16[32,2048]{1,0:T(8,128)(2,1)S(1)}, u32[]{:S(2)}, u32[]{:S(2)}) %collective-permute-start.4) | collective-permute-done | bytes 131104 | tf_op jit(solution)/shard_map/ppermute | solution.py:461
  22.6 0.1 collective-permute-start.5
  22.7 0.5 collective-permute-start.7
  23.2 4.9 %collective-permute-start.8 = (bf16[2,32,2048]{2,1,0:T(8,128)(2,1)S(1)}, bf16[2,32,2048]{2,1,0:T(8,128)(2,1)S(1)}, u32[]{:S(2)}, u32[]{:S(2)}) collective-permute-start(bf16[2,32,2048]{2,1,0:T(8,128)(2,1)S(1)} %bitcast_dynamic-update-slice_fusion.refs_0_), channel_id=1, source_target_pairs={{113,0},{31,8},{1,16},{47,24},{17,32},{63,40},{33,48},{79,56},{49,... | collective-permute-start | bytes 786440 | tf_op jit(solution)/shard_map/ppermute | solution.py:461
  28.1 9.0 %collective-permute-done.5.refs_1_ = bf16[2,32,2048]{2,1,0:T(8,128)(2,1)S(1)} collective-permute-done((bf16[2,32,2048]{2,1,0:T(8,128)(2,1)S(1)}, bf16[2,32,2048]{2,1,0:T(8,128)(2,1)S(1)}, u32[]{:S(2)}, u32[]{:S(2)}) %collective-permute-start.5) | collective-permute-done | bytes 262176 | tf_op jit(solution)/shard_map/ppermute | solution.py:461
  37.1 0.5 collective-permute-start.11
  37.6 1.4 %collective-permute-done.8.two = bf16[2,32,2048]{2,1,0:T(8,128)(2,1)S(1)} collective-permute-done((bf16[2,32,2048]{2,1,0:T(8,128)(2,1)S(1)}, bf16[2,32,2048]{2,1,0:T(8,128)(2,1)S(1)}, u32[]{:S(2)}, u32[]{:S(2)}) %collective-permute-start.8) | collective-permute-done | bytes 262176 | tf_op jit(solution)/shard_map/ppermute | solution.py:461
  39.0 0.1 collective-permute-start.9
  39.1 2.7 %shard_map.140 = (f32[128,2048]{1,0:T(8,128)S(1)}, bf16[160,640]{1,0:T(8,128)(2,1)S(1)}, bf16[40,128]{1,0:T(8,128)(2,1)S(1)}, f32[32,256]{1,0:T(8,128)S(1)}) custom-call(bf16[2,32,2048]{2,1,0:T(8,128)(2,1)S(1)} %bitcast_dynamic-update-slice_fusion.refs_0_, bf16[2,32,2048]{2,1,0:T(8,128)(2,1)S(1)} %collective-permute-done.5.refs_1_, ...), custom_call_target="tpu_custom_call" | custom-call | bytes 1048576 | tf_op jit(solution)/shard_map/pallas_call | solution.py:437
  41.8 3.2 %collective-permute-done.6.relay = bf16[2,32,2048]{2,1,0:T(8,128)(2,1)S(1)} collective-permute-done((bf16[2,32,2048]{2,1,0:T(8,128)(2,1)S(1)}, bf16[2,32,2048]{2,1,0:T(8,128)(2,1)S(1)}, u32[]{:S(2)}, u32[]{:S(2)}) %collective-permute-start.6) | collective-permute-done | bytes 262176 | tf_op jit(solution)/shard_map/ppermute | solution.py:461
  45.0 0.0 collective-permute-start.10
  45.0 0.0 collective-permute-done.11.band_p
  45.0 0.0 collective-permute-done.12.one_p
  45.0 0.0 collective-permute-done.9.two_p
  45.0 1.5 %collective-permute-done.10.relay_p = bf16[2,32,2048]{2,1,0:T(8,128)(2,1)S(1)} collective-permute-done((bf16[2,32,2048]{2,1,0:T(8,128)(2,1)S(1)}, bf16[2,32,2048]{2,1,0:T(8,128)(2,1)S(1)}, u32[]{:S(2)}, u32[]{:S(2)}) %collective-permute-start.10) | collective-permute-done | bytes 262176 | tf_op jit(solution)/shard_map/ppermute | solution.py:461
  46.5 4.6 %shard_map.141 = (f32[2,64,512]{2,1,0:T(8,128)S(1)}, f32[72,128]{1,0:T(8,128)S(1)}, f32[8,512]{1,0:T(8,128)S(1)}) custom-call(bf16[256,512]{1,0:T(8,128)(2,1)S(1)} %get-tuple-element.45.low, bf16[1792,512]{1,0:T(8,128)(2,1)S(1)} %get-tuple-element.52.high, bf16[64,512]{1,0:T(8,128)(2,1)S(1)} %get-tuple-element.58.rim_rows, ...), custom_call_target="tpu_custom_call" | custom-call | bytes 1048576 | tf_op jit(solution)/shard_map/pallas_call | solution.py:437
  51.2 0.2 collective-permute-start.13
  51.3 0.0 collective-permute-start.14
  51.4 1.1 %collective-permute-done.13.partner = f32[72,128]{1,0:T(8,128)S(1)} collective-permute-done((f32[72,128]{1,0:T(8,128)S(1)}, f32[72,128]{1,0:T(8,128)S(1)}, u32[]{:S(2)}, u32[]{:S(2)}) %collective-permute-start.13) | collective-permute-done | bytes 36896 | tf_op jit(solution)/shard_map/ppermute | solution.py:461
  52.4 4.4 %collective-permute-done.14.outer = f32[72,128]{1,0:T(8,128)S(1)} collective-permute-done((f32[72,128]{1,0:T(8,128)S(1)}, f32[72,128]{1,0:T(8,128)S(1)}, u32[]{:S(2)}, u32[]{:S(2)}) %collective-permute-start.14) | collective-permute-done | bytes 36896 | tf_op jit(solution)/shard_map/ppermute | solution.py:461
  56.9 0.1 collective-permute-start.15
  56.9 4.1 %collective-permute-start.16 = (f32[8,512]{1,0:T(8,128)S(1)}, f32[8,512]{1,0:T(8,128)S(1)}, u32[]{:S(2)}, u32[]{:S(2)}) collective-permute-start(f32[8,512]{1,0:T(8,128)S(1)} %maximum_add_fusion), channel_id=1, source_target_pairs={{7,0},{15,8},{23,16},{31,24},{39,32},{47,40},{55,48},{63,56},{71,6... | collective-permute-start | bytes 49160 | tf_op jit(solution)/shard_map/ppermute | solution.py:461
  61.1 1.1 %collective-permute-done.15.even_message = f32[8,512]{1,0:T(8,128)S(1)} collective-permute-done((f32[8,512]{1,0:T(8,128)S(1)}, f32[8,512]{1,0:T(8,128)S(1)}, u32[]{:S(2)}, u32[]{:S(2)}) %collective-permute-start.15) | collective-permute-done | bytes 16416 | tf_op jit(solution)/shard_map/ppermute | solution.py:461
  62.2 2.2 %collective-permute-done.16.odd_message = f32[8,512]{1,0:T(8,128)S(1)} collective-permute-done((f32[8,512]{1,0:T(8,128)S(1)}, f32[8,512]{1,0:T(8,128)S(1)}, u32[]{:S(2)}, u32[]{:S(2)}) %collective-permute-start.16) | collective-permute-done | bytes 16416 | tf_op jit(solution)/shard_map/ppermute | solution.py:461
  64.4 0.8 %shard_map.142 = f32[2,64,512]{2,1,0:T(8,128)} custom-call(f32[2,64,512]{2,1,0:T(8,128)S(1)} %get-tuple-element.68.inner, f32[72,128]{1,0:T(8,128)S(1)} %collective-permute-done.13.partner, f32[72,128]{1,0:T(8,128)S(1)} %collective-permute-done.14.outer, f32[8,512]{1,0:T(8,128)S(1)} %collective-permute-done.15.even_message, ...), custom_call_target="tpu_custom_call" | custom-call | bytes 1048576 | tf_op jit(solution)/shard_map/pallas_call | solution.py:437
  (33 shorter events, 0.1 us)
Async XLA Ops:
  0.0 6.5 %copy-start.5 = (f32[32,4]{0,1:T(4,128)S(1)}, f32[32,4]{0,1:T(4,128)}, u32[]{:S(2)}) copy-start(f32[32,4]{0,1:T(4,128)} %param.18) | copy-start | bytes 1540
  0.0 6.5 %copy-start.7 = (f32[32]{0:T(128)S(1)}, f32[32]{0:T(128)}, u32[]{:S(2)}) copy-start(f32[32]{0:T(128)} %param.19) | copy-start | bytes 388
  0.0 6.5 %copy-start.8 = (f32[32]{0:T(128)S(1)}, f32[32]{0:T(128)}, u32[]{:S(2)}) copy-start(f32[32]{0:T(128)} %param.20) | copy-start | bytes 388
  0.0 6.5 %copy-start.9 = (f32[32]{0:T(128)S(1)}, f32[32]{0:T(128)}, u32[]{:S(2)}) copy-start(f32[32]{0:T(128)} %param.22) | copy-start | bytes 388
  0.0 6.5 %copy-start.2 = (bf16[32,288]{1,0:T(8,128)(2,1)S(1)}, bf16[32,288]{1,0:T(8,128)(2,1)}, u32[]{:S(2)}) copy-start(bf16[32,288]{1,0:T(8,128)(2,1)} %conv_w.5) | copy-start | bytes 55300
  0.0 1.1 %copy-start.12 = (s32[4,64,512]{2,1,0:T(8,128)S(1)}, s32[4,64,512]{2,1,0:T(8,128)}, u32[]{:S(2)}) copy-start(s32[4,64,512]{2,1,0:T(8,128)} %rasters.1) | copy-start | bytes 1572868
  1.1 0.9 %copy-start.13 = (f32[64,512]{1,0:T(8,128)S(1)}, f32[64,512]{1,0:T(8,128)}, u32[]{:S(2)}) copy-start(f32[64,512]{1,0:T(8,128)} %aerial.1) | copy-start | bytes 393220
  2.3 5.4 %collective-permute-start = (f32[16,128]{1,0:T(8,128)S(1)}, f32[16,128]{1,0:T(8,128)S(1)}, u32[]{:S(2)}, u32[]{:S(2)}) collective-permute-start(f32[16,128]{1,0:T(8,128)S(1)} %get-tuple-element.47), channel_id=1, source_target_pairs={{8,0},{0,8},{24,16},{16,24},{40,32},{32,40},{56,48},{48,56},{72,64... | collective-permute-start | bytes 24584 | tf_op jit(solution)/shard_map/ppermute | solution.py:461
  2.4 5.5 %collective-permute-start.1 = (f32[16,128]{1,0:T(8,128)S(1)}, f32[16,128]{1,0:T(8,128)S(1)}, u32[]{:S(2)}, u32[]{:S(2)}) collective-permute-start(f32[16,128]{1,0:T(8,128)S(1)} %get-tuple-element.47), channel_id=1, source_target_pairs={{120,0},{16,8},{8,16},{32,24},{24,32},{48,40},{40,48},{64,56},{56,... | collective-permute-start | bytes 24584 | tf_op jit(solution)/shard_map/ppermute | solution.py:461
  8.2 30.9 %copy-start = (bf16[128,1920]{1,0:T(8,128)(2,1)S(1)}, bf16[128,1920]{1,0:T(8,128)(2,1)}, u32[]{:S(2)}) copy-start(bf16[128,1920]{1,0:T(8,128)(2,1)} %ctx_w.1) | copy-start | bytes 1474564
  8.2 30.9 %copy-start.1 = (bf16[128,32]{0,1:T(8,128)(2,1)S(1)}, bf16[128,32]{0,1:T(8,128)(2,1)}, u32[]{:S(2)}) copy-start(bf16[128,32]{0,1:T(8,128)(2,1)} %param.23) | copy-start | bytes 24580
  8.2 30.9 %copy-start.4 = (bf16[2,800]{1,0:T(2,128)(2,1)S(1)}, bf16[2,800]{1,0:T(2,128)(2,1)}, u32[]{:S(2)}) copy-start(bf16[2,800]{1,0:T(2,128)(2,1)} %refs_6_.1) | copy-start | bytes 9604
  8.2 30.9 %copy-start.6 = (f32[128]{0:T(128)S(1)}, f32[128]{0:T(128)}, u32[]{:S(2)}) copy-start(f32[128]{0:T(128)} %param.24) | copy-start | bytes 1540
  8.2 30.9 %copy-start.10 = (f32[32]{0:T(128)S(1)}, f32[32]{0:T(128)}, u32[]{:S(2)}) copy-start(f32[32]{0:T(128)} %param.27) | copy-start | bytes 388
  8.3 11.2 %collective-permute-start.2 = (f32[8,640]{1,0:T(8,128)S(1)}, f32[8,640]{1,0:T(8,128)S(1)}, u32[]{:S(2)}, u32[]{:S(2)}) collective-permute-start(f32[8,640]{1,0:T(8,128)S(1)} %get-tuple-element.54), channel_id=1, source_target_pairs={{1,0},{9,8},{17,16},{25,24},{33,32},{41,40},{49,48},{57,56},{65,64... | collective-permute-start | bytes 61448 | tf_op jit(solution)/shard_map/ppermute | solution.py:461
  11.2 8.2 %collective-permute-start.3 = (f32[8,640]{1,0:T(8,128)S(1)}, f32[8,640]{1,0:T(8,128)S(1)}, u32[]{:S(2)}, u32[]{:S(2)}) collective-permute-start(f32[8,640]{1,0:T(8,128)S(1)} %get-tuple-element.55), channel_id=1, source_target_pairs={{7,0},{15,8},{23,16},{31,24},{39,32},{47,40},{55,48},{63,56},{71,6... | collective-permute-start | bytes 61448 | tf_op jit(solution)/shard_map/ppermute | solution.py:461
  19.4 27.1 %copy-start.3 = (bf16[32,128]{1,0:T(8,128)(2,1)S(1)}, bf16[32,128]{1,0:T(8,128)(2,1)}, u32[]{:S(2)}) copy-start(bf16[32,128]{1,0:T(8,128)(2,1)} %up_w.1) | copy-start | bytes 24580
  19.4 27.1 %copy-start.11 = (f32[2]{0:T(128)S(1)}, f32[2]{0:T(128)}, u32[]{:S(2)}) copy-start(f32[2]{0:T(128)} %head_b.1) | copy-start | bytes 28
  21.2 1.4 %collective-permute-start.4 = (bf16[32,2048]{1,0:T(8,128)(2,1)S(1)}, bf16[32,2048]{1,0:T(8,128)(2,1)S(1)}, u32[]{:S(2)}, u32[]{:S(2)}) collective-permute-start(bf16[32,2048]{1,0:T(8,128)(2,1)S(1)} %get-tuple-element.61), channel_id=1, source_target_pairs={{8,0},{0,8},{24,16},{16,24},{40,32},{32,40},{56,48},{48,56},{72,64... | collective-permute-start | bytes 393224 | tf_op jit(solution)/shard_map/ppermute | solution.py:461
  22.6 14.5 %collective-permute-start.5 = (bf16[2,32,2048]{2,1,0:T(8,128)(2,1)S(1)}, bf16[2,32,2048]{2,1,0:T(8,128)(2,1)S(1)}, u32[]{:S(2)}, u32[]{:S(2)}) collective-permute-start(bf16[2,32,2048]{2,1,0:T(8,128)(2,1)S(1)} %bitcast_dynamic-update-slice_fusion.refs_0_), channel_id=1, source_target_pairs={{119,0},{25,8},{7,16},{41,24},{23,32},{57,40},{39,48},{73,56},{55,... | collective-permute-start | bytes 786440 | tf_op jit(solution)/shard_map/ppermute | solution.py:461
  22.7 14.4 %collective-permute-start.7 = (bf16[2,32,2048]{2,1,0:T(8,128)(2,1)S(1)}, bf16[2,32,2048]{2,1,0:T(8,128)(2,1)S(1)}, u32[]{:S(2)}, u32[]{:S(2)}) collective-permute-start(bf16[2,32,2048]{2,1,0:T(8,128)(2,1)S(1)} %bitcast_dynamic-update-slice_fusion.refs_0_), channel_id=1, source_target_pairs={{112,0},{24,8},{0,16},{40,24},{16,32},{56,40},{32,48},{72,56},{48,... | collective-permute-start | bytes 786440 | tf_op jit(solution)/shard_map/ppermute | solution.py:461
  23.2 15.8 %collective-permute-start.8 = (bf16[2,32,2048]{2,1,0:T(8,128)(2,1)S(1)}, bf16[2,32,2048]{2,1,0:T(8,128)(2,1)S(1)}, u32[]{:S(2)}, u32[]{:S(2)}) collective-permute-start(bf16[2,32,2048]{2,1,0:T(8,128)(2,1)S(1)} %bitcast_dynamic-update-slice_fusion.refs_0_), channel_id=1, source_target_pairs={{113,0},{31,8},{1,16},{47,24},{17,32},{63,40},{33,48},{79,56},{49,... | collective-permute-start | bytes 786440 | tf_op jit(solution)/shard_map/ppermute | solution.py:461
  37.1 7.9 %collective-permute-start.6 = (bf16[2,32,2048]{2,1,0:T(8,128)(2,1)S(1)}, bf16[2,32,2048]{2,1,0:T(8,128)(2,1)S(1)}, u32[]{:S(2)}, u32[]{:S(2)}) collective-permute-start(bf16[2,32,2048]{2,1,0:T(8,128)(2,1)S(1)} %collective-permute-done.5.refs_1_), channel_id=1, source_target_pairs={{120,0},{16,8},{8,16},{32,24},{24,32},{48,40},{40,48},{64,56},{56,... | collective-permute-start | bytes 786440 | tf_op jit(solution)/shard_map/ppermute | solution.py:461
  37.1 7.9 %collective-permute-start.12 = (bf16[2,32,2048]{2,1,0:T(8,128)(2,1)S(1)}, bf16[2,32,2048]{2,1,0:T(8,128)(2,1)S(1)}, u32[]{:S(2)}, u32[]{:S(2)}) collective-permute-start(bf16[2,32,2048]{2,1,0:T(8,128)(2,1)S(1)} %collective-permute-done.5.refs_1_), channel_id=1, source_target_pairs={{8,0},{0,8},{24,16},{16,24},{40,32},{32,40},{56,48},{48,56},{72,64... | collective-permute-start | bytes 786440 | tf_op jit(solution)/shard_map/ppermute | solution.py:461
  37.1 7.9 %collective-permute-start.11 = (bf16[2,32,2048]{2,1,0:T(8,128)(2,1)S(1)}, bf16[2,32,2048]{2,1,0:T(8,128)(2,1)S(1)}, u32[]{:S(2)}, u32[]{:S(2)}) collective-permute-start(bf16[2,32,2048]{2,1,0:T(8,128)(2,1)S(1)} %collective-permute-done.7.refs_2_), channel_id=1, source_target_pairs={{8,0},{0,8},{24,16},{16,24},{40,32},{32,40},{56,48},{48,56},{72,64... | collective-permute-start | bytes 786440 | tf_op jit(solution)/shard_map/ppermute | solution.py:461
  39.0 6.0 %collective-permute-start.9 = (bf16[2,32,2048]{2,1,0:T(8,128)(2,1)S(1)}, bf16[2,32,2048]{2,1,0:T(8,128)(2,1)S(1)}, u32[]{:S(2)}, u32[]{:S(2)}) collective-permute-start(bf16[2,32,2048]{2,1,0:T(8,128)(2,1)S(1)} %collective-permute-done.8.two), channel_id=1, source_target_pairs={{8,0},{0,8},{24,16},{16,24},{40,32},{32,40},{56,48},{48,56},{72,64... | collective-permute-start | bytes 786440 | tf_op jit(solution)/shard_map/ppermute | solution.py:461
  45.0 1.5 %collective-permute-start.10 = (bf16[2,32,2048]{2,1,0:T(8,128)(2,1)S(1)}, bf16[2,32,2048]{2,1,0:T(8,128)(2,1)S(1)}, u32[]{:S(2)}, u32[]{:S(2)}) collective-permute-start(bf16[2,32,2048]{2,1,0:T(8,128)(2,1)S(1)} %collective-permute-done.6.relay), channel_id=1, source_target_pairs={{8,0},{0,8},{24,16},{16,24},{40,32},{32,40},{56,48},{48,56},{72,64... | collective-permute-start | bytes 786440 | tf_op jit(solution)/shard_map/ppermute | solution.py:461
  51.2 1.3 %collective-permute-start.13 = (f32[72,128]{1,0:T(8,128)S(1)}, f32[72,128]{1,0:T(8,128)S(1)}, u32[]{:S(2)}, u32[]{:S(2)}) collective-permute-start(f32[72,128]{1,0:T(8,128)S(1)} %get-tuple-element.69), channel_id=1, source_target_pairs={{8,0},{0,8},{24,16},{16,24},{40,32},{32,40},{56,48},{48,56},{72,64... | collective-permute-start | bytes 110600 | tf_op jit(solution)/shard_map/ppermute | solution.py:461
  51.3 5.5 %collective-permute-start.14 = (f32[72,128]{1,0:T(8,128)S(1)}, f32[72,128]{1,0:T(8,128)S(1)}, u32[]{:S(2)}, u32[]{:S(2)}) collective-permute-start(f32[72,128]{1,0:T(8,128)S(1)} %get-tuple-element.69), channel_id=1, source_target_pairs={{120,0},{16,8},{8,16},{32,24},{24,32},{48,40},{40,48},{64,56},{56,... | collective-permute-start | bytes 110600 | tf_op jit(solution)/shard_map/ppermute | solution.py:461
  56.9 5.3 %collective-permute-start.15 = (f32[8,512]{1,0:T(8,128)S(1)}, f32[8,512]{1,0:T(8,128)S(1)}, u32[]{:S(2)}, u32[]{:S(2)}) collective-permute-start(f32[8,512]{1,0:T(8,128)S(1)} %maximum_add_fusion), channel_id=1, source_target_pairs={{1,0},{9,8},{17,16},{25,24},{33,32},{41,40},{49,48},{57,56},{65,64... | collective-permute-start | bytes 49160 | tf_op jit(solution)/shard_map/ppermute | solution.py:461
  56.9 7.4 %collective-permute-start.16 = (f32[8,512]{1,0:T(8,128)S(1)}, f32[8,512]{1,0:T(8,128)S(1)}, u32[]{:S(2)}, u32[]{:S(2)}) collective-permute-start(f32[8,512]{1,0:T(8,128)S(1)} %maximum_add_fusion), channel_id=1, source_target_pairs={{7,0},{15,8},{23,16},{31,24},{39,32},{47,40},{55,48},{63,56},{71,6... | collective-permute-start | bytes 49160 | tf_op jit(solution)/shard_map/ppermute | solution.py:461

commit v8 on v7

--- a/solution.py
+++ b/solution.py
@@ -264,7 +264,7 @@
     (-1, -2): ("one", 0), (-1, -1): ("one", 1), (-1, 0): ("relay_p", 0), (-1, 1): ("relay_p", 1), (-1, 2): ("two_p", 1),
     (1, -2): ("two", 0), (1, -1): ("two", 1), (1, 0): ("relay", 1), (1, 1): ("relay", 0), (1, 2): ("one_p", 1),
 }
-PHASES = (("own", "one", "band"), ("two", "two_p", "relay", "relay_p", "band_p", "one_p"))
+PHASES = (("own", "one", "band"), ("two_p", "relay", "relay_p"), ("one_p", "band_p", "two"))
 TILES = [[at for at in range(15) if MAPS[(at // 5 - 1, at % 5 - 2)][0] in names] for names in PHASES]
 
 
@@ -313,12 +313,21 @@
     context_sum(cells, TILES[0], arrays, proj_w, proj_b, ctx_w, weights, proj, finish)
 
 
+def middle_kernel(cells, one_p, band_p, two, before, proj_w, proj_b, ctx_w, context, weights, proj):
+    arrays = dict(zip(PHASES[2], (one_p, band_p, two)))
+
+    def finish(at, spots, total):
+        context[:, spots] = total + before[:, spots]
+
+    context_sum(cells, TILES[2], arrays, proj_w, proj_b, ctx_w, weights, proj, finish)
+
+
 def logits_kernel(
-    cells, low, high, rim_rows, rim_cols, context, two, two_p, relay, relay_p, band_p, one_p,
+    cells, low, high, rim_rows, rim_cols, context, two_p, relay, relay_p,
     proj_w, proj_b, ctx_w, up_w, up_b, head_w, rim_w, head_b,
     logits, col_out, row_out, weights, proj, low_up, lifted, decoded,
 ):
-    arrays = dict(zip(PHASES[1], (two, two_p, relay, relay_p, band_p, one_p)))
+    arrays = dict(zip(PHASES[1], (two_p, relay, relay_p)))
 
     def finish(part, spots, total):
         mixed = jnp.maximum(total + context[:, spots], 0.0).astype(BF16)
@@ -537,12 +546,15 @@
     relay, context = tie((relay, context))
     relay_p, two_p = partner(relay), partner(two)
     band_p, one_p = partner(band), partner(one)
+    context = context_call(
+        middle_kernel, 2, shape_of(WIDE, SPOTS), [one_p, band_p, two, context, *proj_args]
+    )
 
     inner_logits, col_out, row_out = context_call(
         logits_kernel, 1,
         [shape_of(2, ROWS, COLS), shape_of(ROWS + 8, 128), shape_of(8, COLS)],
         [
-            feat_low, feat_high, rim_rows, rim_cols, context, two, two_p, relay, relay_p, band_p, one_p,
+            feat_low, feat_high, rim_rows, rim_cols, context, two_p, relay, relay_p,
             *proj_args, w_up, up_bias, head_w, rim_w, b_head,
         ],
         [
@@ -550,7 +562,7 @@
             pltpu.VMEM((POOL_ROWS * CH, COLS), F32),
             pltpu.VMEM(((ROWS + 4) * CH, COLS), BF16),
         ],
-        smem=(19,),
+        smem=(16,),
     )
     near, far = partner(col_out), outer(col_out)
     row_out = row_sums(cells, row_out, near, far)

time: 65.3 us -> 64.4 us (0.986)
  waiting for transfers between devices: 25.3 us -> 24.1 us
    ppermute x17, waiting for transfers between devices: 25.3 us -> 24.1 us  [moved(): return lax.ppermute(x, ('band', 'cross'), route)]
    pallas_call x7 -> x8, Pallas kernels: 15.3 us -> 15.5 us  [call(): pl.pallas_call(fetching if hbm else kernel, out_shape=outs, in_specs=[SME...]
  transfers between devices with their start and end apart: 17 -> 17, of which waited for: 10 -> 10; matrix products, arithmetic and copies ran while one was open for 0% -> 0% of each run, Pallas kernels for 12% -> 14%
where the time goes in v8:
time: 64.4 us; the launch traced here: 64.2 us
  waiting for transfers between devices  24.1 us (37%)
  starting transfers between devices  21.9 us (34%)
  Pallas kernels  15.5 us (24%)
  local copies, waits for them, and re-layouts  2.09 us (3%)
    ppermute x17, waiting for transfers between devices, moved(): return lax.ppermute(x, ('band', 'cross'), route)  24.1 us
    ppermute x17, starting transfers between devices, moved(): return lax.ppermute(x, ('band', 'cross'), route)  21.9 us
    pallas_call x8, Pallas kernels, call(): pl.pallas_call(fetching if hbm else kernel, out_shape=outs, in_specs=[SME...  15.5 us
    unnamed x28, local copies, waits for them, and re-layouts  2.07 us
  transfers between devices with their start and end apart: 17, of which 10 were waited for; matrix products, arithmetic and copies ran while one was open for 0% of the time, Pallas kernels for 14%

profile of v8, /device:TPU:0, one launch (start us, length us, event | category | flops | bytes accessed | tf_op | source)
XLA Modules:
  0.0 64.2 jit_solution(3576568216876230545)
XLA Ops:
  0.0 1.1 %copy-done.12 = s32[4,64,512]{2,1,0:T(8,128)S(1)} copy-done((s32[4,64,512]{2,1,0:T(8,128)S(1)}, s32[4,64,512]{2,1,0:T(8,128)}, u32[]{:S(2)}) %copy-start.12) | copy-done | bytes 524312
  1.1 0.9 %copy-done.13 = f32[64,512]{1,0:T(8,128)S(1)} copy-done((f32[64,512]{1,0:T(8,128)S(1)}, f32[64,512]{1,0:T(8,128)}, u32[]{:S(2)}) %copy-start.13) | copy-done | bytes 131096
  2.0 0.3 shard_map.136
  2.3 0.1 collective-permute-start
  2.4 4.1 %collective-permute-start.1 = (f32[16,128]{1,0:T(8,128)S(1)}, f32[16,128]{1,0:T(8,128)S(1)}, u32[]{:S(2)}, u32[]{:S(2)}) collective-permute-start(f32[16,128]{1,0:T(8,128)S(1)} %get-tuple-element.47), channel_id=1, source_target_pairs={{120,0},{16,8},{8,16},{32,24},{24,32},{48,40},{40,48},{64,56},{56,... | collective-permute-start | bytes 24584 | tf_op jit(solution)/shard_map/ppermute | solution.py:470
  6.6 1.1 %shard_map.137 = (bf16[256,512]{1,0:T(8,128)(2,1)S(1)}, f32[32,256]{1,0:T(8,128)S(1)}) custom-call(bf16[512,512]{1,0:T(8,128)(2,1)S(1)} %get-tuple-element.51.stem_in, f32[4,32]{1,0:T(4,128)S(1)} %bitcast.15, f32[1,32]{1,0:T(1,128)S(1)} %bitcast.18, f32[1,32]{1,0:T(1,128)S(1)} %bitcast.21, bf16[32,288]{1,0:T(8,128)(2,1)S(1)} %copy-done.2, f32[1,32]{1,0:T(1,128)S(1)} %bitcast.24), custom_call_target="tpu_custom_call" | custom-call | flops 4000000000 | bytes 1048576 | tf_op jit(solution)/shard_map/pallas_call | solution.py:446
  7.7 0.0 collective-permute-done.partner
  7.7 0.2 collective-permute-done.1.outer
  7.9 0.2 multiply_reduce_fusion.2
  8.1 0.1 select_select_fusion.1
  8.2 0.0 copy-start
  8.2 0.0 copy-start.1
  8.2 0.0 copy-start.4
  8.2 0.0 copy-start.5
  8.2 0.0 copy-start.10
  8.3 3.0 %collective-permute-start.2 = (f32[8,640]{1,0:T(8,128)S(1)}, f32[8,640]{1,0:T(8,128)S(1)}, u32[]{:S(2)}, u32[]{:S(2)}) collective-permute-start(f32[8,640]{1,0:T(8,128)S(1)} %get-tuple-element.54), channel_id=1, source_target_pairs={{1,0},{9,8},{17,16},{25,24},{33,32},{41,40},{49,48},{57,56},{65,64... | collective-permute-start | bytes 61448 | tf_op jit(solution)/shard_map/ppermute | solution.py:470
  11.2 4.1 %collective-permute-start.3 = (f32[8,640]{1,0:T(8,128)S(1)}, f32[8,640]{1,0:T(8,128)S(1)}, u32[]{:S(2)}, u32[]{:S(2)}) collective-permute-start(f32[8,640]{1,0:T(8,128)S(1)} %get-tuple-element.55), channel_id=1, source_target_pairs={{7,0},{15,8},{23,16},{31,24},{39,32},{47,40},{55,48},{63,56},{71,6... | collective-permute-start | bytes 61448 | tf_op jit(solution)/shard_map/ppermute | solution.py:470
  15.3 4.1 %shard_map.138 = (bf16[1792,512]{1,0:T(8,128)(2,1)S(1)}, f32[32,1792]{1,0:T(8,128)S(1)}) custom-call(bf16[512,512]{1,0:T(8,128)(2,1)S(1)} %get-tuple-element.51.stem_in, f32[4,32]{1,0:T(4,128)S(1)} %bitcast.16, f32[1,32]{1,0:T(1,128)S(1)} %bitcast.19, f32[1,32]{1,0:T(1,128)S(1)} %bitcast.22, bf16[32,288]{1,0:T(8,128)(2,1)S(1)} %copy-done.2, f32[1,32]{1,0:T(1,128)S(1)} %bitcast.25), custom_call_target="tpu_custom_call" | custom-call | flops 4000000000 | bytes 1048576 | tf_op jit(solution)/shard_map/pallas_call | solution.py:446
  19.4 0.0 collective-permute-done.2.even_message
  19.4 1.7 %shard_map.139 = (bf16[64,512]{1,0:T(8,128)(2,1)S(1)}, bf16[32,256]{1,0:T(8,128)(2,1)S(1)}, bf16[32,2048]{1,0:T(8,128)(2,1)S(1)}, bf16[2,32,2048]{2,1,0:T(8,128)(2,1)S(1)}) custom-call(f32[32,512]{1,0:T(8,128)S(1)} %get-tuple-element.46.rows, f32[32,128]{1,0:T(8,128)S(1)} %get-tuple-element.53.cols, f32[16,128]{1,0:T(8,128)S(1)} %collective-permute-done.partner, ...), custom_call_target="tpu_custom_call" | custom-call | bytes 1048576 | tf_op jit(solution)/shard_map/pallas_call | solution.py:446
  21.1 0.1 collective-permute-start.4
  21.2 1.3 %collective-permute-done.4 = bf16[32,2048]{1,0:T(8,128)(2,1)S(1)} collective-permute-done((bf16[32,2048]{1,0:T(8,128)(2,1)S(1)}, bf16[32,2048]{1,0:T(8,128)(2,1)S(1)}, u32[]{:S(2)}, u32[]{:S(2)}) %collective-permute-start.4) | collective-permute-done | bytes 131104 | tf_op jit(solution)/shard_map/ppermute | solution.py:470
  22.6 0.1 collective-permute-start.5
  22.7 0.5 collective-permute-start.7
  23.2 4.9 %collective-permute-start.9 = (bf16[2,32,2048]{2,1,0:T(8,128)(2,1)S(1)}, bf16[2,32,2048]{2,1,0:T(8,128)(2,1)S(1)}, u32[]{:S(2)}, u32[]{:S(2)}) collective-permute-start(bf16[2,32,2048]{2,1,0:T(8,128)(2,1)S(1)} %bitcast_dynamic-update-slice_fusion.refs_0_), channel_id=1, source_target_pairs={{113,0},{31,8},{1,16},{47,24},{17,32},{63,40},{33,48},{79,56},{49,... | collective-permute-start | bytes 786440 | tf_op jit(solution)/shard_map/ppermute | solution.py:470
  28.0 9.0 %collective-permute-done.5.refs_1_ = bf16[2,32,2048]{2,1,0:T(8,128)(2,1)S(1)} collective-permute-done((bf16[2,32,2048]{2,1,0:T(8,128)(2,1)S(1)}, bf16[2,32,2048]{2,1,0:T(8,128)(2,1)S(1)}, u32[]{:S(2)}, u32[]{:S(2)}) %collective-permute-start.5) | collective-permute-done | bytes 262176 | tf_op jit(solution)/shard_map/ppermute | solution.py:470
  37.1 0.0 collective-permute-start.6
  37.1 0.0 collective-permute-done.7.refs_2_
  37.1 0.5 collective-permute-start.8
  37.6 1.4 %collective-permute-done.9.two = bf16[2,32,2048]{2,1,0:T(8,128)(2,1)S(1)} collective-permute-done((bf16[2,32,2048]{2,1,0:T(8,128)(2,1)S(1)}, bf16[2,32,2048]{2,1,0:T(8,128)(2,1)S(1)}, u32[]{:S(2)}, u32[]{:S(2)}) %collective-permute-start.9) | collective-permute-done | bytes 262176 | tf_op jit(solution)/shard_map/ppermute | solution.py:470
  38.9 0.1 collective-permute-start.11
  39.1 2.7 %shard_map.140 = (f32[128,2048]{1,0:T(8,128)S(1)}, bf16[160,640]{1,0:T(8,128)(2,1)S(1)}, bf16[40,128]{1,0:T(8,128)(2,1)S(1)}, f32[32,256]{1,0:T(8,128)S(1)}) custom-call(bf16[2,32,2048]{2,1,0:T(8,128)(2,1)S(1)} %bitcast_dynamic-update-slice_fusion.refs_0_, bf16[2,32,2048]{2,1,0:T(8,128)(2,1)S(1)} %collective-permute-done.5.refs_1_, ...), custom_call_target="tpu_custom_call" | custom-call | bytes 1048576 | tf_op jit(solution)/shard_map/pallas_call | solution.py:446
  41.8 0.0 copy-start.3
  41.8 0.0 copy-start.11
  41.8 3.1 %collective-permute-done.10.relay = bf16[2,32,2048]{2,1,0:T(8,128)(2,1)S(1)} collective-permute-done((bf16[2,32,2048]{2,1,0:T(8,128)(2,1)S(1)}, bf16[2,32,2048]{2,1,0:T(8,128)(2,1)S(1)}, u32[]{:S(2)}, u32[]{:S(2)}) %collective-permute-start.10) | collective-permute-done | bytes 262176 | tf_op jit(solution)/shard_map/ppermute | solution.py:470
  45.0 0.0 collective-permute-start.12
  45.0 0.0 collective-permute-done.6.one_p
  45.0 1.2 %shard_map.141.context = f32[128,2048]{1,0:T(8,128)S(1)} custom-call(bf16[2,32,2048]{2,1,0:T(8,128)(2,1)S(1)} %collective-permute-done.6.one_p, bf16[2,32,2048]{2,1,0:T(8,128)(2,1)S(1)} %collective-permute-done.8.band_p, bf16[2,32,2048]{2,1,0:T(8,128)(2,1)S(1)} %collective-permute-done.9.two, f32[128,2048]{1,0:T(8,128)S(1)} %get-tuple-element.63.before, ...), custom_call_target="tpu_custom_call" | custom-call | bytes 1048576 | tf_op jit(solution)/shard_map/pallas_call | solution.py:446
  46.2 0.3 collective-permute-done.12.relay_p
  46.5 3.6 %shard_map.142 = (f32[2,64,512]{2,1,0:T(8,128)S(1)}, f32[72,128]{1,0:T(8,128)S(1)}, f32[8,512]{1,0:T(8,128)S(1)}) custom-call(bf16[256,512]{1,0:T(8,128)(2,1)S(1)} %get-tuple-element.45.low, bf16[1792,512]{1,0:T(8,128)(2,1)S(1)} %get-tuple-element.52.high, bf16[64,512]{1,0:T(8,128)(2,1)S(1)} %get-tuple-element.58.rim_rows, ...), custom_call_target="tpu_custom_call" | custom-call | bytes 1048576 | tf_op jit(solution)/shard_map/pallas_call | solution.py:446
  50.1 0.3 collective-permute-start.13
  50.4 1.0 %collective-permute-done.13.partner = f32[72,128]{1,0:T(8,128)S(1)} collective-permute-done((f32[72,128]{1,0:T(8,128)S(1)}, f32[72,128]{1,0:T(8,128)S(1)}, u32[]{:S(2)}, u32[]{:S(2)}) %collective-permute-start.13) | collective-permute-done | bytes 36896 | tf_op jit(solution)/shard_map/ppermute | solution.py:470
  51.4 4.5 %collective-permute-done.14.outer = f32[72,128]{1,0:T(8,128)S(1)} collective-permute-done((f32[72,128]{1,0:T(8,128)S(1)}, f32[72,128]{1,0:T(8,128)S(1)}, u32[]{:S(2)}, u32[]{:S(2)}) %collective-permute-start.14) | collective-permute-done | bytes 36896 | tf_op jit(solution)/shard_map/ppermute | solution.py:470
  55.9 0.1 collective-permute-start.15
  56.0 4.1 %collective-permute-start.16 = (f32[8,512]{1,0:T(8,128)S(1)}, f32[8,512]{1,0:T(8,128)S(1)}, u32[]{:S(2)}, u32[]{:S(2)}) collective-permute-start(f32[8,512]{1,0:T(8,128)S(1)} %maximum_add_fusion), channel_id=1, source_target_pairs={{7,0},{15,8},{23,16},{31,24},{39,32},{47,40},{55,48},{63,56},{71,6... | collective-permute-start | bytes 49160 | tf_op jit(solution)/shard_map/ppermute | solution.py:470
  60.1 1.1 %collective-permute-done.15.even_message = f32[8,512]{1,0:T(8,128)S(1)} collective-permute-done((f32[8,512]{1,0:T(8,128)S(1)}, f32[8,512]{1,0:T(8,128)S(1)}, u32[]{:S(2)}, u32[]{:S(2)}) %collective-permute-start.15) | collective-permute-done | bytes 16416 | tf_op jit(solution)/shard_map/ppermute | solution.py:470
  61.2 2.2 %collective-permute-done.16.odd_message = f32[8,512]{1,0:T(8,128)S(1)} collective-permute-done((f32[8,512]{1,0:T(8,128)S(1)}, f32[8,512]{1,0:T(8,128)S(1)}, u32[]{:S(2)}, u32[]{:S(2)}) %collective-permute-start.16) | collective-permute-done | bytes 16416 | tf_op jit(solution)/shard_map/ppermute | solution.py:470
  63.4 0.8 %shard_map.143 = f32[2,64,512]{2,1,0:T(8,128)} custom-call(f32[2,64,512]{2,1,0:T(8,128)S(1)} %get-tuple-element.68.inner, f32[72,128]{1,0:T(8,128)S(1)} %collective-permute-done.13.partner, f32[72,128]{1,0:T(8,128)S(1)} %collective-permute-done.14.outer, f32[8,512]{1,0:T(8,128)S(1)} %collective-permute-done.15.even_message, ...), custom_call_target="tpu_custom_call" | custom-call | bytes 1048576 | tf_op jit(solution)/shard_map/pallas_call | solution.py:446
  (34 shorter events, 0.1 us)
Async XLA Ops:
  0.0 6.5 %copy-start.6 = (f32[32,4]{0,1:T(4,128)S(1)}, f32[32,4]{0,1:T(4,128)}, u32[]{:S(2)}) copy-start(f32[32,4]{0,1:T(4,128)} %param.18) | copy-start | bytes 1540
  0.0 6.5 %copy-start.7 = (f32[32]{0:T(128)S(1)}, f32[32]{0:T(128)}, u32[]{:S(2)}) copy-start(f32[32]{0:T(128)} %param.19) | copy-start | bytes 388
  0.0 6.5 %copy-start.8 = (f32[32]{0:T(128)S(1)}, f32[32]{0:T(128)}, u32[]{:S(2)}) copy-start(f32[32]{0:T(128)} %param.20) | copy-start | bytes 388
  0.0 6.5 %copy-start.2 = (bf16[32,288]{1,0:T(8,128)(2,1)S(1)}, bf16[32,288]{1,0:T(8,128)(2,1)}, u32[]{:S(2)}) copy-start(bf16[32,288]{1,0:T(8,128)(2,1)} %conv_w.5) | copy-start | bytes 55300
  0.0 6.5 %copy-start.9 = (f32[32]{0:T(128)S(1)}, f32[32]{0:T(128)}, u32[]{:S(2)}) copy-start(f32[32]{0:T(128)} %param.22) | copy-start | bytes 388
  0.0 1.1 %copy-start.12 = (s32[4,64,512]{2,1,0:T(8,128)S(1)}, s32[4,64,512]{2,1,0:T(8,128)}, u32[]{:S(2)}) copy-start(s32[4,64,512]{2,1,0:T(8,128)} %rasters.1) | copy-start | bytes 1572868
  1.1 0.9 %copy-start.13 = (f32[64,512]{1,0:T(8,128)S(1)}, f32[64,512]{1,0:T(8,128)}, u32[]{:S(2)}) copy-start(f32[64,512]{1,0:T(8,128)} %aerial.1) | copy-start | bytes 393220
  2.3 5.4 %collective-permute-start = (f32[16,128]{1,0:T(8,128)S(1)}, f32[16,128]{1,0:T(8,128)S(1)}, u32[]{:S(2)}, u32[]{:S(2)}) collective-permute-start(f32[16,128]{1,0:T(8,128)S(1)} %get-tuple-element.47), channel_id=1, source_target_pairs={{8,0},{0,8},{24,16},{16,24},{40,32},{32,40},{56,48},{48,56},{72,64... | collective-permute-start | bytes 24584 | tf_op jit(solution)/shard_map/ppermute | solution.py:470
  2.4 5.5 %collective-permute-start.1 = (f32[16,128]{1,0:T(8,128)S(1)}, f32[16,128]{1,0:T(8,128)S(1)}, u32[]{:S(2)}, u32[]{:S(2)}) collective-permute-start(f32[16,128]{1,0:T(8,128)S(1)} %get-tuple-element.47), channel_id=1, source_target_pairs={{120,0},{16,8},{8,16},{32,24},{24,32},{48,40},{40,48},{64,56},{56,... | collective-permute-start | bytes 24584 | tf_op jit(solution)/shard_map/ppermute | solution.py:470
  8.2 30.9 %copy-start = (bf16[128,1920]{1,0:T(8,128)(2,1)S(1)}, bf16[128,1920]{1,0:T(8,128)(2,1)}, u32[]{:S(2)}) copy-start(bf16[128,1920]{1,0:T(8,128)(2,1)} %ctx_w.3) | copy-start | bytes 1474564
  8.2 30.9 %copy-start.1 = (bf16[128,32]{0,1:T(8,128)(2,1)S(1)}, bf16[128,32]{0,1:T(8,128)(2,1)}, u32[]{:S(2)}) copy-start(bf16[128,32]{0,1:T(8,128)(2,1)} %param.23) | copy-start | bytes 24580
  8.2 30.8 %copy-start.4 = (f32[128]{0:T(128)S(1)}, f32[128]{0:T(128)}, u32[]{:S(2)}) copy-start(f32[128]{0:T(128)} %param.24) | copy-start | bytes 1540
  8.2 30.8 %copy-start.5 = (bf16[2,800]{1,0:T(2,128)(2,1)S(1)}, bf16[2,800]{1,0:T(2,128)(2,1)}, u32[]{:S(2)}) copy-start(bf16[2,800]{1,0:T(2,128)(2,1)} %refs_6_.1) | copy-start | bytes 9604
  8.2 30.8 %copy-start.10 = (f32[32]{0:T(128)S(1)}, f32[32]{0:T(128)}, u32[]{:S(2)}) copy-start(f32[32]{0:T(128)} %param.27) | copy-start | bytes 388
  8.3 11.2 %collective-permute-start.2 = (f32[8,640]{1,0:T(8,128)S(1)}, f32[8,640]{1,0:T(8,128)S(1)}, u32[]{:S(2)}, u32[]{:S(2)}) collective-permute-start(f32[8,640]{1,0:T(8,128)S(1)} %get-tuple-element.54), channel_id=1, source_target_pairs={{1,0},{9,8},{17,16},{25,24},{33,32},{41,40},{49,48},{57,56},{65,64... | collective-permute-start | bytes 61448 | tf_op jit(solution)/shard_map/ppermute | solution.py:470
  11.2 8.2 %collective-permute-start.3 = (f32[8,640]{1,0:T(8,128)S(1)}, f32[8,640]{1,0:T(8,128)S(1)}, u32[]{:S(2)}, u32[]{:S(2)}) collective-permute-start(f32[8,640]{1,0:T(8,128)S(1)} %get-tuple-element.55), channel_id=1, source_target_pairs={{7,0},{15,8},{23,16},{31,24},{39,32},{47,40},{55,48},{63,56},{71,6... | collective-permute-start | bytes 61448 | tf_op jit(solution)/shard_map/ppermute | solution.py:470
  21.1 1.4 %collective-permute-start.4 = (bf16[32,2048]{1,0:T(8,128)(2,1)S(1)}, bf16[32,2048]{1,0:T(8,128)(2,1)S(1)}, u32[]{:S(2)}, u32[]{:S(2)}) collective-permute-start(bf16[32,2048]{1,0:T(8,128)(2,1)S(1)} %get-tuple-element.61), channel_id=1, source_target_pairs={{8,0},{0,8},{24,16},{16,24},{40,32},{32,40},{56,48},{48,56},{72,64... | collective-permute-start | bytes 393224 | tf_op jit(solution)/shard_map/ppermute | solution.py:470
  22.6 14.5 %collective-permute-start.5 = (bf16[2,32,2048]{2,1,0:T(8,128)(2,1)S(1)}, bf16[2,32,2048]{2,1,0:T(8,128)(2,1)S(1)}, u32[]{:S(2)}, u32[]{:S(2)}) collective-permute-start(bf16[2,32,2048]{2,1,0:T(8,128)(2,1)S(1)} %bitcast_dynamic-update-slice_fusion.refs_0_), channel_id=1, source_target_pairs={{119,0},{25,8},{7,16},{41,24},{23,32},{57,40},{39,48},{73,56},{55,... | collective-permute-start | bytes 786440 | tf_op jit(solution)/shard_map/ppermute | solution.py:470
  22.7 14.4 %collective-permute-start.7 = (bf16[2,32,2048]{2,1,0:T(8,128)(2,1)S(1)}, bf16[2,32,2048]{2,1,0:T(8,128)(2,1)S(1)}, u32[]{:S(2)}, u32[]{:S(2)}) collective-permute-start(bf16[2,32,2048]{2,1,0:T(8,128)(2,1)S(1)} %bitcast_dynamic-update-slice_fusion.refs_0_), channel_id=1, source_target_pairs={{112,0},{24,8},{0,16},{40,24},{16,32},{56,40},{32,48},{72,56},{48,... | collective-permute-start | bytes 786440 | tf_op jit(solution)/shard_map/ppermute | solution.py:470
  23.2 15.8 %collective-permute-start.9 = (bf16[2,32,2048]{2,1,0:T(8,128)(2,1)S(1)}, bf16[2,32,2048]{2,1,0:T(8,128)(2,1)S(1)}, u32[]{:S(2)}, u32[]{:S(2)}) collective-permute-start(bf16[2,32,2048]{2,1,0:T(8,128)(2,1)S(1)} %bitcast_dynamic-update-slice_fusion.refs_0_), channel_id=1, source_target_pairs={{113,0},{31,8},{1,16},{47,24},{17,32},{63,40},{33,48},{79,56},{49,... | collective-permute-start | bytes 786440 | tf_op jit(solution)/shard_map/ppermute | solution.py:470
  37.1 7.9 %collective-permute-start.10 = (bf16[2,32,2048]{2,1,0:T(8,128)(2,1)S(1)}, bf16[2,32,2048]{2,1,0:T(8,128)(2,1)S(1)}, u32[]{:S(2)}, u32[]{:S(2)}) collective-permute-start(bf16[2,32,2048]{2,1,0:T(8,128)(2,1)S(1)} %collective-permute-done.5.refs_1_), channel_id=1, source_target_pairs={{120,0},{16,8},{8,16},{32,24},{24,32},{48,40},{40,48},{64,56},{56,... | collective-permute-start | bytes 786440 | tf_op jit(solution)/shard_map/ppermute | solution.py:470
  37.1 7.9 %collective-permute-start.6 = (bf16[2,32,2048]{2,1,0:T(8,128)(2,1)S(1)}, bf16[2,32,2048]{2,1,0:T(8,128)(2,1)S(1)}, u32[]{:S(2)}, u32[]{:S(2)}) collective-permute-start(bf16[2,32,2048]{2,1,0:T(8,128)(2,1)S(1)} %collective-permute-done.5.refs_1_), channel_id=1, source_target_pairs={{8,0},{0,8},{24,16},{16,24},{40,32},{32,40},{56,48},{48,56},{72,64... | collective-permute-start | bytes 786440 | tf_op jit(solution)/shard_map/ppermute | solution.py:470
  37.1 7.9 %collective-permute-start.8 = (bf16[2,32,2048]{2,1,0:T(8,128)(2,1)S(1)}, bf16[2,32,2048]{2,1,0:T(8,128)(2,1)S(1)}, u32[]{:S(2)}, u32[]{:S(2)}) collective-permute-start(bf16[2,32,2048]{2,1,0:T(8,128)(2,1)S(1)} %collective-permute-done.7.refs_2_), channel_id=1, source_target_pairs={{8,0},{0,8},{24,16},{16,24},{40,32},{32,40},{56,48},{48,56},{72,64... | collective-permute-start | bytes 786440 | tf_op jit(solution)/shard_map/ppermute | solution.py:470
  38.9 7.2 %collective-permute-start.11 = (bf16[2,32,2048]{2,1,0:T(8,128)(2,1)S(1)}, bf16[2,32,2048]{2,1,0:T(8,128)(2,1)S(1)}, u32[]{:S(2)}, u32[]{:S(2)}) collective-permute-start(bf16[2,32,2048]{2,1,0:T(8,128)(2,1)S(1)} %collective-permute-done.9.two), channel_id=1, source_target_pairs={{8,0},{0,8},{24,16},{16,24},{40,32},{32,40},{56,48},{48,56},{72,64... | collective-permute-start | bytes 786440 | tf_op jit(solution)/shard_map/ppermute | solution.py:470
  41.8 4.7 %copy-start.3 = (bf16[32,128]{1,0:T(8,128)(2,1)S(1)}, bf16[32,128]{1,0:T(8,128)(2,1)}, u32[]{:S(2)}) copy-start(bf16[32,128]{1,0:T(8,128)(2,1)} %up_w.1) | copy-start | bytes 24580
  41.8 4.7 %copy-start.11 = (f32[2]{0:T(128)S(1)}, f32[2]{0:T(128)}, u32[]{:S(2)}) copy-start(f32[2]{0:T(128)} %head_b.1) | copy-start | bytes 28
  45.0 1.5 %collective-permute-start.12 = (bf16[2,32,2048]{2,1,0:T(8,128)(2,1)S(1)}, bf16[2,32,2048]{2,1,0:T(8,128)(2,1)S(1)}, u32[]{:S(2)}, u32[]{:S(2)}) collective-permute-start(bf16[2,32,2048]{2,1,0:T(8,128)(2,1)S(1)} %collective-permute-done.10.relay), channel_id=1, source_target_pairs={{8,0},{0,8},{24,16},{16,24},{40,32},{32,40},{56,48},{48,56},{72,64... | collective-permute-start | bytes 786440 | tf_op jit(solution)/shard_map/ppermute | solution.py:470
  50.1 1.3 %collective-permute-start.13 = (f32[72,128]{1,0:T(8,128)S(1)}, f32[72,128]{1,0:T(8,128)S(1)}, u32[]{:S(2)}, u32[]{:S(2)}) collective-permute-start(f32[72,128]{1,0:T(8,128)S(1)} %get-tuple-element.69), channel_id=1, source_target_pairs={{8,0},{0,8},{24,16},{16,24},{40,32},{32,40},{56,48},{48,56},{72,64... | collective-permute-start | bytes 110600 | tf_op jit(solution)/shard_map/ppermute | solution.py:470
  50.4 5.5 %collective-permute-start.14 = (f32[72,128]{1,0:T(8,128)S(1)}, f32[72,128]{1,0:T(8,128)S(1)}, u32[]{:S(2)}, u32[]{:S(2)}) collective-permute-start(f32[72,128]{1,0:T(8,128)S(1)} %get-tuple-element.69), channel_id=1, source_target_pairs={{120,0},{16,8},{8,16},{32,24},{24,32},{48,40},{40,48},{64,56},{56,... | collective-permute-start | bytes 110600 | tf_op jit(solution)/shard_map/ppermute | solution.py:470
  55.9 5.3 %collective-permute-start.15 = (f32[8,512]{1,0:T(8,128)S(1)}, f32[8,512]{1,0:T(8,128)S(1)}, u32[]{:S(2)}, u32[]{:S(2)}) collective-permute-start(f32[8,512]{1,0:T(8,128)S(1)} %maximum_add_fusion), channel_id=1, source_target_pairs={{1,0},{9,8},{17,16},{25,24},{33,32},{41,40},{49,48},{57,56},{65,64... | collective-permute-start | bytes 49160 | tf_op jit(solution)/shard_map/ppermute | solution.py:470
  56.0 7.4 %collective-permute-start.16 = (f32[8,512]{1,0:T(8,128)S(1)}, f32[8,512]{1,0:T(8,128)S(1)}, u32[]{:S(2)}, u32[]{:S(2)}) collective-permute-start(f32[8,512]{1,0:T(8,128)S(1)} %maximum_add_fusion), channel_id=1, source_target_pairs={{7,0},{15,8},{23,16},{31,24},{39,32},{47,40},{55,48},{63,56},{71,6... | collective-permute-start | bytes 49160 | tf_op jit(solution)/shard_map/ppermute | solution.py:470
